TPU v7x, 128 devices: a whole 4x4x4 slice. The times are simulated.
128 devices in a mesh: depth: 4 (over y), xline: 32 (over x, z, core).
Axes of the slice: x: 4, y: 4, z: 4, core: 2. Of those that a mesh axis runs over, the one named last changes fastest.
Arguments:
- receiver_data: bfloat16 [4, 2, 1024, 4096], P(None, None, None, 'xline'), may hold values from -6 to 6
- source_amp: bfloat16 [4, 2, 256], replicated, may hold values from -6 to 6
- source_x: int32 [256], replicated, may hold values from 0 to 1023
- source_y: int32 [256], replicated, may hold values from 0 to 4095
- omegas: float32 [4], replicated, may hold values from 0.5 to 3
- slowness: float32 [4, 1024, 4096], P('depth', None, 'xline'), may hold values from 0.2 to 2
- inverses: bfloat16 [4, 4, 2, 256, 256], replicated, may hold values from -0.1875 to 0.1875
- zones_x: int32 [4, 4], P('depth'), may hold values from 0 to 3
- zones_y: int32 [4, 16], P('depth'), may hold values from 0 to 3
Outputs:
- gradient: float32 [4, 1024, 4096], P('depth', None, 'xline')
All inputs are finite; a program needn't handle non-finite values.
Results may differ from a plain program's by a relative error of at most 0.015.
Values may be sent and summed in bfloat16 or wider, within the bound.
No kernel may reach another device: no remote copies, remote signals or barrier semaphores. Data moves between devices by JAX's collectives and lax.ppermute only.
A program may use at most 64 MiB of HBM per device.

v0:
```python
import jax
import jax.numpy as jnp
from jax import lax
from jax.sharding import PartitionSpec as P


def partner(block, axis, bit):
    count = lax.axis_size(axis)
    route = []
    for low in range(count):
        high = low | 1 << bit
        if high != low and high < count:
            route += [(low, high), (high, low)]
    return lax.ppermute(block, axis, route)


def in_one_piece(arrays, axis, dim, along):
    widths = [a.shape[along] for a in arrays]
    both = jnp.concatenate(arrays, axis=along)
    filled = lax.all_gather(both, axis, axis=dim, tiled=True)
    return tuple(jnp.split(filled, [sum(widths[:k]) for k in range(1, len(widths))], axis=along))


def cut_along(value, dim, size):
    before, after = (value.shape[:dim], value.shape[dim + 1 :])
    return jnp.moveaxis(value.reshape(*before, size, -1, *after), dim, 0)


def sum_at_owner(value, axis, dim):
    size = lax.axis_size(axis)
    blocks = lax.all_to_all(cut_along(value, dim, size), axis, 0, 0, tiled=True)
    return jnp.sum(blocks, axis=0)


def rotate(field, angle, sign):
    field_real = field[0].astype(jnp.float32)
    field_imag = field[1].astype(jnp.float32)
    cosine = jnp.cos(angle)
    sine = jnp.sin(angle) * sign
    return jnp.stack(
        [field_real * cosine - field_imag * sine, field_real * sine + field_imag * cosine]
    ).astype(jnp.bfloat16)


def complex_apply(parts, k_real, k_imag, form):

    def blockwise(matrix, vector):
        return jnp.einsum(form, matrix, vector, preferred_element_type=jnp.float32)

    out_real = (
        parts[0].astype(jnp.float32) + blockwise(k_real, parts[0]) - blockwise(k_imag, parts[1])
    )
    out_imag = (
        parts[1].astype(jnp.float32) + blockwise(k_real, parts[1]) + blockwise(k_imag, parts[0])
    )
    return jnp.stack([out_real, out_imag]).astype(jnp.bfloat16)


def solve_inline(field, blocks, sign):
    order = blocks.shape[2]
    parts = field.reshape(2, field.shape[1] // order, order, field.shape[2])
    k_imag = blocks[:, 1] if sign > 0 else -blocks[:, 1]
    return complex_apply(parts, blocks[:, 0], k_imag, "bij,bjy->biy").reshape(field.shape)


def solve_crossline(field, blocks, sign):
    order = blocks.shape[2]
    parts = field.reshape(2, field.shape[1], field.shape[2] // order, order)
    k_imag = blocks[:, 1] if sign > 0 else -blocks[:, 1]
    return complex_apply(parts, blocks[:, 0], k_imag, "bij,xbj->xbi").reshape(field.shape)


def per_device(
    receiver_data, source_amp, source_x, source_y, omegas, slowness, inverses, zones_x, zones_y
):
    sections = lax.axis_size("depth")
    line_index = lax.axis_index("xline")
    section = lax.axis_index("depth")
    freqs, _, width_x, width_y = receiver_data.shape
    onehot_x = (jnp.arange(width_x)[:, None] == source_x[None, :]).astype(jnp.bfloat16)
    local_y = source_y - line_index * width_y
    onehot_y = (local_y[:, None] == jnp.arange(width_y)[None, :]).astype(jnp.bfloat16)
    spread = source_amp[:, :, :, None] * onehot_y[None, None]
    sources = jnp.einsum(
        "xs,fcsy->fcxy", onehot_x, spread, preferred_element_type=jnp.float32
    ).astype(jnp.bfloat16)
    half = width_x // 2
    parity = line_index % 2
    slow_whole = lax.all_gather(slowness, "depth", axis=0, tiled=True)
    zone_whole_x, zone_whole_y = in_one_piece((zones_x, zones_y), "depth", 0, 1)
    all_levels = slow_whole.shape[0]
    per_section = freqs // sections
    terms = jnp.zeros((all_levels, width_x, width_y), jnp.float32)
    freq_index = section * per_section + 0
    src_field = lax.dynamic_index_in_dim(sources, freq_index, 0, keepdims=False)
    rec_field = lax.dynamic_index_in_dim(receiver_data, freq_index, 0, keepdims=False)
    table = lax.dynamic_index_in_dim(inverses, freq_index, 0, keepdims=False)
    omega = lax.dynamic_index_in_dim(omegas, freq_index, 0, keepdims=False)
    weight = omega * omega
    for level in range(all_levels):
        level_src_field = src_field
        level_rec_field = rec_field
        angle = omega * slow_whole[level]
        inline_blocks = jnp.take(table, zone_whole_x[level], axis=0)
        level_src_field = solve_inline(rotate(level_src_field, angle, 1.0), inline_blocks, 1.0)
        level_rec_field = solve_inline(rotate(level_rec_field, angle, -1.0), inline_blocks, -1.0)
        mine_start = parity * half
        other_start = (1 - parity) * half
        incoming = partner(
            (
                lax.dynamic_slice_in_dim(level_src_field, other_start, half, 1),
                lax.dynamic_slice_in_dim(level_rec_field, other_start, half, 1),
            ),
            "xline",
            0,
        )

        def assemble(kept, got, axis):
            return jnp.where(
                parity == 0, jnp.concatenate([kept, got], axis), jnp.concatenate([got, kept], axis)
            )

        block_src = assemble(
            lax.dynamic_slice_in_dim(level_src_field, mine_start, half, 1), incoming[0], 2
        )
        block_rec = assemble(
            lax.dynamic_slice_in_dim(level_rec_field, mine_start, half, 1), incoming[1], 2
        )
        blocks = jnp.take(
            table, lax.dynamic_slice_in_dim(zone_whole_y[level], line_index // 2, 1), axis=0
        )
        solved_src = solve_crossline(block_src, blocks, 1.0)
        solved_rec = solve_crossline(block_rec, blocks, -1.0)
        other_rows = (1 - parity) * width_y
        mine_rows = parity * width_y
        returned = partner(
            (
                lax.dynamic_slice_in_dim(solved_src, other_rows, width_y, 2),
                lax.dynamic_slice_in_dim(solved_rec, other_rows, width_y, 2),
            ),
            "xline",
            0,
        )
        new_src = assemble(
            lax.dynamic_slice_in_dim(solved_src, mine_rows, width_y, 2), returned[0], 1
        )
        new_rec = assemble(
            lax.dynamic_slice_in_dim(solved_rec, mine_rows, width_y, 2), returned[1], 1
        )
        level_src_field = new_src
        level_rec_field = new_rec
        correlation = level_src_field[0].astype(jnp.float32) * level_rec_field[0].astype(
            jnp.float32
        ) + level_src_field[1].astype(jnp.float32) * level_rec_field[1].astype(jnp.float32)
        src_field, rec_field, correlation = (level_src_field, level_rec_field, correlation)
        terms = terms.at[level].add(weight * correlation)
    return sum_at_owner(terms, "depth", 0)


def solution(mesh):
    in_specs = (
        P(None, None, None, "xline"),
        P(),
        P(),
        P(),
        P(),
        P("depth", None, "xline"),
        P(),
        P("depth", None),
        P("depth", None),
    )
    out_specs = P("depth", None, "xline")
    return jax.shard_map(
        per_device, mesh=mesh, in_specs=in_specs, out_specs=out_specs, check_vma=False
    )
```

profile of v0, /device:TPU:0, one launch (start us, length us, event | category | flops | bytes accessed | tf_op | source)
XLA Modules:
  0.0 191.1 jit_solution(12033378358790410047)
XLA Ops:
  8.0 10.0 %all-gather = s32[4,1,20]{2,1,0:T(1,128)S(1)} all-gather(s32[1,1,20]{2,1,0:T(1,128)S(1)} %add_bitcast_fusion), channel_id=1, replica_groups=mesh['depth'=4,'xline'=32] {'depth'}, dimensions={0}, use_global_device_ids=true | all-gather | bytes 400 | tf_op jit(solution)/shard_map/all_gather | solution.py:20
  28.1 1.3 dynamic_slice.163
  31.4 1.3 dynamic-slice_bitcast_fusion
  32.8 1.6 gather_fusion
  34.4 1.6 gather_fusion.1
  38.4 4.0 %all-gather.3.cloned.1.call-done = f32[4,1024,128]{2,1,0:T(8,128)} async-done(((f32[1,1024,128]{2,1,0:T(8,128)}), f32[4,1024,128]{2,1,0:T(8,128)}) %all-gather.3.cloned.1.call-update) | async-done | bytes 2097168 | tf_op jit(solution)/shard_map/all_gather | solution.py:89
  42.4 2.9 %fusion.180 = (f32[1,1024,128]{2,1,0:T(8,128)}, f32[1,1024,128]{2,1,0:T(8,128)}, f32[1,1024,128]{2,1,0:T(8,128)}, f32[1,1024,128]{2,1,0:T(8,128)}) fusion(f32[4,1024,128]{2,1,0:T(8,128)} %all-gather.3.cloned.1.call-done), kind=kLoop, calls=%fused_computation.437 | loop fusion | bytes 4194304 | tf_op jit(solution)/shard_map/slice | solution.py:103
  45.2 2.0 %copy.242 = f32[1,1024,128]{1,2,0:T(8,128)} copy(f32[1,1024,128]{2,1,0:T(8,128)} %get-tuple-element.77) | data formatting | bytes 1048576
  47.3 4.8 %fusion.54 = (bf16[1,1024,128]{1,2,0:T(8,128)(2,1)}, bf16[1,1024,128]{1,2,0:T(8,128)(2,1)}, bf16[1,1024,128]{1,2,0:T(8,128)(2,1)}, bf16[1,1024,128]{1,2,0:T(8,128)(2,1)}) fusion(f32[1,1024,128]{1,2,0:T(8,128)} %copy.242, f32[]{:T(128)} %bitcast, bf16[1,2,1024,128]{2,3,1,0:T(8,128)(2,1)} %fusion.92, bf16[1,1,1024,128]{2,3,1,0:T(8,128)(2,1)S(1)} %copy.245, ...), kind=kLoop, calls=%fused_computation.231 | loop fusion | flops 2883584 | bytes 2621444 | tf_op jit(solution)/shard_map/slice | solution.py:51
  53.2 1.8 copy.227
  55.2 1.3 convolution_add_fusion.46
  60.2 1.8 copy.229
  62.0 1.3 convolution_add_fusion.43
  63.3 1.4 fusion.2
  71.2 1.3 fusion.45
  74.9 1.4 copy_select_fusion.2
  77.6 1.6 gather_fusion.2
  80.4 1.8 copy.156
  82.2 1.8 copy.165
  84.0 1.4 maximum_select_fusion.1
  85.5 1.4 maximum_select_fusion.3
  86.8 3.8 %fusion.62 = (bf16[1,1024,128]{1,2,0:T(8,128)(2,1)}, bf16[1,1024,128]{1,2,0:T(8,128)(2,1)}, f32[1,1024,128]{1,2,0:T(8,128)}, bf16[1,1024,128]{1,2,0:T(8,128)(2,1)}, bf16[1,1024,128]{1,2,0:T(8,128)(2,1)}) fusion(f32[1,1024,128]{1,2,0:T(8,128)S(1)} %copy.246, f32[]{:T(128)} %bitcast, bf16[2,1024,128]{1,2,0:T(8,128)(2,1)S(1)} %maximum_select_fusion.1, ...), kind=kLoop, calls=%fused_computation.239 | loop fusion | flops 3407872 | bytes 3145736 | tf_op jit(solution)/shard_map/slice | solution.py:51
  97.6 1.4 fusion.6
  103.8 1.8 copy.176
  107.6 1.4 copy_select_fusion.1
  109.1 1.6 gather_fusion.3
  110.6 1.3 copy.247
  111.9 1.6 scatter-add.14
  116.2 3.6 %fusion.72 = (bf16[1,1024,128]{1,2,0:T(8,128)(2,1)S(1)}, bf16[1,1024,128]{1,2,0:T(8,128)(2,1)}, f32[4,1024,128]{1,2,0:T(8,128)}, bf16[1,1024,128]{1,2,0:T(8,128)(2,1)S(1)}, bf16[1,1024,128]{1,2,0:T(8,128)(2,1)S(1)}) fusion(f32[1,1024,128]{1,2,0:T(8,128)S(1)} %copy.247, f32[]{:T(128)} %bitcast, bf16[2,1024,128]{1,2,0:T(8,128)(2,1)S(1)} %maximum_select_fusion.5, ...), kind=kLoop, calls=%fused_computation.249 | loop fusion | flops 3407872 | bytes 3146244 | tf_op jit(solution)/shard_map/slice | solution.py:51
  135.1 4.9 %fusion.83 = (bf16[1,1024,128]{1,2,0:T(8,128)(2,1)S(1)}, bf16[1,1024,128]{1,2,0:T(8,128)(2,1)S(1)}, f32[4,1024,128]{1,2,0:T(8,128)}, bf16[1,1024,128]{1,2,0:T(8,128)(2,1)S(1)}, bf16[1,1024,128]{1,2,0:T(8,128)(2,1)S(1)}) fusion(f32[1,1024,128]{1,2,0:T(8,128)S(1)} %copy.248, f32[]{:T(128)} %bitcast, bf16[2,1024,128]{1,2,0:T(8,128)(2,1)S(1)} %maximum_select_fusion.9, ...), kind=kLoop, calls=%fused_computation.260 | loop fusion | flops 3538944 | bytes 3670532 | tf_op jit(solution)/shard_map/slice | solution.py:51
  148.0 1.6 copy.255
  153.5 29.6 %all_to_all.5 = f32[4,1,1024,128]{2,3,1,0:T(8,128)S(1)} all-to-all(f32[4,1,1024,128]{2,3,1,0:T(8,128)S(1)} %bitcast.422), channel_id=1, replica_groups=mesh['depth'=4,'xline'=32] {'depth'}, dimensions={0} | all-to-all | bytes 4194304 | tf_op jit(solution)/shard_map/all_to_all | solution.py:31
  (203 shorter events, 67.5 us)
Async XLA Ops:
  6.5 35.8 %all-gather.3.cloned.1.call-start = ((), (), s32[]{:S(2)}) async-start(), calls=%async_computation.1 | async-start | bytes 2621440 | tf_op jit(solution)/shard_map/all_gather | solution.py:89
  32.8 3.2 %copy-start.11 = (s32[256]{0:T(256)S(1)}, s32[256]{0:T(256)}, u32[]{:S(2)}) copy-start(s32[256]{0:T(256)} %param.24) | copy-start | bytes 3076
  32.8 3.2 %copy-start.12 = (bf16[4,2,256]{2,1,0:T(2,128)(2,1)S(1)}, bf16[4,2,256]{2,1,0:T(2,128)(2,1)}, u32[]{:S(2)}) copy-start(bf16[4,2,256]{2,1,0:T(2,128)(2,1)} %param.22) | copy-start | bytes 12292
  32.8 3.2 %copy-start.13 = (s32[256]{0:T(256)S(1)}, s32[256]{0:T(256)}, u32[]{:S(2)}) copy-start(s32[256]{0:T(256)} %param.23) | copy-start | bytes 3076
  36.8 1.4 copy-start.1
  55.0 1.6 copy-start.2
  58.0 7.7 %collective-permute-start = (bf16[2,512,128]{2,1,0:T(8,128)(2,1)}, bf16[2,512,128]{2,1,0:T(8,128)(2,1)}, u32[]{:S(2)}, u32[]{:S(2)}) collective-permute-start(bf16[2,512,128]{2,1,0:T(8,128)(2,1)} %get-tuple-element.136), channel_id=1, source_target_pairs={{0,1},{1,0},{2,3},{3,2},{4,5},{5,4},{6,7},{7,6},{8,9},{9,8},{10,11... | collective-permute-start | bytes 786440 | tf_op jit(solution)/shard_map/ppermute | solution.py:14
  63.3 2.4 %copy-start.8 = (bf16[2,512,128]{2,1,0:T(8,128)(2,1)S(1)}, bf16[2,512,128]{2,1,0:T(8,128)(2,1)}, u32[]{:S(2)}) copy-start(bf16[2,512,128]{2,1,0:T(8,128)(2,1)} %get-tuple-element.135) | copy-start | bytes 786436
  65.1 2.3 %collective-permute-start.2 = (bf16[2,512,128]{2,1,0:T(8,128)(2,1)S(1)}, bf16[2,512,128]{2,1,0:T(8,128)(2,1)S(1)}, u32[]{:S(2)}, u32[]{:S(2)}) collective-permute-start(bf16[2,512,128]{2,1,0:T(8,128)(2,1)S(1)} %get-tuple-element.142), channel_id=1, source_target_pairs={{0,1},{1,0},{2,3},{3,2},{4,5},{5,4},{6,7},{7,6},{8,9},{9,8},{10,11... | collective-permute-start | bytes 786440 | tf_op jit(solution)/shard_map/ppermute | solution.py:14
  71.1 12.9 %collective-permute-start.1 = (bf16[2,512,128]{1,2,0:T(8,128)(2,1)}, bf16[2,512,128]{1,2,0:T(8,128)(2,1)}, u32[]{:S(2)}, u32[]{:S(2)}) collective-permute-start(bf16[2,512,128]{1,2,0:T(8,128)(2,1)} %bitcast.481), channel_id=1, source_target_pairs={{0,1},{1,0},{2,3},{3,2},{4,5},{5,4},{6,7},{7,6},{8,9},{9,8},{10,11... | collective-permute-start | bytes 786440 | tf_op jit(solution)/shard_map/ppermute | solution.py:14
  74.4 11.1 %collective-permute-start.3 = (bf16[2,512,128]{1,2,0:T(8,128)(2,1)}, bf16[2,512,128]{1,2,0:T(8,128)(2,1)}, u32[]{:S(2)}, u32[]{:S(2)}) collective-permute-start(bf16[2,512,128]{1,2,0:T(8,128)(2,1)} %bitcast.39), channel_id=1, source_target_pairs={{0,1},{1,0},{2,3},{3,2},{4,5},{5,4},{6,7},{7,6},{8,9},{9,8},{10,11... | collective-permute-start | bytes 786440 | tf_op jit(solution)/shard_map/ppermute | solution.py:14
  93.8 1.2 copy-start.7
  94.9 5.0 %collective-permute-start.4 = (bf16[2,512,128]{2,1,0:T(8,128)(2,1)}, bf16[2,512,128]{2,1,0:T(8,128)(2,1)}, u32[]{:S(2)}, u32[]{:S(2)}) collective-permute-start(bf16[2,512,128]{2,1,0:T(8,128)(2,1)} %get-tuple-element.125), channel_id=1, source_target_pairs={{0,1},{1,0},{2,3},{3,2},{4,5},{5,4},{6,7},{7,6},{8,9},{9,8},{10,11... | collective-permute-start | bytes 786440 | tf_op jit(solution)/shard_map/ppermute | solution.py:14
  97.6 2.3 %copy-start.9 = (bf16[2,512,128]{2,1,0:T(8,128)(2,1)S(1)}, bf16[2,512,128]{2,1,0:T(8,128)(2,1)}, u32[]{:S(2)}) copy-start(bf16[2,512,128]{2,1,0:T(8,128)(2,1)} %get-tuple-element.124) | copy-start | bytes 786436
  99.3 2.3 %collective-permute-start.6 = (bf16[2,512,128]{2,1,0:T(8,128)(2,1)S(1)}, bf16[2,512,128]{2,1,0:T(8,128)(2,1)S(1)}, u32[]{:S(2)}, u32[]{:S(2)}) collective-permute-start(bf16[2,512,128]{2,1,0:T(8,128)(2,1)S(1)} %get-tuple-element.132), channel_id=1, source_target_pairs={{0,1},{1,0},{2,3},{3,2},{4,5},{5,4},{6,7},{7,6},{8,9},{9,8},{10,11... | collective-permute-start | bytes 786440 | tf_op jit(solution)/shard_map/ppermute | solution.py:14
  105.6 8.2 %collective-permute-start.5 = (bf16[2,512,128]{1,2,0:T(8,128)(2,1)}, bf16[2,512,128]{1,2,0:T(8,128)(2,1)}, u32[]{:S(2)}, u32[]{:S(2)}) collective-permute-start(bf16[2,512,128]{1,2,0:T(8,128)(2,1)} %bitcast.480), channel_id=1, source_target_pairs={{0,1},{1,0},{2,3},{3,2},{4,5},{5,4},{6,7},{7,6},{8,9},{9,8},{10,11... | collective-permute-start | bytes 786440 | tf_op jit(solution)/shard_map/ppermute | solution.py:14
  107.1 7.9 %collective-permute-start.7 = (bf16[2,512,128]{1,2,0:T(8,128)(2,1)}, bf16[2,512,128]{1,2,0:T(8,128)(2,1)}, u32[]{:S(2)}, u32[]{:S(2)}) collective-permute-start(bf16[2,512,128]{1,2,0:T(8,128)(2,1)} %bitcast.64), channel_id=1, source_target_pairs={{0,1},{1,0},{2,3},{3,2},{4,5},{5,4},{6,7},{7,6},{8,9},{9,8},{10,11... | collective-permute-start | bytes 786440 | tf_op jit(solution)/shard_map/ppermute | solution.py:14
  109.0 2.9 %copy-start.3 = (f32[1,1024,128]{1,2,0:T(8,128)S(1)}, f32[1,1024,128]{1,2,0:T(8,128)}, u32[]{:S(2)}) copy-start(f32[1,1024,128]{1,2,0:T(8,128)} %get-tuple-element.126) | copy-start | bytes 1572868
  110.6 2.9 %copy-start.5 = (bf16[2,512,1,128]{3,1,2,0:T(8,128)(2,1)S(1)}, bf16[2,512,1,128]{3,1,2,0:T(8,128)(2,1)}, u32[]{:S(2)}) copy-start(bf16[2,512,1,128]{3,1,2,0:T(8,128)(2,1)} %get-tuple-element.122) | copy-start | bytes 786436
  123.2 2.2 %collective-permute-start.8 = (bf16[2,512,128]{2,1,0:T(8,128)(2,1)}, bf16[2,512,128]{2,1,0:T(8,128)(2,1)}, u32[]{:S(2)}, u32[]{:S(2)}) collective-permute-start(bf16[2,512,128]{2,1,0:T(8,128)(2,1)} %get-tuple-element.114), channel_id=1, source_target_pairs={{0,1},{1,0},{2,3},{3,2},{4,5},{5,4},{6,7},{7,6},{8,9},{9,8},{10,11... | collective-permute-start | bytes 786440 | tf_op jit(solution)/shard_map/ppermute | solution.py:14
  124.1 1.2 copy-start.10
  124.8 2.3 %collective-permute-start.10 = (bf16[2,512,128]{2,1,0:T(8,128)(2,1)S(1)}, bf16[2,512,128]{2,1,0:T(8,128)(2,1)S(1)}, u32[]{:S(2)}, u32[]{:S(2)}) collective-permute-start(bf16[2,512,128]{2,1,0:T(8,128)(2,1)S(1)} %get-tuple-element.121), channel_id=1, source_target_pairs={{0,1},{1,0},{2,3},{3,2},{4,5},{5,4},{6,7},{7,6},{8,9},{9,8},{10,11... | collective-permute-start | bytes 786440 | tf_op jit(solution)/shard_map/ppermute | solution.py:14
  130.0 2.1 %copy-start = (bf16[4,2,256,256]{3,2,1,0:T(8,128)(2,1)S(1)}, bf16[4,2,256,256]{3,2,1,0:T(8,128)(2,1)}, u32[]{:S(2)}) copy-start(bf16[4,2,256,256]{3,2,1,0:T(8,128)(2,1)} %gather_fusion.3) | copy-start | bytes 3145732
  130.0 2.8 %collective-permute-start.9 = (bf16[2,512,128]{1,2,0:T(8,128)(2,1)}, bf16[2,512,128]{1,2,0:T(8,128)(2,1)}, u32[]{:S(2)}, u32[]{:S(2)}) collective-permute-start(bf16[2,512,128]{1,2,0:T(8,128)(2,1)} %bitcast.482), channel_id=1, source_target_pairs={{0,1},{1,0},{2,3},{3,2},{4,5},{5,4},{6,7},{7,6},{8,9},{9,8},{10,11... | collective-permute-start | bytes 786440 | tf_op jit(solution)/shard_map/ppermute | solution.py:14
  130.7 1.5 copy-start.4
  130.8 1.6 copy-start.6
  131.7 2.2 %collective-permute-start.11 = (bf16[2,512,128]{1,2,0:T(8,128)(2,1)}, bf16[2,512,128]{1,2,0:T(8,128)(2,1)}, u32[]{:S(2)}, u32[]{:S(2)}) collective-permute-start(bf16[2,512,128]{1,2,0:T(8,128)(2,1)} %bitcast.89), channel_id=1, source_target_pairs={{0,1},{1,0},{2,3},{3,2},{4,5},{5,4},{6,7},{7,6},{8,9},{9,8},{10,11... | collective-permute-start | bytes 786440 | tf_op jit(solution)/shard_map/ppermute | solution.py:14
  141.5 2.3 %collective-permute-start.14 = (bf16[2,512,128]{2,1,0:T(8,128)(2,1)S(1)}, bf16[2,512,128]{2,1,0:T(8,128)(2,1)S(1)}, u32[]{:S(2)}, u32[]{:S(2)}) collective-permute-start(bf16[2,512,128]{2,1,0:T(8,128)(2,1)S(1)} %get-tuple-element.110), channel_id=1, source_target_pairs={{0,1},{1,0},{2,3},{3,2},{4,5},{5,4},{6,7},{7,6},{8,9},{9,8},{10,11... | collective-permute-start | bytes 786440 | tf_op jit(solution)/shard_map/ppermute | solution.py:14
  143.4 1.6 collective-permute-start.12
  147.2 2.7 %collective-permute-start.15 = (bf16[2,512,128]{1,2,0:T(8,128)(2,1)S(1)}, bf16[2,512,128]{1,2,0:T(8,128)(2,1)}, u32[]{:S(2)}, u32[]{:S(2)}) collective-permute-start(bf16[2,512,128]{1,2,0:T(8,128)(2,1)S(1)} %bitcast.484), channel_id=1, source_target_pairs={{0,1},{1,0},{2,3},{3,2},{4,5},{5,4},{6,7},{7,6},{8,9},{9,8},{10,11... | collective-permute-start | bytes 786440 | tf_op jit(solution)/shard_map/ppermute | solution.py:14
  147.7 3.4 %collective-permute-start.13 = (bf16[2,512,128]{1,2,0:T(8,128)(2,1)S(1)}, bf16[2,512,128]{1,2,0:T(8,128)(2,1)}, u32[]{:S(2)}, u32[]{:S(2)}) collective-permute-start(bf16[2,512,128]{1,2,0:T(8,128)(2,1)S(1)} %bitcast.483), channel_id=1, source_target_pairs={{0,1},{1,0},{2,3},{3,2},{4,5},{5,4},{6,7},{7,6},{8,9},{9,8},{10,11... | collective-permute-start | bytes 786440 | tf_op jit(solution)/shard_map/ppermute | solution.py:14
Sparse Core Ops, SparseCore 0:
  9.0 33.3 all-gather.2
where the time goes:
time: 193 us; the launch traced here: 191 us
  local copies, waits for them, and re-layouts  49.1 us (25%)
  other arithmetic  43.1 us (22%)
  blocking collectives  39.6 us (21%)
  matrix products  25.9 us (13%)
  between operations  23.4 us (12%)
  waiting for transfers between devices  5.27 us (3%)
  starting transfers between devices  4.67 us (2%)
    all_to_all x1, blocking collectives, sum_at_owner(): blocks = lax.all_to_all(cut_along(value, dim, size), axis, 0, 0, tiled=True)  29.6 us
    dot_general x64, matrix products, blockwise(): return jnp.einsum(form, matrix, vector, preferred_element_type=jnp.float32)  25.2 us
    slice x4, other arithmetic, complex_apply(): parts[1]  17.1 us
    select_n x16, other arithmetic, assemble(): jnp.where(parity == 0, jnp.concatenate([kept, got], axis), jnp.concatenat...  14.2 us
    all_gather x1, blocking collectives, in_one_piece(): filled = lax.all_gather(both, axis, axis=dim, tiled=True)  9.99 us
    unnamed x35, local copies, waits for them, and re-layouts  7.88 us
    squeeze x8, local copies, waits for them, and re-layouts, complex_apply(): parts[1]  6.49 us
    another operation x15, other arithmetic, complex_apply(): return jnp.stack([out_real, out_imag]).astype(jnp.bfloat16)  6.47 us
  transfers between devices with their start and end apart: 17, of which 2 were waited for; matrix products, arithmetic and copies ran while one was open for 32% of the time, Pallas kernels for 0%

commit v1 on v0

v1 whole, which is shorter than its diff:
```python
import math

import jax
import jax.numpy as jnp
from jax import lax
from jax.experimental import pallas as pl
from jax.experimental.pallas import tpu as pltpu
from jax.sharding import PartitionSpec as P

F32 = jnp.float32
BF16 = jnp.bfloat16
I32 = jnp.int32
I16 = jnp.int16

SECTIONS = 4
LEVELS = 4
FREQS = 4
MINE = 2
B = 256
H = 128
EXTRA = 16

MIDDLE = 1.1
STEPS = 36000.0

SIN = (4.4428679, -7.30744341, 3.59478797, -0.78437374)
COS = (1.4142135, -6.97885099, 5.73946117, -1.88356295, 0.3106981)

MB = 1 << 20


def horner(u, coefs):
    total = coefs[-1]
    for c in coefs[-2::-1]:
        total = total * u + c
    return total


def place():
    line = lax.axis_index("xline")
    return lax.axis_index("depth"), line // 2, lax.rem(line, 2)


def pack_kernel(slow, zones_x, zones_y, receiver, q0, q1, q2, q3, rec_own, rec_send, sems):
    section, pair, core = place()
    rows = pl.ds(section * B, B)
    copies = [
        pltpu.make_async_copy(
            receiver.at[pl.ds(which * MINE, MINE), :, rows, :], out, sems.at[k]
        )
        for k, (which, out) in enumerate(((1 - core, rec_send), (core, rec_own)))
    ]
    for copy in copies:
        copy.start()
    zone_y = zones_y[0, pair]
    upper = lax.broadcasted_iota(I32, (EXTRA, H), 0) < EXTRA // 2
    for shift, q in enumerate((q0, q1, q2, q3)):
        to = lax.rem(section + shift, SECTIONS)
        start = pl.multiple_of(to * B, B)
        for r in range(0, B, 32):
            value = slow[0, pl.ds(start + r, 32), :]
            level = jnp.clip((value - MIDDLE) * STEPS, -32767.0, 32767.0)
            q[r : r + 32, :] = jnp.round(level).astype(I32).astype(I16)
        q[B:, :] = jnp.where(upper, zones_x[0, to], zone_y).astype(I16)
    for copy in copies:
        copy.wait()


def pack(slowness, zones_x, zones_y, receiver):
    block = jax.ShapeDtypeStruct((B + EXTRA, H), I16)
    part = jax.ShapeDtypeStruct((MINE, 2, B, H), BF16)
    vmem = pl.BlockSpec(memory_space=pltpu.VMEM)
    smem = pl.BlockSpec(memory_space=pltpu.SMEM)
    hbm = pl.BlockSpec(memory_space=pl.ANY)
    return pl.pallas_call(
        pack_kernel,
        out_shape=[block] * 4 + [part] * 2,
        in_specs=[vmem, smem, smem, hbm],
        out_specs=[vmem] * 4 + [hbm] * 2,
        scratch_shapes=[pltpu.SemaphoreType.DMA((2,))],
        name="pack",
    )(slowness, zones_x, zones_y, receiver)


def prepare_kernel(amp, source_x, source_y, inverses, sources, operators, table, spread, sem):
    section, pair, core = place()
    copy = pltpu.make_async_copy(inverses.at[pl.ds(core * MINE, MINE)], table, sem)
    copy.start()
    count = source_x.shape[1]
    cells = lax.broadcasted_iota(I32, (B, count), 0)
    hot_x = jnp.where(cells + section * B == source_x[...], 1.0, 0.0).astype(BF16)
    hot_y = cells + pair * B == source_y[...]
    for f in range(MINE):
        for part in range(2):
            row = amp[pl.ds(core * MINE + f, 1), part, :].astype(F32)
            spread[part * B : (part + 1) * B, :] = jnp.where(hot_y, row, 0.0).astype(BF16)
        sources[f] = lax.dot_general(
            hot_x, spread[...], (((1,), (1,)), ((), ())), preferred_element_type=F32
        ).astype(BF16)
    copy.wait()
    for f in range(MINE):
        for zone in range(table.shape[1]):
            real = table[f, zone, 0]
            imag = table[f, zone, 1]
            operators[f, zone, :B, :B] = real
            operators[f, zone, B:, B:] = real
            operators[f, zone, B:, :B] = imag
            operators[f, zone, :B, B:] = -imag


def prepare(amp, source_x, source_y, inverses):
    zones = inverses.shape[1]
    vmem = pl.BlockSpec(memory_space=pltpu.VMEM)
    hbm = pl.BlockSpec(memory_space=pl.ANY)
    return pl.pallas_call(
        prepare_kernel,
        out_shape=[
            jax.ShapeDtypeStruct((MINE, B, 2 * B), BF16),
            jax.ShapeDtypeStruct((MINE, zones, 2 * B, 2 * B), BF16),
        ],
        in_specs=[vmem, vmem, vmem, hbm],
        out_specs=[vmem, vmem],
        scratch_shapes=[
            pltpu.VMEM((MINE, zones, 2, B, B), BF16),
            pltpu.VMEM((2 * B, source_x.shape[1]), BF16),
            pltpu.SemaphoreType.DMA,
        ],
        compiler_params=pltpu.CompilerParams(vmem_limit_bytes=24 * MB),
        cost_estimate=pl.CostEstimate(
            flops=4 * B**3 * 4, bytes_accessed=8 * MB, transcendentals=0
        ),
        name="prepare",
    )(amp, source_x, source_y, inverses)


def continue_kernel(
    omegas, sources, operators, rec_mine, rec_other,
    q0, q1, q2, q3, p0, p1, p2, p3,
    grad_mine, grad_other,
    slow, zones, W, X, Y,
):
    section, _, core = place()
    mine = pl.ds(pl.multiple_of(core * H, H), H)
    other = pl.ds(pl.multiple_of((1 - core) * H, H), H)

    for shift, (q, p) in enumerate(((q0, p0), (q1, p1), (q2, p2), (q3, p3))):
        level = lax.rem(section + SECTIONS - shift, SECTIONS)
        for r in range(0, B, 32):
            slow[level, r : r + 32, mine] = q[r : r + 32, :].astype(I32).astype(F32)
            slow[level, r : r + 32, other] = p[r : r + 32, :].astype(I32).astype(F32)
        marks = q[B:, :].astype(I32)
        zones[level, 0] = jnp.max(marks[: EXTRA // 2])
        zones[level, 1] = jnp.max(marks[EXTRA // 2 :])

    for f in range(MINE):
        W[f, :B, :] = sources[f]
        for columns, rec in ((mine, rec_mine), (other, rec_other)):
            W[f, B:, columns] = rec[f, 0]
        imag_mine = pl.ds(pl.multiple_of(B + core * H, H), H)
        imag_other = pl.ds(pl.multiple_of(B + (1 - core) * H, H), H)
        for columns, rec in ((imag_mine, rec_mine), (imag_other, rec_other)):
            W[f, B:, columns] = -rec[f, 1]

    def one_level(level, carry):
        zone_x = zones[level, 0]
        zone_y = zones[level, 1]
        for f in range(MINE):
            omega = omegas[core * MINE + f]
            scale = omega * (0.5 / math.pi / STEPS)
            base = omega * (0.5 / math.pi * MIDDLE) - 0.5
            for c in range(0, B, H):
                for r in range(0, B, 32):
                    turn = slow[level, r : r + 32, c : c + H] * scale + base
                    square = turn * turn
                    half_sin = turn * horner(square, SIN)
                    half_cos = horner(square, COS)
                    cosine = half_sin * half_sin - 1.0
                    sine = -half_sin * half_cos
                    for wave in range(0, 2 * B, B):
                        real = W[f, wave + r : wave + r + 32, c : c + H].astype(F32)
                        imag = W[f, wave + r : wave + r + 32, B + c : B + c + H].astype(F32)
                        X[f, r : r + 32, wave + c : wave + c + H] = (
                            real * cosine - imag * sine
                        ).astype(BF16)
                        X[f, B + r : B + r + 32, wave + c : wave + c + H] = (
                            real * sine + imag * cosine
                        ).astype(BF16)
        for f in range(MINE):
            for wave in range(0, 2 * B, B):
                update = jnp.dot(
                    operators[f, zone_x], X[f, :, wave : wave + B], preferred_element_type=F32
                )
                for part in range(0, 2 * B, B):
                    Y[f, wave : wave + B, part : part + B] = (
                        X[f, part : part + B, wave : wave + B].astype(F32)
                        + update[part : part + B]
                    ).astype(BF16)
        for f in range(MINE):
            for part in range(0, 2 * B, B):
                update = lax.dot_general(
                    Y[f],
                    operators[f, zone_y, part : part + B, :],
                    (((1,), (1,)), ((), ())),
                    preferred_element_type=F32,
                )
                W[f, :, part : part + B] = (
                    Y[f, :, part : part + B].astype(F32) + update
                ).astype(BF16)
        for out, offset in ((grad_mine, core * H), (grad_other, (1 - core) * H)):
            real_at = pl.ds(pl.multiple_of(offset, H), H)
            imag_at = pl.ds(pl.multiple_of(B + offset, H), H)
            for r in range(0, B, 32):
                total = None
                for f in range(MINE):
                    omega = omegas[core * MINE + f]
                    down = slice(r, r + 32)
                    up = slice(B + r, B + r + 32)
                    term = W[f, down, real_at].astype(F32) * W[f, up, real_at].astype(F32)
                    term -= W[f, down, imag_at].astype(F32) * W[f, up, imag_at].astype(F32)
                    term *= omega * omega
                    total = term if total is None else total + term
                out[level, r : r + 32, :] = total.astype(out.dtype)
        return carry

    lax.fori_loop(0, LEVELS, one_level, 0)


def continue_all(omegas, sources, operators, rec_mine, rec_other, mine, other):
    vmem = pl.BlockSpec(memory_space=pltpu.VMEM)
    smem = pl.BlockSpec(memory_space=pltpu.SMEM)
    return pl.pallas_call(
        continue_kernel,
        out_shape=[
            jax.ShapeDtypeStruct((LEVELS, B, H), F32),
            jax.ShapeDtypeStruct((LEVELS, B, H), BF16),
        ],
        in_specs=[smem] + [vmem] * 12,
        out_specs=[vmem, vmem],
        scratch_shapes=[
            pltpu.VMEM((LEVELS, B, B), F32),
            pltpu.SMEM((LEVELS, 2), I32),
            pltpu.VMEM((MINE, 2 * B, 2 * B), BF16),
            pltpu.VMEM((MINE, 2 * B, 2 * B), BF16),
            pltpu.VMEM((MINE, 2 * B, 2 * B), BF16),
        ],
        compiler_params=pltpu.CompilerParams(vmem_limit_bytes=32 * MB),
        cost_estimate=pl.CostEstimate(
            flops=2 * 128 * B**3, bytes_accessed=8 * MB, transcendentals=0
        ),
        name="continue_levels",
    )(omegas, sources, operators, rec_mine, rec_other, *mine, *other)


def merge_kernel(mine, got, own, s1, s2, s3):
    section, _, _ = place()
    for shift, out in enumerate((own, s1, s2, s3)):
        level = lax.rem(section + shift, SECTIONS)
        out[...] = (mine[level] + got[level].astype(F32)).astype(out.dtype)


def merge(mine, got):
    vmem = pl.BlockSpec(memory_space=pltpu.VMEM)
    return pl.pallas_call(
        merge_kernel,
        out_shape=[jax.ShapeDtypeStruct((B, H), F32)]
        + [jax.ShapeDtypeStruct((B, H), BF16)] * 3,
        in_specs=[vmem, vmem],
        out_specs=[vmem] * 4,
        name="merge",
    )(mine, got)


def assemble_kernel(own, g1, g2, g3, out):
    section, _, _ = place()
    for shift, block in enumerate((own, g1, g2, g3)):
        origin = lax.rem(section + SECTIONS - shift, SECTIONS)
        out[0, pl.ds(pl.multiple_of(origin * B, B), B), :] = block[...].astype(F32)


def assemble(own, blocks):
    vmem = pl.BlockSpec(memory_space=pltpu.VMEM)
    return pl.pallas_call(
        assemble_kernel,
        out_shape=jax.ShapeDtypeStruct((1, SECTIONS * B, H), F32),
        in_specs=[vmem] * 4,
        out_specs=vmem,
        name="assemble",
    )(own, *blocks)


def along_depth(block, shift):
    return lax.ppermute(block, "depth", [(i, (i + shift) % SECTIONS) for i in range(SECTIONS)])


def other_core(block):
    count = lax.axis_size("xline")
    return lax.ppermute(block, "xline", [(i, i ^ 1) for i in range(count)])


def per_device(
    receiver_data, source_amp, source_x, source_y, omegas, slowness, inverses, zones_x, zones_y
):
    *blocks, rec_mine, rec_send = pack(slowness, zones_x, zones_y, receiver_data)
    mine = [blocks[0]] + [along_depth(blocks[k], k) for k in (1, 2, 3)]
    other = [other_core(block) for block in mine]
    rec_other = other_core(rec_send)
    sources, operators = prepare(
        source_amp, source_x.reshape(1, -1), source_y.reshape(1, -1), inverses
    )
    grad_mine, grad_other = continue_all(
        omegas, sources, operators, rec_mine, rec_other, mine, other
    )
    own, *parts = merge(grad_mine, other_core(grad_other))
    return assemble(own, [along_depth(parts[k - 1], k) for k in (1, 2, 3)])


def solution(mesh):
    in_specs = (
        P(None, None, None, "xline"),
        P(),
        P(),
        P(),
        P(),
        P("depth", None, "xline"),
        P(),
        P("depth", None),
        P("depth", None),
    )
    return jax.shard_map(
        per_device,
        mesh=mesh,
        in_specs=in_specs,
        out_specs=P("depth", None, "xline"),
        check_vma=False,
    )
```

time: 193 us -> 58.9 us (0.31)
  other arithmetic: 43.1 us -> 0 us
  local copies, waits for them, and re-layouts: 49.1 us -> 6.47 us
  blocking collectives: 39.6 us -> 0 us
  Pallas kernels: 0 us -> 32.6 us
  matrix products: 25.9 us -> 0 us
  between operations: 23.4 us -> 0.11 us
  starting transfers between devices: 4.67 us -> 11.7 us
  waiting for transfers between devices: 5.27 us -> 7.7 us
    pallas_call x0 -> x5, Pallas kernels: none -> 32.6 us  [the longest x1 18.8 us: pack(): pl.pallas_call(pack_kernel, out_shape=[block] * 4 + [part] * 2, in_specs=...]
    all_to_all x1 -> x0, blocking collectives: 29.6 us -> none  [sum_at_owner(): blocks = lax.all_to_all(cut_along(value, dim, size), axis, 0, 0, tiled=True)]
    dot_general x65 -> x0, matrix products: 25.9 us -> none  [the longest x64 25.2 us: blockwise(): return jnp.einsum(form, matrix, vector, preferred_element_type=jnp.float32)]
    select_n x21 -> x0, other arithmetic: 17.4 us -> none  [the longest x16 14.2 us: assemble(): jnp.where(parity == 0, jnp.concatenate([kept, got], axis), jnp.concatenat...]
    slice x4 -> x0, other arithmetic: 17.1 us -> none  [complex_apply(): parts[1]]
    dynamic_slice x22 -> x0, local copies, waits for them, and re-layouts: 15.4 us -> none  [the longest x4 3.67 us: per_device(): lax.dynamic_slice_in_dim(solved_src, other_rows, width_y, 2)]
    squeeze x17 -> x0, local copies, waits for them, and re-layouts: 12.9 us -> none  [the longest x8 6.49 us: complex_apply(): parts[1]]
    all_gather x1 -> x0, blocking collectives: 9.99 us -> none  [in_one_piece(): filled = lax.all_gather(both, axis, axis=dim, tiled=True)]
  transfers between devices with their start and end apart: 17 -> 12, of which waited for: 2 -> 7; matrix products, arithmetic and copies ran while one was open for 32% -> 0% of each run, Pallas kernels for 0% -> 1%
where the time goes in v1:
time: 58.9 us; the launch traced here: 58.6 us
  Pallas kernels  32.6 us (55%)
  starting transfers between devices  11.7 us (20%)
  waiting for transfers between devices  7.7 us (13%)
  local copies, waits for them, and re-layouts  6.47 us (11%)
    pallas_call x1, Pallas kernels, pack(): pl.pallas_call(pack_kernel, out_shape=[block] * 4 + [part] * 2, in_specs=...  18.8 us
    ppermute x6, starting transfers between devices, along_depth(): lax.ppermute(block, 'depth', [(i, (i + shift) % SECTIONS) for i in range(...  10.8 us
    pallas_call x1, Pallas kernels, continue_all(): pl.pallas_call(continue_kernel, out_shape=[jax.ShapeDtypeStruct((LEVELS,...  9.33 us
    unnamed x24, local copies, waits for them, and re-layouts  6.47 us
    ppermute x6, waiting for transfers between devices, along_depth(): lax.ppermute(block, 'depth', [(i, (i + shift) % SECTIONS) for i in range(...  6.46 us
    pallas_call x1, Pallas kernels, merge(): pl.pallas_call(merge_kernel, out_shape=[jax.ShapeDtypeStruct((B, H), F32)...  1.88 us
    pallas_call x1, Pallas kernels, assemble(): pl.pallas_call(assemble_kernel, out_shape=jax.ShapeDtypeStruct((1, SECTIO...  1.8 us
    ppermute x6, waiting for transfers between devices, other_core(): return lax.ppermute(block, 'xline', [(i, i ^ 1) for i in range(count)])  1.24 us
  transfers between devices with their start and end apart: 12, of which 7 were waited for; matrix products, arithmetic and copies ran while one was open for 0% of the time, Pallas kernels for 1%

profile of v1, /device:TPU:0, one launch (start us, length us, event | category | flops | bytes accessed | tf_op | source)
XLA Modules:
  0.0 58.6 jit_solution(14273932594787160389)
XLA Ops:
  0.0 18.8 %pack.1 = (s16[272,128]{1,0:T(8,128)(2,1)}, s16[272,128]{1,0:T(8,128)(2,1)}, s16[272,128]{1,0:T(8,128)(2,1)}, s16[272,128]{1,0:T(8,128)(2,1)}, bf16[2,2,256,128]...) custom-call(f32[1,1024,128]{2,1,0:T(8,128)} %slow.1, s32[1,4]{1,0:T(1,128)} %zones_x.1, s32[1,16]{1,0:T(1,128)} %zones_y.1, ...), custom_call_target="tpu_custom_call" | custom-call | tf_op jit(solution)/shard_map/pack/pallas_call | solution.py:75
  18.8 0.1 collective-permute-start
  18.9 1.7 %collective-permute-start.1 = (s16[272,128]{1,0:T(8,128)(2,1)}, s16[272,128]{1,0:T(8,128)(2,1)S(1)}, u32[]{:S(2)}, u32[]{:S(2)}) collective-permute-start(s16[272,128]{1,0:T(8,128)(2,1)} %get-tuple-element.24), channel_id=1, source_target_pairs={{0,32},{32,64},{64,96},{96,0},{1,33},{33,65},{65,97},{97,1},{2,34}... | collective-permute-start | bytes 208904 | tf_op jit(solution)/shard_map/ppermute | solution.py:292
  20.7 2.9 %collective-permute-start.2 = (s16[272,128]{1,0:T(8,128)(2,1)}, s16[272,128]{1,0:T(8,128)(2,1)S(1)}, u32[]{:S(2)}, u32[]{:S(2)}) collective-permute-start(s16[272,128]{1,0:T(8,128)(2,1)} %get-tuple-element.25), channel_id=1, source_target_pairs={{0,64},{32,96},{64,0},{96,32},{1,65},{33,97},{65,1},{97,33},{2,66}... | collective-permute-start | bytes 208904 | tf_op jit(solution)/shard_map/ppermute | solution.py:292
  23.6 1.3 %collective-permute-start.3 = (s16[272,128]{1,0:T(8,128)(2,1)}, s16[272,128]{1,0:T(8,128)(2,1)S(1)}, u32[]{:S(2)}, u32[]{:S(2)}) collective-permute-start(s16[272,128]{1,0:T(8,128)(2,1)} %get-tuple-element.26), channel_id=1, source_target_pairs={{0,96},{32,0},{64,32},{96,64},{1,97},{33,1},{65,33},{97,65},{2,98}... | collective-permute-start | bytes 208904 | tf_op jit(solution)/shard_map/ppermute | solution.py:292
  24.9 0.2 collective-permute-done.1.q1
  25.1 0.3 collective-permute-start.5
  25.4 2.3 %collective-permute-done.2.q2 = s16[272,128]{1,0:T(8,128)(2,1)S(1)} collective-permute-done((s16[272,128]{1,0:T(8,128)(2,1)}, s16[272,128]{1,0:T(8,128)(2,1)S(1)}, u32[]{:S(2)}, u32[]{:S(2)}) %collective-permute-start.2) | collective-permute-done | bytes 69664 | tf_op jit(solution)/shard_map/ppermute | solution.py:292
  27.8 0.3 collective-permute-done.3.q3
  28.1 0.2 collective-permute-start.7
  28.3 2.2 %copy-done = bf16[4,4,2,256,256]{4,3,2,1,0:T(8,128)(2,1)S(1)} copy-done((bf16[4,4,2,256,256]{4,3,2,1,0:T(8,128)(2,1)S(1)}, bf16[4,4,2,256,256]{4,3,2,1,0:T(8,128)(2,1)}, u32[]{:S(2)}) %copy-start) | copy-done | bytes 4194328
  30.5 0.7 %copy-done.2 = bf16[4,2,256]{2,1,0:T(2,128)(2,1)S(1)} copy-done((bf16[4,2,256]{2,1,0:T(2,128)(2,1)S(1)}, bf16[4,2,256]{2,1,0:T(2,128)(2,1)}, u32[]{:S(2)}) %copy-start.2) | copy-done | bytes 4120
  31.2 0.7 %copy-done.3 = s32[256]{0:T(256)S(1)} copy-done((s32[256]{0:T(256)S(1)}, s32[256]{0:T(256)}, u32[]{:S(2)}) %copy-start.3) | copy-done | bytes 1048
  31.8 0.7 %copy-done.4 = s32[256]{0:T(256)S(1)} copy-done((s32[256]{0:T(256)S(1)}, s32[256]{0:T(256)}, u32[]{:S(2)}) %copy-start.4) | copy-done | bytes 1048
  32.5 0.8 %prepare.1 = (bf16[2,256,512]{2,1,0:T(8,128)(2,1)S(1)}, bf16[2,4,512,512]{3,2,1,0:T(8,128)(2,1)S(1)}) custom-call(bf16[4,2,256]{2,1,0:T(2,128)(2,1)S(1)} %copy-done.2, s32[1,256]{1,0:T(1,128)S(1)} %bitcast.2, s32[1,256]{1,0:T(1,128)S(1)} %bitcast.3, bf16[4,4,2,256,256]{4,3,2,1,0:T(8,128)(2,1)S(1)} %copy-done), custom_call_target="tpu_custom_call" | custom-call | flops 268435456 | bytes 8388608 | tf_op jit(solution)/shard_map/prepare/pallas_call | solution.py:115
  33.3 0.1 copy-done.5
  33.5 0.0 copy-done.6
  33.5 9.3 %continue_levels.1 = (f32[4,256,128]{2,1,0:T(8,128)S(1)}, bf16[4,256,128]{2,1,0:T(8,128)(2,1)S(1)}) custom-call(f32[4]{0:T(128)S(1)} %copy-done.7, bf16[2,256,512]{2,1,0:T(8,128)(2,1)S(1)} %get-tuple-element.19.sources, bf16[2,4,512,512]{3,2,1,0:T(8,128)(2,1)S(1)} %get-tuple-element.20.operators, bf16[2,2,256,128]{3,2,1,0:T(8,128)(2,1)S(1)} %copy-done.5, ...), custom_call_target="tpu_custom_call" | custom-call | flops 4294967296 | bytes 8388608 | tf_op jit(solution)/shard_map/continue_levels/pallas_call | solution.py:231
  42.8 0.8 %copy-done.1 = f32[4,256,128]{2,1,0:T(8,128)} copy-done((f32[4,256,128]{2,1,0:T(8,128)}, f32[4,256,128]{2,1,0:T(8,128)S(1)}, u32[]{:S(2)}) %copy-start.1) | copy-done | bytes 524312
  43.6 0.3 collective-permute-start.8
  43.9 1.2 %collective-permute-done.8.got = bf16[4,256,128]{2,1,0:T(8,128)(2,1)S(1)} collective-permute-done((bf16[4,256,128]{2,1,0:T(8,128)(2,1)S(1)}, bf16[4,256,128]{2,1,0:T(8,128)(2,1)S(1)}, u32[]{:S(2)}, u32[]{:S(2)}) %collective-permute-start.8) | collective-permute-done | bytes 262176 | tf_op jit(solution)/shard_map/ppermute | solution.py:297
  45.1 0.7 %copy-done.8 = bf16[4,256,128]{2,1,0:T(8,128)(2,1)} copy-done((bf16[4,256,128]{2,1,0:T(8,128)(2,1)}, bf16[4,256,128]{2,1,0:T(8,128)(2,1)S(1)}, u32[]{:S(2)}) %copy-start.8) | copy-done | bytes 262168
  45.8 1.9 %merge.1 = (f32[256,128]{1,0:T(8,128)}, bf16[256,128]{1,0:T(8,128)(2,1)}, bf16[256,128]{1,0:T(8,128)(2,1)}, bf16[256,128]{1,0:T(8,128)(2,1)}) custom-call(f32[4,256,128]{2,1,0:T(8,128)} %copy-done.1, bf16[4,256,128]{2,1,0:T(8,128)(2,1)} %copy-done.8), custom_call_target="tpu_custom_call" | custom-call | tf_op jit(solution)/shard_map/merge/pallas_call | solution.py:263
  47.7 1.2 %collective-permute-start.9 = (bf16[256,128]{1,0:T(8,128)(2,1)}, bf16[256,128]{1,0:T(8,128)(2,1)S(1)}, u32[]{:S(2)}, u32[]{:S(2)}) collective-permute-start(bf16[256,128]{1,0:T(8,128)(2,1)} %get-tuple-element.30), channel_id=1, source_target_pairs={{0,32},{32,64},{64,96},{96,0},{1,33},{33,65},{65,97},{97,1},{2,34}... | collective-permute-start | bytes 196616 | tf_op jit(solution)/shard_map/ppermute | solution.py:292
  48.9 2.8 %collective-permute-start.10 = (bf16[256,128]{1,0:T(8,128)(2,1)}, bf16[256,128]{1,0:T(8,128)(2,1)S(1)}, u32[]{:S(2)}, u32[]{:S(2)}) collective-permute-start(bf16[256,128]{1,0:T(8,128)(2,1)} %get-tuple-element.31), channel_id=1, source_target_pairs={{0,64},{32,96},{64,0},{96,32},{1,65},{33,97},{65,1},{97,33},{2,66}... | collective-permute-start | bytes 196616 | tf_op jit(solution)/shard_map/ppermute | solution.py:292
  51.7 0.8 %collective-permute-start.11 = (bf16[256,128]{1,0:T(8,128)(2,1)}, bf16[256,128]{1,0:T(8,128)(2,1)S(1)}, u32[]{:S(2)}, u32[]{:S(2)}) collective-permute-start(bf16[256,128]{1,0:T(8,128)(2,1)} %get-tuple-element.32), channel_id=1, source_target_pairs={{0,96},{32,0},{64,32},{96,64},{1,97},{33,1},{65,33},{97,65},{2,98}... | collective-permute-start | bytes 196616 | tf_op jit(solution)/shard_map/ppermute | solution.py:292
  52.5 0.9 %collective-permute-done.9.g1 = bf16[256,128]{1,0:T(8,128)(2,1)S(1)} collective-permute-done((bf16[256,128]{1,0:T(8,128)(2,1)}, bf16[256,128]{1,0:T(8,128)(2,1)S(1)}, u32[]{:S(2)}, u32[]{:S(2)}) %collective-permute-start.9) | collective-permute-done | bytes 65568 | tf_op jit(solution)/shard_map/ppermute | solution.py:292
  53.4 2.2 %collective-permute-done.10.g2 = bf16[256,128]{1,0:T(8,128)(2,1)S(1)} collective-permute-done((bf16[256,128]{1,0:T(8,128)(2,1)}, bf16[256,128]{1,0:T(8,128)(2,1)S(1)}, u32[]{:S(2)}, u32[]{:S(2)}) %collective-permute-start.10) | collective-permute-done | bytes 65568 | tf_op jit(solution)/shard_map/ppermute | solution.py:292
  55.6 0.5 collective-permute-done.11.g3
  56.2 0.1 copy-done.10
  56.3 0.5 copy-done.11
  56.8 1.8 %assemble.1 = f32[1,1024,128]{2,1,0:T(8,128)} custom-call(f32[256,128]{1,0:T(8,128)} %get-tuple-element.29.own, bf16[256,128]{1,0:T(8,128)(2,1)} %copy-done.9, bf16[256,128]{1,0:T(8,128)(2,1)} %copy-done.10, bf16[256,128]{1,0:T(8,128)(2,1)} %copy-done.11), custom_call_target="tpu_custom_call" | custom-call | tf_op jit(solution)/shard_map/assemble/pallas_call | solution.py:282
  (21 shorter events, 0.0 us)
Async XLA Ops:
  0.0 33.3 %copy-start.7 = (f32[4]{0:T(128)S(1)}, f32[4]{0:T(128)}, u32[]{:S(2)}) copy-start(f32[4]{0:T(128)} %omegas.1) | copy-start | bytes 52
  18.8 14.5 %collective-permute-start = (bf16[2,2,256,128]{3,2,1,0:T(8,128)(2,1)}, bf16[2,2,256,128]{3,2,1,0:T(8,128)(2,1)S(1)}, u32[]{:S(2)}, u32[]{:S(2)}) collective-permute-start(bf16[2,2,256,128]{3,2,1,0:T(8,128)(2,1)} %get-tuple-element.22), channel_id=1, source_target_pairs={{0,1},{1,0},{2,3},{3,2},{4,5},{5,4},{6,7},{7,6},{8,9},{9,8},{10,11... | collective-permute-start | bytes 786440 | tf_op jit(solution)/shard_map/ppermute | solution.py:297
  18.9 6.1 %collective-permute-start.1 = (s16[272,128]{1,0:T(8,128)(2,1)}, s16[272,128]{1,0:T(8,128)(2,1)S(1)}, u32[]{:S(2)}, u32[]{:S(2)}) collective-permute-start(s16[272,128]{1,0:T(8,128)(2,1)} %get-tuple-element.24), channel_id=1, source_target_pairs={{0,32},{32,64},{64,96},{96,0},{1,33},{33,65},{65,97},{97,1},{2,34}... | collective-permute-start | bytes 208904 | tf_op jit(solution)/shard_map/ppermute | solution.py:292
  20.7 7.1 %collective-permute-start.2 = (s16[272,128]{1,0:T(8,128)(2,1)}, s16[272,128]{1,0:T(8,128)(2,1)S(1)}, u32[]{:S(2)}, u32[]{:S(2)}) collective-permute-start(s16[272,128]{1,0:T(8,128)(2,1)} %get-tuple-element.25), channel_id=1, source_target_pairs={{0,64},{32,96},{64,0},{96,32},{1,65},{33,97},{65,1},{97,33},{2,66}... | collective-permute-start | bytes 208904 | tf_op jit(solution)/shard_map/ppermute | solution.py:292
  23.6 4.5 %collective-permute-start.3 = (s16[272,128]{1,0:T(8,128)(2,1)}, s16[272,128]{1,0:T(8,128)(2,1)S(1)}, u32[]{:S(2)}, u32[]{:S(2)}) collective-permute-start(s16[272,128]{1,0:T(8,128)(2,1)} %get-tuple-element.26), channel_id=1, source_target_pairs={{0,96},{32,0},{64,32},{96,64},{1,97},{33,1},{65,33},{97,65},{2,98}... | collective-permute-start | bytes 208904 | tf_op jit(solution)/shard_map/ppermute | solution.py:292
  24.9 8.4 %collective-permute-start.4 = (s16[272,128]{1,0:T(8,128)(2,1)}, s16[272,128]{1,0:T(8,128)(2,1)S(1)}, u32[]{:S(2)}, u32[]{:S(2)}) collective-permute-start(s16[272,128]{1,0:T(8,128)(2,1)} %get-tuple-element.23.q0), channel_id=1, source_target_pairs={{0,1},{1,0},{2,3},{3,2},{4,5},{5,4},{6,7},{7,6},{8,9},{9,8},{10,11... | collective-permute-start | bytes 208904 | tf_op jit(solution)/shard_map/ppermute | solution.py:297
  25.1 8.2 %collective-permute-start.5 = (s16[272,128]{1,0:T(8,128)(2,1)S(1)}, s16[272,128]{1,0:T(8,128)(2,1)S(1)}, u32[]{:S(2)}, u32[]{:S(2)}) collective-permute-start(s16[272,128]{1,0:T(8,128)(2,1)S(1)} %collective-permute-done.1.q1), channel_id=1, source_target_pairs={{0,1},{1,0},{2,3},{3,2},{4,5},{5,4},{6,7},{7,6},{8,9},{9,8},{10,11... | collective-permute-start | bytes 208904 | tf_op jit(solution)/shard_map/ppermute | solution.py:297
  27.8 5.5 %collective-permute-start.6 = (s16[272,128]{1,0:T(8,128)(2,1)S(1)}, s16[272,128]{1,0:T(8,128)(2,1)S(1)}, u32[]{:S(2)}, u32[]{:S(2)}) collective-permute-start(s16[272,128]{1,0:T(8,128)(2,1)S(1)} %collective-permute-done.2.q2), channel_id=1, source_target_pairs={{0,1},{1,0},{2,3},{3,2},{4,5},{5,4},{6,7},{7,6},{8,9},{9,8},{10,11... | collective-permute-start | bytes 208904 | tf_op jit(solution)/shard_map/ppermute | solution.py:297
  28.1 5.2 %collective-permute-start.7 = (s16[272,128]{1,0:T(8,128)(2,1)S(1)}, s16[272,128]{1,0:T(8,128)(2,1)S(1)}, u32[]{:S(2)}, u32[]{:S(2)}) collective-permute-start(s16[272,128]{1,0:T(8,128)(2,1)S(1)} %collective-permute-done.3.q3), channel_id=1, source_target_pairs={{0,1},{1,0},{2,3},{3,2},{4,5},{5,4},{6,7},{7,6},{8,9},{9,8},{10,11... | collective-permute-start | bytes 208904 | tf_op jit(solution)/shard_map/ppermute | solution.py:297
  28.3 2.2 %copy-start = (bf16[4,4,2,256,256]{4,3,2,1,0:T(8,128)(2,1)S(1)}, bf16[4,4,2,256,256]{4,3,2,1,0:T(8,128)(2,1)}, u32[]{:S(2)}) copy-start(bf16[4,4,2,256,256]{4,3,2,1,0:T(8,128)(2,1)} %inverses.1) | copy-start | bytes 12582916
  30.5 0.7 %copy-start.2 = (bf16[4,2,256]{2,1,0:T(2,128)(2,1)S(1)}, bf16[4,2,256]{2,1,0:T(2,128)(2,1)}, u32[]{:S(2)}) copy-start(bf16[4,2,256]{2,1,0:T(2,128)(2,1)} %amp.1) | copy-start | bytes 12292
  31.1 0.7 %copy-start.3 = (s32[256]{0:T(256)S(1)}, s32[256]{0:T(256)}, u32[]{:S(2)}) copy-start(s32[256]{0:T(256)} %param.11) | copy-start | bytes 3076
  31.8 0.7 %copy-start.4 = (s32[256]{0:T(256)S(1)}, s32[256]{0:T(256)}, u32[]{:S(2)}) copy-start(s32[256]{0:T(256)} %param.12) | copy-start | bytes 3076
  32.5 0.9 %copy-start.5 = (bf16[2,2,256,128]{3,2,1,0:T(8,128)(2,1)S(1)}, bf16[2,2,256,128]{3,2,1,0:T(8,128)(2,1)}, u32[]{:S(2)}) copy-start(bf16[2,2,256,128]{3,2,1,0:T(8,128)(2,1)} %get-tuple-element.21.rec_mine) | copy-start | bytes 786436
  32.5 1.0 %copy-start.6 = (s16[272,128]{1,0:T(8,128)(2,1)S(1)}, s16[272,128]{1,0:T(8,128)(2,1)}, u32[]{:S(2)}) copy-start(s16[272,128]{1,0:T(8,128)(2,1)} %get-tuple-element.23.q0) | copy-start | bytes 208900
  42.8 0.8 %copy-start.1 = (f32[4,256,128]{2,1,0:T(8,128)}, f32[4,256,128]{2,1,0:T(8,128)S(1)}, u32[]{:S(2)}) copy-start(f32[4,256,128]{2,1,0:T(8,128)S(1)} %get-tuple-element.27.mine) | copy-start | bytes 1572868
  43.6 1.5 %collective-permute-start.8 = (bf16[4,256,128]{2,1,0:T(8,128)(2,1)S(1)}, bf16[4,256,128]{2,1,0:T(8,128)(2,1)S(1)}, u32[]{:S(2)}, u32[]{:S(2)}) collective-permute-start(bf16[4,256,128]{2,1,0:T(8,128)(2,1)S(1)} %get-tuple-element.28), channel_id=1, source_target_pairs={{0,1},{1,0},{2,3},{3,2},{4,5},{5,4},{6,7},{7,6},{8,9},{9,8},{10,11... | collective-permute-start | bytes 786440 | tf_op jit(solution)/shard_map/ppermute | solution.py:297
  45.1 0.7 %copy-start.8 = (bf16[4,256,128]{2,1,0:T(8,128)(2,1)}, bf16[4,256,128]{2,1,0:T(8,128)(2,1)S(1)}, u32[]{:S(2)}) copy-start(bf16[4,256,128]{2,1,0:T(8,128)(2,1)S(1)} %collective-permute-done.8.got) | copy-start | bytes 786436
  47.7 5.7 %collective-permute-start.9 = (bf16[256,128]{1,0:T(8,128)(2,1)}, bf16[256,128]{1,0:T(8,128)(2,1)S(1)}, u32[]{:S(2)}, u32[]{:S(2)}) collective-permute-start(bf16[256,128]{1,0:T(8,128)(2,1)} %get-tuple-element.30), channel_id=1, source_target_pairs={{0,32},{32,64},{64,96},{96,0},{1,33},{33,65},{65,97},{97,1},{2,34}... | collective-permute-start | bytes 196616 | tf_op jit(solution)/shard_map/ppermute | solution.py:292
  48.9 6.7 %collective-permute-start.10 = (bf16[256,128]{1,0:T(8,128)(2,1)}, bf16[256,128]{1,0:T(8,128)(2,1)S(1)}, u32[]{:S(2)}, u32[]{:S(2)}) collective-permute-start(bf16[256,128]{1,0:T(8,128)(2,1)} %get-tuple-element.31), channel_id=1, source_target_pairs={{0,64},{32,96},{64,0},{96,32},{1,65},{33,97},{65,1},{97,33},{2,66}... | collective-permute-start | bytes 196616 | tf_op jit(solution)/shard_map/ppermute | solution.py:292
  51.7 4.5 %collective-permute-start.11 = (bf16[256,128]{1,0:T(8,128)(2,1)}, bf16[256,128]{1,0:T(8,128)(2,1)S(1)}, u32[]{:S(2)}, u32[]{:S(2)}) collective-permute-start(bf16[256,128]{1,0:T(8,128)(2,1)} %get-tuple-element.32), channel_id=1, source_target_pairs={{0,96},{32,0},{64,32},{96,64},{1,97},{33,1},{65,33},{97,65},{2,98}... | collective-permute-start | bytes 196616 | tf_op jit(solution)/shard_map/ppermute | solution.py:292
  53.4 2.7 %copy-start.9 = (bf16[256,128]{1,0:T(8,128)(2,1)}, bf16[256,128]{1,0:T(8,128)(2,1)S(1)}, u32[]{:S(2)}) copy-start(bf16[256,128]{1,0:T(8,128)(2,1)S(1)} %collective-permute-done.9.g1) | copy-start | bytes 196612
  55.6 0.6 %copy-start.10 = (bf16[256,128]{1,0:T(8,128)(2,1)}, bf16[256,128]{1,0:T(8,128)(2,1)S(1)}, u32[]{:S(2)}) copy-start(bf16[256,128]{1,0:T(8,128)(2,1)S(1)} %collective-permute-done.10.g2) | copy-start | bytes 196612
  56.2 0.6 %copy-start.11 = (bf16[256,128]{1,0:T(8,128)(2,1)}, bf16[256,128]{1,0:T(8,128)(2,1)S(1)}, u32[]{:S(2)}) copy-start(bf16[256,128]{1,0:T(8,128)(2,1)S(1)} %collective-permute-done.11.g3) | copy-start | bytes 196612

commit v2 on v1

--- a/solution.py
+++ b/solution.py
@@ -41,51 +41,50 @@
     return lax.axis_index("depth"), line // 2, lax.rem(line, 2)
 
 
-def pack_kernel(slow, zones_x, zones_y, receiver, q0, q1, q2, q3, rec_own, rec_send, sems):
+def pack_kernel(
+    slow, zones_x, zones_y, receiver, amp_hbm, source_x_hbm, source_y_hbm,
+    q0, q1, q2, q3, rec_mine, rec_send, sources,
+    level_slow, packed, rec, amp, source_x, source_y, spread, fields, in_sems, out_sems,
+):
     section, pair, core = place()
-    rows = pl.ds(section * B, B)
-    copies = [
-        pltpu.make_async_copy(
-            receiver.at[pl.ds(which * MINE, MINE), :, rows, :], out, sems.at[k]
-        )
-        for k, (which, out) in enumerate(((1 - core, rec_send), (core, rec_own)))
-    ]
-    for copy in copies:
+    order = ((1, q1), (2, q2), (3, q3), (0, q0))
+    rows = pl.ds(pl.multiple_of(section * B, B), B)
+    arrivals = []
+    for shift, _ in order:
+        to = lax.rem(section + shift, SECTIONS)
+        start = pl.ds(pl.multiple_of(to * B, B), B)
+        arrivals.append((slow.at[0, start, :], level_slow.at[shift]))
+    arrivals += [(amp_hbm, amp), (source_x_hbm, source_x), (source_y_hbm, source_y)]
+    for k in range(2):
+        freqs = pl.ds(lax.rem(core + k, 2) * MINE, MINE)
+        arrivals.append((receiver.at[freqs, :, rows, :], rec.at[k]))
+    arrivals = [pltpu.make_async_copy(*ends, in_sems.at[k]) for k, ends in enumerate(arrivals)]
+    for copy in arrivals:
         copy.start()
+
+    departures = []
+
+    def send(source, target):
+        copy = pltpu.make_async_copy(source, target, out_sems.at[len(departures)])
+        copy.start()
+        departures.append(copy)
+
     zone_y = zones_y[0, pair]
     upper = lax.broadcasted_iota(I32, (EXTRA, H), 0) < EXTRA // 2
-    for shift, q in enumerate((q0, q1, q2, q3)):
+    for (shift, q), copy in zip(order, arrivals):
         to = lax.rem(section + shift, SECTIONS)
-        start = pl.multiple_of(to * B, B)
+        packed[shift, B:, :] = jnp.where(upper, zones_x[0, to], zone_y).astype(I16)
+        copy.wait()
         for r in range(0, B, 32):
-            value = slow[0, pl.ds(start + r, 32), :]
-            level = jnp.clip((value - MIDDLE) * STEPS, -32767.0, 32767.0)
-            q[r : r + 32, :] = jnp.round(level).astype(I32).astype(I16)
-        q[B:, :] = jnp.where(upper, zones_x[0, to], zone_y).astype(I16)
-    for copy in copies:
+            level = (level_slow[shift, r : r + 32, :] - MIDDLE) * STEPS
+            level = jnp.clip(level, -32767.0, 32767.0)
+            packed[shift, r : r + 32, :] = jnp.round(level).astype(I32).astype(I16)
+        send(packed.at[shift], q)
+    for copy in arrivals[SECTIONS:]:
         copy.wait()
-
-
-def pack(slowness, zones_x, zones_y, receiver):
-    block = jax.ShapeDtypeStruct((B + EXTRA, H), I16)
-    part = jax.ShapeDtypeStruct((MINE, 2, B, H), BF16)
-    vmem = pl.BlockSpec(memory_space=pltpu.VMEM)
-    smem = pl.BlockSpec(memory_space=pltpu.SMEM)
-    hbm = pl.BlockSpec(memory_space=pl.ANY)
-    return pl.pallas_call(
-        pack_kernel,
-        out_shape=[block] * 4 + [part] * 2,
-        in_specs=[vmem, smem, smem, hbm],
-        out_specs=[vmem] * 4 + [hbm] * 2,
-        scratch_shapes=[pltpu.SemaphoreType.DMA((2,))],
-        name="pack",
-    )(slowness, zones_x, zones_y, receiver)
-
-
-def prepare_kernel(amp, source_x, source_y, inverses, sources, operators, table, spread, sem):
-    section, pair, core = place()
-    copy = pltpu.make_async_copy(inverses.at[pl.ds(core * MINE, MINE)], table, sem)
-    copy.start()
+    send(rec.at[1], rec_send)
+    send(rec.at[0], rec_mine)
+
     count = source_x.shape[1]
     cells = lax.broadcasted_iota(I32, (B, count), 0)
     hot_x = jnp.where(cells + section * B == source_x[...], 1.0, 0.0).astype(BF16)
@@ -94,11 +93,51 @@
         for part in range(2):
             row = amp[pl.ds(core * MINE + f, 1), part, :].astype(F32)
             spread[part * B : (part + 1) * B, :] = jnp.where(hot_y, row, 0.0).astype(BF16)
-        sources[f] = lax.dot_general(
+        fields[f] = lax.dot_general(
             hot_x, spread[...], (((1,), (1,)), ((), ())), preferred_element_type=F32
         ).astype(BF16)
-    copy.wait()
+    send(fields, sources)
+    for copy in departures:
+        copy.wait()
+
+
+def pack(slowness, zones_x, zones_y, receiver, amp, source_x, source_y):
+    block = jax.ShapeDtypeStruct((B + EXTRA, H), I16)
+    part = jax.ShapeDtypeStruct((MINE, 2, B, H), BF16)
+    field = jax.ShapeDtypeStruct((MINE, B, 2 * B), BF16)
+    smem = pl.BlockSpec(memory_space=pltpu.SMEM)
+    hbm = pl.BlockSpec(memory_space=pl.ANY)
+    return pl.pallas_call(
+        pack_kernel,
+        out_shape=[block] * 4 + [part] * 2 + [field],
+        in_specs=[hbm, smem, smem] + [hbm] * 4,
+        out_specs=[hbm] * 7,
+        scratch_shapes=[
+            pltpu.VMEM((SECTIONS, B, H), F32),
+            pltpu.VMEM((SECTIONS, B + EXTRA, H), I16),
+            pltpu.VMEM((2, MINE, 2, B, H), BF16),
+            pltpu.VMEM(amp.shape, BF16),
+            pltpu.VMEM(source_x.shape, I32),
+            pltpu.VMEM(source_y.shape, I32),
+            pltpu.VMEM((2 * B, source_x.shape[1]), BF16),
+            pltpu.VMEM((MINE, B, 2 * B), BF16),
+            pltpu.SemaphoreType.DMA((9,)),
+            pltpu.SemaphoreType.DMA((7,)),
+        ],
+        name="pack",
+    )(slowness, zones_x, zones_y, receiver, amp, source_x, source_y)
+
+
+def prepare_kernel(inverses, operators, table, sems):
+    core = place()[2]
+    copies = [
+        pltpu.make_async_copy(inverses.at[core * MINE + f], table.at[f], sems.at[f])
+        for f in range(MINE)
+    ]
+    for copy in copies:
+        copy.start()
     for f in range(MINE):
+        copies[f].wait()
         for zone in range(table.shape[1]):
             real = table[f, zone, 0]
             imag = table[f, zone, 1]
@@ -108,29 +147,21 @@
             operators[f, zone, :B, B:] = -imag
 
 
-def prepare(amp, source_x, source_y, inverses):
+def prepare(inverses):
     zones = inverses.shape[1]
-    vmem = pl.BlockSpec(memory_space=pltpu.VMEM)
-    hbm = pl.BlockSpec(memory_space=pl.ANY)
     return pl.pallas_call(
         prepare_kernel,
-        out_shape=[
-            jax.ShapeDtypeStruct((MINE, B, 2 * B), BF16),
-            jax.ShapeDtypeStruct((MINE, zones, 2 * B, 2 * B), BF16),
-        ],
-        in_specs=[vmem, vmem, vmem, hbm],
-        out_specs=[vmem, vmem],
+        out_shape=jax.ShapeDtypeStruct((MINE, zones, 2 * B, 2 * B), BF16),
+        in_specs=[pl.BlockSpec(memory_space=pltpu.HBM)],
+        out_specs=pl.BlockSpec(memory_space=pltpu.VMEM),
         scratch_shapes=[
             pltpu.VMEM((MINE, zones, 2, B, B), BF16),
-            pltpu.VMEM((2 * B, source_x.shape[1]), BF16),
-            pltpu.SemaphoreType.DMA,
+            pltpu.SemaphoreType.DMA((MINE,)),
         ],
-        compiler_params=pltpu.CompilerParams(vmem_limit_bytes=24 * MB),
-        cost_estimate=pl.CostEstimate(
-            flops=4 * B**3 * 4, bytes_accessed=8 * MB, transcendentals=0
-        ),
+        compiler_params=pltpu.CompilerParams(vmem_limit_bytes=48 * MB),
+        cost_estimate=pl.CostEstimate(flops=0, bytes_accessed=6 * MB, transcendentals=0),
         name="prepare",
-    )(amp, source_x, source_y, inverses)
+    )(inverses)
 
 
 def continue_kernel(
@@ -266,6 +297,7 @@
         + [jax.ShapeDtypeStruct((B, H), BF16)] * 3,
         in_specs=[vmem, vmem],
         out_specs=[vmem] * 4,
+        compiler_params=pltpu.CompilerParams(vmem_limit_bytes=8 * MB),
         name="merge",
     )(mine, got)
 
@@ -284,6 +316,7 @@
         out_shape=jax.ShapeDtypeStruct((1, SECTIONS * B, H), F32),
         in_specs=[vmem] * 4,
         out_specs=vmem,
+        compiler_params=pltpu.CompilerParams(vmem_limit_bytes=8 * MB),
         name="assemble",
     )(own, *blocks)
 
@@ -300,13 +333,23 @@
 def per_device(
     receiver_data, source_amp, source_x, source_y, omegas, slowness, inverses, zones_x, zones_y
 ):
-    *blocks, rec_mine, rec_send = pack(slowness, zones_x, zones_y, receiver_data)
-    mine = [blocks[0]] + [along_depth(blocks[k], k) for k in (1, 2, 3)]
+    *blocks, rec_mine, rec_send, sources = pack(
+        slowness,
+        zones_x,
+        zones_y,
+        receiver_data,
+        source_amp,
+        source_x.reshape(1, -1),
+        source_y.reshape(1, -1),
+    )
+    moved = [along_depth(blocks[k], k) for k in (1, 2, 3)]
+    operators = prepare(inverses)
+    operators, rec_send, own, *moved = lax.optimization_barrier(
+        (operators, rec_send, blocks[0], *moved)
+    )
+    mine = [own, *moved]
+    rec_other = other_core(rec_send)
     other = [other_core(block) for block in mine]
-    rec_other = other_core(rec_send)
-    sources, operators = prepare(
-        source_amp, source_x.reshape(1, -1), source_y.reshape(1, -1), inverses
-    )
     grad_mine, grad_other = continue_all(
         omegas, sources, operators, rec_mine, rec_other, mine, other
     )

time: 58.9 us -> 35.2 us (0.60)
  Pallas kernels: 32.6 us -> 15.2 us
  local copies, waits for them, and re-layouts: 6.47 us -> 0.02 us
    pallas_call x2, Pallas kernels: 19.6 us -> 4.99 us  [the longest x1 3.3 us: pack(): pl.pallas_call(pack_kernel, out_shape=[block] * 4 + [part] * 2 + [field],...]
    unnamed x24 -> x10, local copies, waits for them, and re-layouts: 6.47 us -> 0.02 us
    pallas_call x1, Pallas kernels: 1.88 us -> 0.06 us  [merge(): pl.pallas_call(merge_kernel, out_shape=[jax.ShapeDtypeStruct((B, H), F32)...]
    ppermute x6, waiting for transfers between devices: 1.24 us -> 2.56 us  [other_core(): return lax.ppermute(block, 'xline', [(i, i ^ 1) for i in range(count)])]
    pallas_call x1, Pallas kernels: 1.8 us -> 0.84 us  [assemble(): pl.pallas_call(assemble_kernel, out_shape=jax.ShapeDtypeStruct((1, SECTIO...]
    ppermute x6, waiting for transfers between devices: 6.46 us -> 5.6 us  [along_depth(): lax.ppermute(block, 'depth', [(i, (i + shift) % SECTIONS) for i in range(...]
  transfers between devices with their start and end apart: 12 -> 12, of which waited for: 7 -> 10; matrix products, arithmetic and copies ran while one was open for 0% -> 0% of each run, Pallas kernels for 1% -> 5%
where the time goes in v2:
time: 35.2 us; the launch traced here: 35.1 us
  Pallas kernels  15.2 us (43%)
  starting transfers between devices  11.6 us (33%)
  waiting for transfers between devices  8.16 us (23%)
    ppermute x6, starting transfers between devices, along_depth(): lax.ppermute(block, 'depth', [(i, (i + shift) % SECTIONS) for i in range(...  10.3 us
    pallas_call x1, Pallas kernels, continue_all(): pl.pallas_call(continue_kernel, out_shape=[jax.ShapeDtypeStruct((LEVELS,...  9.33 us
    ppermute x6, waiting for transfers between devices, along_depth(): lax.ppermute(block, 'depth', [(i, (i + shift) % SECTIONS) for i in range(...  5.6 us
    pallas_call x1, Pallas kernels, pack(): pl.pallas_call(pack_kernel, out_shape=[block] * 4 + [part] * 2 + [field],...  3.3 us
    ppermute x6, waiting for transfers between devices, other_core(): return lax.ppermute(block, 'xline', [(i, i ^ 1) for i in range(count)])  2.56 us
    pallas_call x1, Pallas kernels, prepare(): pl.pallas_call(prepare_kernel, out_shape=jax.ShapeDtypeStruct((MINE, zone...  1.69 us
    ppermute x6, starting transfers between devices, other_core(): return lax.ppermute(block, 'xline', [(i, i ^ 1) for i in range(count)])  1.33 us
    pallas_call x1, Pallas kernels, assemble(): pl.pallas_call(assemble_kernel, out_shape=jax.ShapeDtypeStruct((1, SECTIO...  0.84 us
  transfers between devices with their start and end apart: 12, of which 10 were waited for; matrix products, arithmetic and copies ran while one was open for 0% of the time, Pallas kernels for 5%

profile of v2, /device:TPU:0, one launch (start us, length us, event | category | flops | bytes accessed | tf_op | source)
XLA Modules:
  0.0 35.1 jit_solution(4417549225501179351)
XLA Ops:
  0.0 3.3 %pack.1 = (s16[272,128]{1,0:T(8,128)(2,1)}, s16[272,128]{1,0:T(8,128)(2,1)}, s16[272,128]{1,0:T(8,128)(2,1)}, s16[272,128]{1,0:T(8,128)(2,1)}, bf16[2,2,256,128]...) custom-call(f32[1,1024,128]{2,1,0:T(8,128)} %slow.1, s32[1,4]{1,0:T(1,128)} %zones_x.1, ...), custom_call_target="tpu_custom_call" | custom-call | tf_op jit(solution)/shard_map/pack/pallas_call | solution.py:110
  3.3 1.7 %collective-permute-start = (s16[272,128]{1,0:T(8,128)(2,1)}, s16[272,128]{1,0:T(8,128)(2,1)S(1)}, u32[]{:S(2)}, u32[]{:S(2)}) collective-permute-start(s16[272,128]{1,0:T(8,128)(2,1)} %get-tuple-element.27), channel_id=1, source_target_pairs={{0,32},{32,64},{64,96},{96,0},{1,33},{33,65},{65,97},{97,1},{2,34}... | collective-permute-start | bytes 208904 | tf_op jit(solution)/shard_map/ppermute | solution.py:325
  5.0 2.9 %collective-permute-start.1 = (s16[272,128]{1,0:T(8,128)(2,1)}, s16[272,128]{1,0:T(8,128)(2,1)S(1)}, u32[]{:S(2)}, u32[]{:S(2)}) collective-permute-start(s16[272,128]{1,0:T(8,128)(2,1)} %get-tuple-element.28), channel_id=1, source_target_pairs={{0,64},{32,96},{64,0},{96,32},{1,65},{33,97},{65,1},{97,33},{2,66}... | collective-permute-start | bytes 208904 | tf_op jit(solution)/shard_map/ppermute | solution.py:325
  8.0 0.0 copy-start.3
  8.0 1.4 %collective-permute-start.2 = (s16[272,128]{1,0:T(8,128)(2,1)}, s16[272,128]{1,0:T(8,128)(2,1)S(1)}, u32[]{:S(2)}, u32[]{:S(2)}) collective-permute-start(s16[272,128]{1,0:T(8,128)(2,1)} %get-tuple-element.29), channel_id=1, source_target_pairs={{0,96},{32,0},{64,32},{96,64},{1,97},{33,1},{65,33},{97,65},{2,98}... | collective-permute-start | bytes 208904 | tf_op jit(solution)/shard_map/ppermute | solution.py:325
  9.4 1.7 %prepare.1.operators = bf16[2,4,512,512]{3,2,1,0:T(8,128)(2,1)S(1)} custom-call(bf16[4,4,2,256,256]{4,3,2,1,0:T(8,128)(2,1)} %inverses.1), custom_call_target="tpu_custom_call" | custom-call | bytes 6291456 | tf_op jit(solution)/shard_map/prepare/pallas_call | solution.py:152
  11.1 0.0 collective-permute-done.q1
  11.1 0.4 %collective-permute-done.1.q2 = s16[272,128]{1,0:T(8,128)(2,1)S(1)} collective-permute-done((s16[272,128]{1,0:T(8,128)(2,1)}, s16[272,128]{1,0:T(8,128)(2,1)S(1)}, u32[]{:S(2)}, u32[]{:S(2)}) %collective-permute-start.1) | collective-permute-done | bytes 69664 | tf_op jit(solution)/shard_map/ppermute | solution.py:325
  11.5 1.0 %collective-permute-done.2.q3 = s16[272,128]{1,0:T(8,128)(2,1)S(1)} collective-permute-done((s16[272,128]{1,0:T(8,128)(2,1)}, s16[272,128]{1,0:T(8,128)(2,1)S(1)}, u32[]{:S(2)}, u32[]{:S(2)}) %collective-permute-start.2) | collective-permute-done | bytes 69664 | tf_op jit(solution)/shard_map/ppermute | solution.py:325
  12.6 0.0 copy-done.4
  12.6 0.0 collective-permute-start.3
  12.6 0.5 %collective-permute-start.4 = (s16[272,128]{1,0:T(8,128)(2,1)S(1)}, s16[272,128]{1,0:T(8,128)(2,1)S(1)}, u32[]{:S(2)}, u32[]{:S(2)}) collective-permute-start(s16[272,128]{1,0:T(8,128)(2,1)S(1)} %copy-done.2), channel_id=1, source_target_pairs={{0,1},{1,0},{2,3},{3,2},{4,5},{5,4},{6,7},{7,6},{8,9},{9,8},{10,11... | collective-permute-start | bytes 208904 | tf_op jit(solution)/shard_map/ppermute | solution.py:330
  13.1 0.1 collective-permute-start.5
  13.2 0.4 %collective-permute-start.6 = (s16[272,128]{1,0:T(8,128)(2,1)S(1)}, s16[272,128]{1,0:T(8,128)(2,1)S(1)}, u32[]{:S(2)}, u32[]{:S(2)}) collective-permute-start(s16[272,128]{1,0:T(8,128)(2,1)S(1)} %collective-permute-done.1.q2), channel_id=1, source_target_pairs={{0,1},{1,0},{2,3},{3,2},{4,5},{5,4},{6,7},{7,6},{8,9},{9,8},{10,11... | collective-permute-start | bytes 208904 | tf_op jit(solution)/shard_map/ppermute | solution.py:330
  13.6 0.1 collective-permute-start.7
  13.7 0.5 %collective-permute-done.4.p0 = s16[272,128]{1,0:T(8,128)(2,1)S(1)} collective-permute-done((s16[272,128]{1,0:T(8,128)(2,1)S(1)}, s16[272,128]{1,0:T(8,128)(2,1)S(1)}, u32[]{:S(2)}, u32[]{:S(2)}) %collective-permute-start.4) | collective-permute-done | bytes 69664 | tf_op jit(solution)/shard_map/ppermute | solution.py:330
  14.2 0.1 collective-permute-done.5.p1
  14.3 0.2 collective-permute-done.6.p2
  14.5 0.4 %collective-permute-done.7.p3 = s16[272,128]{1,0:T(8,128)(2,1)S(1)} collective-permute-done((s16[272,128]{1,0:T(8,128)(2,1)S(1)}, s16[272,128]{1,0:T(8,128)(2,1)S(1)}, u32[]{:S(2)}, u32[]{:S(2)}) %collective-permute-start.7) | collective-permute-done | bytes 69664 | tf_op jit(solution)/shard_map/ppermute | solution.py:330
  14.8 0.0 collective-permute-done.3.rec_other
  14.9 0.0 copy-done.3
  14.9 9.3 %continue_levels.1 = (f32[4,256,128]{2,1,0:T(8,128)S(1)}, bf16[4,256,128]{2,1,0:T(8,128)(2,1)S(1)}) custom-call(f32[4]{0:T(128)S(1)} %copy-done.3, bf16[2,256,512]{2,1,0:T(8,128)(2,1)S(1)} %copy-done, bf16[2,4,512,512]{3,2,1,0:T(8,128)(2,1)S(1)} %prepare.1.operators, bf16[2,2,256,128]{3,2,1,0:T(8,128)(2,1)S(1)} %copy-done.1, ...), custom_call_target="tpu_custom_call" | custom-call | flops 4294967296 | bytes 8388608 | tf_op jit(solution)/shard_map/continue_levels/pallas_call | solution.py:262
  24.2 0.2 collective-permute-start.8
  24.4 1.4 %collective-permute-done.8.got = bf16[4,256,128]{2,1,0:T(8,128)(2,1)S(1)} collective-permute-done((bf16[4,256,128]{2,1,0:T(8,128)(2,1)S(1)}, bf16[4,256,128]{2,1,0:T(8,128)(2,1)S(1)}, u32[]{:S(2)}, u32[]{:S(2)}) %collective-permute-start.8) | collective-permute-done | bytes 262176 | tf_op jit(solution)/shard_map/ppermute | solution.py:330
  25.8 0.1 merge.1
  25.9 0.4 %collective-permute-start.9 = (bf16[256,128]{1,0:T(8,128)(2,1)S(1)}, bf16[256,128]{1,0:T(8,128)(2,1)S(1)}, u32[]{:S(2)}, u32[]{:S(2)}) collective-permute-start(bf16[256,128]{1,0:T(8,128)(2,1)S(1)} %get-tuple-element.40), channel_id=1, source_target_pairs={{0,32},{32,64},{64,96},{96,0},{1,33},{33,65},{65,97},{97,1},{2,34}... | collective-permute-start | bytes 196616 | tf_op jit(solution)/shard_map/ppermute | solution.py:325
  26.3 3.7 %collective-permute-start.10 = (bf16[256,128]{1,0:T(8,128)(2,1)S(1)}, bf16[256,128]{1,0:T(8,128)(2,1)S(1)}, u32[]{:S(2)}, u32[]{:S(2)}) collective-permute-start(bf16[256,128]{1,0:T(8,128)(2,1)S(1)} %get-tuple-element.41), channel_id=1, source_target_pairs={{0,64},{32,96},{64,0},{96,32},{1,65},{33,97},{65,1},{97,33},{2,66}... | collective-permute-start | bytes 196616 | tf_op jit(solution)/shard_map/ppermute | solution.py:325
  30.0 0.1 collective-permute-start.11
  30.1 1.3 %collective-permute-done.9.g1 = bf16[256,128]{1,0:T(8,128)(2,1)S(1)} collective-permute-done((bf16[256,128]{1,0:T(8,128)(2,1)S(1)}, bf16[256,128]{1,0:T(8,128)(2,1)S(1)}, u32[]{:S(2)}, u32[]{:S(2)}) %collective-permute-start.9) | collective-permute-done | bytes 65568 | tf_op jit(solution)/shard_map/ppermute | solution.py:325
  31.4 2.1 %collective-permute-done.10.g2 = bf16[256,128]{1,0:T(8,128)(2,1)S(1)} collective-permute-done((bf16[256,128]{1,0:T(8,128)(2,1)S(1)}, bf16[256,128]{1,0:T(8,128)(2,1)S(1)}, u32[]{:S(2)}, u32[]{:S(2)}) %collective-permute-start.10) | collective-permute-done | bytes 65568 | tf_op jit(solution)/shard_map/ppermute | solution.py:325
  33.5 0.7 %collective-permute-done.11.g3 = bf16[256,128]{1,0:T(8,128)(2,1)S(1)} collective-permute-done((bf16[256,128]{1,0:T(8,128)(2,1)S(1)}, bf16[256,128]{1,0:T(8,128)(2,1)S(1)}, u32[]{:S(2)}, u32[]{:S(2)}) %collective-permute-start.11) | collective-permute-done | bytes 65568 | tf_op jit(solution)/shard_map/ppermute | solution.py:325
  34.2 0.8 %assemble.1 = f32[1,1024,128]{2,1,0:T(8,128)} custom-call(f32[256,128]{1,0:T(8,128)S(1)} %get-tuple-element.39.own, bf16[256,128]{1,0:T(8,128)(2,1)S(1)} %collective-permute-done.9.g1, bf16[256,128]{1,0:T(8,128)(2,1)S(1)} %collective-permute-done.10.g2, bf16[256,128]{1,0:T(8,128)(2,1)S(1)} %collective-permute-done.11.g3), custom_call_target="tpu_custom_call" | custom-call | tf_op jit(solution)/shard_map/assemble/pallas_call | solution.py:314
  (7 shorter events, 0.0 us)
Async XLA Ops:
  3.3 7.8 %collective-permute-start = (s16[272,128]{1,0:T(8,128)(2,1)}, s16[272,128]{1,0:T(8,128)(2,1)S(1)}, u32[]{:S(2)}, u32[]{:S(2)}) collective-permute-start(s16[272,128]{1,0:T(8,128)(2,1)} %get-tuple-element.27), channel_id=1, source_target_pairs={{0,32},{32,64},{64,96},{96,0},{1,33},{33,65},{65,97},{97,1},{2,34}... | collective-permute-start | bytes 208904 | tf_op jit(solution)/shard_map/ppermute | solution.py:325
  5.0 6.5 %collective-permute-start.1 = (s16[272,128]{1,0:T(8,128)(2,1)}, s16[272,128]{1,0:T(8,128)(2,1)S(1)}, u32[]{:S(2)}, u32[]{:S(2)}) collective-permute-start(s16[272,128]{1,0:T(8,128)(2,1)} %get-tuple-element.28), channel_id=1, source_target_pairs={{0,64},{32,96},{64,0},{96,32},{1,65},{33,97},{65,1},{97,33},{2,66}... | collective-permute-start | bytes 208904 | tf_op jit(solution)/shard_map/ppermute | solution.py:325
  7.9 4.6 %copy-start.4 = (bf16[2,2,256,128]{3,2,1,0:T(8,128)(2,1)S(1)}, bf16[2,2,256,128]{3,2,1,0:T(8,128)(2,1)}, u32[]{:S(2)}) copy-start(bf16[2,2,256,128]{3,2,1,0:T(8,128)(2,1)} %get-tuple-element.32) | copy-start | bytes 786436
  7.9 4.6 %copy-start.2 = (s16[272,128]{1,0:T(8,128)(2,1)S(1)}, s16[272,128]{1,0:T(8,128)(2,1)}, u32[]{:S(2)}) copy-start(s16[272,128]{1,0:T(8,128)(2,1)} %get-tuple-element.33.q0) | copy-start | bytes 208900
  7.9 6.9 %copy-start = (bf16[2,256,512]{2,1,0:T(8,128)(2,1)S(1)}, bf16[2,256,512]{2,1,0:T(8,128)(2,1)}, u32[]{:S(2)}) copy-start(bf16[2,256,512]{2,1,0:T(8,128)(2,1)} %get-tuple-element.24.sources) | copy-start | bytes 1572868
  7.9 6.9 %copy-start.1 = (bf16[2,2,256,128]{3,2,1,0:T(8,128)(2,1)S(1)}, bf16[2,2,256,128]{3,2,1,0:T(8,128)(2,1)}, u32[]{:S(2)}) copy-start(bf16[2,2,256,128]{3,2,1,0:T(8,128)(2,1)} %get-tuple-element.31.rec_mine) | copy-start | bytes 786436
  8.0 6.9 %copy-start.3 = (f32[4]{0:T(128)S(1)}, f32[4]{0:T(128)}, u32[]{:S(2)}) copy-start(f32[4]{0:T(128)} %omegas.1) | copy-start | bytes 52
  8.0 4.6 %collective-permute-start.2 = (s16[272,128]{1,0:T(8,128)(2,1)}, s16[272,128]{1,0:T(8,128)(2,1)S(1)}, u32[]{:S(2)}, u32[]{:S(2)}) collective-permute-start(s16[272,128]{1,0:T(8,128)(2,1)} %get-tuple-element.29), channel_id=1, source_target_pairs={{0,96},{32,0},{64,32},{96,64},{1,97},{33,1},{65,33},{97,65},{2,98}... | collective-permute-start | bytes 208904 | tf_op jit(solution)/shard_map/ppermute | solution.py:325
  12.6 2.3 %collective-permute-start.3 = (bf16[2,2,256,128]{3,2,1,0:T(8,128)(2,1)S(1)}, bf16[2,2,256,128]{3,2,1,0:T(8,128)(2,1)S(1)}, u32[]{:S(2)}, u32[]{:S(2)}) collective-permute-start(bf16[2,2,256,128]{3,2,1,0:T(8,128)(2,1)S(1)} %copy-done.4), channel_id=1, source_target_pairs={{0,1},{1,0},{2,3},{3,2},{4,5},{5,4},{6,7},{7,6},{8,9},{9,8},{10,11... | collective-permute-start | bytes 786440 | tf_op jit(solution)/shard_map/ppermute | solution.py:330
  12.6 1.6 %collective-permute-start.4 = (s16[272,128]{1,0:T(8,128)(2,1)S(1)}, s16[272,128]{1,0:T(8,128)(2,1)S(1)}, u32[]{:S(2)}, u32[]{:S(2)}) collective-permute-start(s16[272,128]{1,0:T(8,128)(2,1)S(1)} %copy-done.2), channel_id=1, source_target_pairs={{0,1},{1,0},{2,3},{3,2},{4,5},{5,4},{6,7},{7,6},{8,9},{9,8},{10,11... | collective-permute-start | bytes 208904 | tf_op jit(solution)/shard_map/ppermute | solution.py:330
  13.1 1.3 %collective-permute-start.5 = (s16[272,128]{1,0:T(8,128)(2,1)S(1)}, s16[272,128]{1,0:T(8,128)(2,1)S(1)}, u32[]{:S(2)}, u32[]{:S(2)}) collective-permute-start(s16[272,128]{1,0:T(8,128)(2,1)S(1)} %collective-permute-done.q1), channel_id=1, source_target_pairs={{0,1},{1,0},{2,3},{3,2},{4,5},{5,4},{6,7},{7,6},{8,9},{9,8},{10,11... | collective-permute-start | bytes 208904 | tf_op jit(solution)/shard_map/ppermute | solution.py:330
  13.2 1.3 %collective-permute-start.6 = (s16[272,128]{1,0:T(8,128)(2,1)S(1)}, s16[272,128]{1,0:T(8,128)(2,1)S(1)}, u32[]{:S(2)}, u32[]{:S(2)}) collective-permute-start(s16[272,128]{1,0:T(8,128)(2,1)S(1)} %collective-permute-done.1.q2), channel_id=1, source_target_pairs={{0,1},{1,0},{2,3},{3,2},{4,5},{5,4},{6,7},{7,6},{8,9},{9,8},{10,11... | collective-permute-start | bytes 208904 | tf_op jit(solution)/shard_map/ppermute | solution.py:330
  13.6 1.3 %collective-permute-start.7 = (s16[272,128]{1,0:T(8,128)(2,1)S(1)}, s16[272,128]{1,0:T(8,128)(2,1)S(1)}, u32[]{:S(2)}, u32[]{:S(2)}) collective-permute-start(s16[272,128]{1,0:T(8,128)(2,1)S(1)} %collective-permute-done.2.q3), channel_id=1, source_target_pairs={{0,1},{1,0},{2,3},{3,2},{4,5},{5,4},{6,7},{7,6},{8,9},{9,8},{10,11... | collective-permute-start | bytes 208904 | tf_op jit(solution)/shard_map/ppermute | solution.py:330
  24.2 1.6 %collective-permute-start.8 = (bf16[4,256,128]{2,1,0:T(8,128)(2,1)S(1)}, bf16[4,256,128]{2,1,0:T(8,128)(2,1)S(1)}, u32[]{:S(2)}, u32[]{:S(2)}) collective-permute-start(bf16[4,256,128]{2,1,0:T(8,128)(2,1)S(1)} %get-tuple-element.38), channel_id=1, source_target_pairs={{0,1},{1,0},{2,3},{3,2},{4,5},{5,4},{6,7},{7,6},{8,9},{9,8},{10,11... | collective-permute-start | bytes 786440 | tf_op jit(solution)/shard_map/ppermute | solution.py:330
  25.9 5.6 %collective-permute-start.9 = (bf16[256,128]{1,0:T(8,128)(2,1)S(1)}, bf16[256,128]{1,0:T(8,128)(2,1)S(1)}, u32[]{:S(2)}, u32[]{:S(2)}) collective-permute-start(bf16[256,128]{1,0:T(8,128)(2,1)S(1)} %get-tuple-element.40), channel_id=1, source_target_pairs={{0,32},{32,64},{64,96},{96,0},{1,33},{33,65},{65,97},{97,1},{2,34}... | collective-permute-start | bytes 196616 | tf_op jit(solution)/shard_map/ppermute | solution.py:325
  26.3 7.2 %collective-permute-start.10 = (bf16[256,128]{1,0:T(8,128)(2,1)S(1)}, bf16[256,128]{1,0:T(8,128)(2,1)S(1)}, u32[]{:S(2)}, u32[]{:S(2)}) collective-permute-start(bf16[256,128]{1,0:T(8,128)(2,1)S(1)} %get-tuple-element.41), channel_id=1, source_target_pairs={{0,64},{32,96},{64,0},{96,32},{1,65},{33,97},{65,1},{97,33},{2,66}... | collective-permute-start | bytes 196616 | tf_op jit(solution)/shard_map/ppermute | solution.py:325
  30.0 4.3 %collective-permute-start.11 = (bf16[256,128]{1,0:T(8,128)(2,1)S(1)}, bf16[256,128]{1,0:T(8,128)(2,1)S(1)}, u32[]{:S(2)}, u32[]{:S(2)}) collective-permute-start(bf16[256,128]{1,0:T(8,128)(2,1)S(1)} %get-tuple-element.42), channel_id=1, source_target_pairs={{0,96},{32,0},{64,32},{96,64},{1,97},{33,1},{65,33},{97,65},{2,98}... | collective-permute-start | bytes 196616 | tf_op jit(solution)/shard_map/ppermute | solution.py:325

commit v3 on v2

--- a/solution.py
+++ b/solution.py
@@ -18,7 +18,7 @@
 MINE = 2
 B = 256
 H = 128
-EXTRA = 16
+EBF16RA = 16
 
 MIDDLE = 1.1
 STEPS = 36000.0
@@ -51,7 +51,7 @@
     rows = pl.ds(pl.multiple_of(section * B, B), B)
     arrivals = []
     for shift, _ in order:
-        to = lax.rem(section + shift, SECTIONS)
+        to = lax.bitwise_xor(section, shift)
         start = pl.ds(pl.multiple_of(to * B, B), B)
         arrivals.append((slow.at[0, start, :], level_slow.at[shift]))
     arrivals += [(amp_hbm, amp), (source_x_hbm, source_x), (source_y_hbm, source_y)]
@@ -70,9 +70,9 @@
         departures.append(copy)
 
     zone_y = zones_y[0, pair]
-    upper = lax.broadcasted_iota(I32, (EXTRA, H), 0) < EXTRA // 2
+    upper = lax.broadcasted_iota(I32, (EBF16RA, H), 0) < EBF16RA // 2
     for (shift, q), copy in zip(order, arrivals):
-        to = lax.rem(section + shift, SECTIONS)
+        to = lax.bitwise_xor(section, shift)
         packed[shift, B:, :] = jnp.where(upper, zones_x[0, to], zone_y).astype(I16)
         copy.wait()
         for r in range(0, B, 32):
@@ -102,7 +102,7 @@
 
 
 def pack(slowness, zones_x, zones_y, receiver, amp, source_x, source_y):
-    block = jax.ShapeDtypeStruct((B + EXTRA, H), I16)
+    block = jax.ShapeDtypeStruct((B + EBF16RA, H), I16)
     part = jax.ShapeDtypeStruct((MINE, 2, B, H), BF16)
     field = jax.ShapeDtypeStruct((MINE, B, 2 * B), BF16)
     smem = pl.BlockSpec(memory_space=pltpu.SMEM)
@@ -114,7 +114,7 @@
         out_specs=[hbm] * 7,
         scratch_shapes=[
             pltpu.VMEM((SECTIONS, B, H), F32),
-            pltpu.VMEM((SECTIONS, B + EXTRA, H), I16),
+            pltpu.VMEM((SECTIONS, B + EBF16RA, H), I16),
             pltpu.VMEM((2, MINE, 2, B, H), BF16),
             pltpu.VMEM(amp.shape, BF16),
             pltpu.VMEM(source_x.shape, I32),
@@ -168,92 +168,97 @@
     omegas, sources, operators, rec_mine, rec_other,
     q0, q1, q2, q3, p0, p1, p2, p3,
     grad_mine, grad_other,
-    slow, zones, W, X, Y,
+    slow, zones, total, *waves,
 ):
     section, _, core = place()
+    W, X, Y = waves[:MINE], waves[MINE : 2 * MINE], waves[2 * MINE :]
     mine = pl.ds(pl.multiple_of(core * H, H), H)
     other = pl.ds(pl.multiple_of((1 - core) * H, H), H)
 
     for shift, (q, p) in enumerate(((q0, p0), (q1, p1), (q2, p2), (q3, p3))):
-        level = lax.rem(section + SECTIONS - shift, SECTIONS)
+        level = lax.bitwise_xor(section, shift)
         for r in range(0, B, 32):
             slow[level, r : r + 32, mine] = q[r : r + 32, :].astype(I32).astype(F32)
             slow[level, r : r + 32, other] = p[r : r + 32, :].astype(I32).astype(F32)
         marks = q[B:, :].astype(I32)
-        zones[level, 0] = jnp.max(marks[: EXTRA // 2])
-        zones[level, 1] = jnp.max(marks[EXTRA // 2 :])
+        zones[level, 0] = jnp.max(marks[: EBF16RA // 2])
+        zones[level, 1] = jnp.max(marks[EBF16RA // 2 :])
 
     for f in range(MINE):
-        W[f, :B, :] = sources[f]
+        W[f][:B, :] = sources[f]
         for columns, rec in ((mine, rec_mine), (other, rec_other)):
-            W[f, B:, columns] = rec[f, 0]
+            W[f][B:, columns] = rec[f, 0]
         imag_mine = pl.ds(pl.multiple_of(B + core * H, H), H)
         imag_other = pl.ds(pl.multiple_of(B + (1 - core) * H, H), H)
         for columns, rec in ((imag_mine, rec_mine), (imag_other, rec_other)):
-            W[f, B:, columns] = -rec[f, 1]
+            W[f][B:, columns] = -rec[f, 1]
+
+    CH = 32
+
+    def rotate(level, f):
+        omega = omegas[core * MINE + f]
+        scale = omega * (0.5 / math.pi / STEPS)
+        base = omega * (0.5 / math.pi * MIDDLE) - 0.5
+        for c in range(0, B, H):
+            for r in range(0, B, CH):
+                turn = slow[level, r : r + CH, c : c + H] * scale + base
+                square = turn * turn
+                half_sin = turn * horner(square, SIN)
+                half_cos = horner(square, COS)
+                cosine = half_sin * half_sin - 1.0
+                sine = -half_sin * half_cos
+                for wave in range(0, 2 * B, B):
+                    rows = slice(wave + r, wave + r + CH)
+                    columns = slice(wave + c, wave + c + H)
+                    real = W[f][rows, c : c + H].astype(F32)
+                    imag = W[f][rows, B + c : B + c + H].astype(F32)
+                    X[f][r : r + CH, columns] = (real * cosine - imag * sine).astype(BF16)
+                    X[f][B + r : B + r + CH, columns] = (real * sine + imag * cosine).astype(BF16)
+
+    def inline(level, f):
+        zone = zones[level, 0]
+        for wave in range(0, 2 * B, B):
+            update = jnp.dot(
+                operators[f, zone], X[f][:, wave : wave + B].astype(BF16), preferred_element_type=F32
+            )
+            for part in range(0, 2 * B, B):
+                Y[f][wave : wave + B, part : part + B] = (
+                    X[f][part : part + B, wave : wave + B].astype(F32) + update[part : part + B]
+                ).astype(BF16)
+
+    def crossline(level, f):
+        zone = zones[level, 1]
+        omega = omegas[core * MINE + f]
+        update = lax.dot_general(
+            Y[f][...], operators[f, zone], (((1,), (1,)), ((), ())), preferred_element_type=F32
+        )
+        for c in range(0, B, H):
+            for r in range(0, B, CH):
+                new = []
+                for part in range(0, 2 * B, B):
+                    for wave in range(0, 2 * B, B):
+                        rows = slice(wave + r, wave + r + CH)
+                        columns = slice(part + c, part + c + H)
+                        value = Y[f][rows, columns].astype(F32) + update[rows, columns]
+                        W[f][rows, columns] = value.astype(BF16)
+                        new.append(value)
+                term = (new[0] * new[1] - new[2] * new[3]) * (omega * omega)
+                if f > 0:
+                    term += total[c // H, level, r : r + CH, :]
+                total[c // H, level, r : r + CH, :] = term
 
     def one_level(level, carry):
-        zone_x = zones[level, 0]
-        zone_y = zones[level, 1]
         for f in range(MINE):
-            omega = omegas[core * MINE + f]
-            scale = omega * (0.5 / math.pi / STEPS)
-            base = omega * (0.5 / math.pi * MIDDLE) - 0.5
-            for c in range(0, B, H):
-                for r in range(0, B, 32):
-                    turn = slow[level, r : r + 32, c : c + H] * scale + base
-                    square = turn * turn
-                    half_sin = turn * horner(square, SIN)
-                    half_cos = horner(square, COS)
-                    cosine = half_sin * half_sin - 1.0
-                    sine = -half_sin * half_cos
-                    for wave in range(0, 2 * B, B):
-                        real = W[f, wave + r : wave + r + 32, c : c + H].astype(F32)
-                        imag = W[f, wave + r : wave + r + 32, B + c : B + c + H].astype(F32)
-                        X[f, r : r + 32, wave + c : wave + c + H] = (
-                            real * cosine - imag * sine
-                        ).astype(BF16)
-                        X[f, B + r : B + r + 32, wave + c : wave + c + H] = (
-                            real * sine + imag * cosine
-                        ).astype(BF16)
+            rotate(level, f)
         for f in range(MINE):
-            for wave in range(0, 2 * B, B):
-                update = jnp.dot(
-                    operators[f, zone_x], X[f, :, wave : wave + B], preferred_element_type=F32
-                )
-                for part in range(0, 2 * B, B):
-                    Y[f, wave : wave + B, part : part + B] = (
-                        X[f, part : part + B, wave : wave + B].astype(F32)
-                        + update[part : part + B]
-                    ).astype(BF16)
+            inline(level, f)
         for f in range(MINE):
-            for part in range(0, 2 * B, B):
-                update = lax.dot_general(
-                    Y[f],
-                    operators[f, zone_y, part : part + B, :],
-                    (((1,), (1,)), ((), ())),
-                    preferred_element_type=F32,
-                )
-                W[f, :, part : part + B] = (
-                    Y[f, :, part : part + B].astype(F32) + update
-                ).astype(BF16)
-        for out, offset in ((grad_mine, core * H), (grad_other, (1 - core) * H)):
-            real_at = pl.ds(pl.multiple_of(offset, H), H)
-            imag_at = pl.ds(pl.multiple_of(B + offset, H), H)
-            for r in range(0, B, 32):
-                total = None
-                for f in range(MINE):
-                    omega = omegas[core * MINE + f]
-                    down = slice(r, r + 32)
-                    up = slice(B + r, B + r + 32)
-                    term = W[f, down, real_at].astype(F32) * W[f, up, real_at].astype(F32)
-                    term -= W[f, down, imag_at].astype(F32) * W[f, up, imag_at].astype(F32)
-                    term *= omega * omega
-                    total = term if total is None else total + term
-                out[level, r : r + 32, :] = total.astype(out.dtype)
+            crossline(level, f)
         return carry
 
     lax.fori_loop(0, LEVELS, one_level, 0)
+    grad_mine[...] = total[core]
+    grad_other[...] = total[1 - core].astype(BF16)
 
 
 def continue_all(omegas, sources, operators, rec_mine, rec_other, mine, other):
@@ -270,9 +275,10 @@
         scratch_shapes=[
             pltpu.VMEM((LEVELS, B, B), F32),
             pltpu.SMEM((LEVELS, 2), I32),
-            pltpu.VMEM((MINE, 2 * B, 2 * B), BF16),
-            pltpu.VMEM((MINE, 2 * B, 2 * B), BF16),
-            pltpu.VMEM((MINE, 2 * B, 2 * B), BF16),
+            pltpu.VMEM((2, LEVELS, B, H), F32),
+            *[pltpu.VMEM((2 * B, 2 * B), BF16)] * MINE,
+            *[pltpu.VMEM((2 * B, 2 * B), BF16)] * MINE,
+            *[pltpu.VMEM((2 * B, 2 * B), BF16)] * MINE,
         ],
         compiler_params=pltpu.CompilerParams(vmem_limit_bytes=32 * MB),
         cost_estimate=pl.CostEstimate(
@@ -285,7 +291,7 @@
 def merge_kernel(mine, got, own, s1, s2, s3):
     section, _, _ = place()
     for shift, out in enumerate((own, s1, s2, s3)):
-        level = lax.rem(section + shift, SECTIONS)
+        level = lax.bitwise_xor(section, shift)
         out[...] = (mine[level] + got[level].astype(F32)).astype(out.dtype)
 
 
@@ -305,7 +311,7 @@
 def assemble_kernel(own, g1, g2, g3, out):
     section, _, _ = place()
     for shift, block in enumerate((own, g1, g2, g3)):
-        origin = lax.rem(section + SECTIONS - shift, SECTIONS)
+        origin = lax.bitwise_xor(section, shift)
         out[0, pl.ds(pl.multiple_of(origin * B, B), B), :] = block[...].astype(F32)
 
 
@@ -322,7 +328,7 @@
 
 
 def along_depth(block, shift):
-    return lax.ppermute(block, "depth", [(i, (i + shift) % SECTIONS) for i in range(SECTIONS)])
+    return lax.ppermute(block, "depth", [(i, i ^ shift) for i in range(SECTIONS)])
 
 
 def other_core(block):
@@ -343,13 +349,11 @@
         source_y.reshape(1, -1),
     )
     moved = [along_depth(blocks[k], k) for k in (1, 2, 3)]
-    operators = prepare(inverses)
-    operators, rec_send, own, *moved = lax.optimization_barrier(
-        (operators, rec_send, blocks[0], *moved)
-    )
-    mine = [own, *moved]
     rec_other = other_core(rec_send)
-    other = [other_core(block) for block in mine]
+    own_other = other_core(blocks[0])
+    operators, *moved = lax.optimization_barrier((prepare(inverses), *moved))
+    mine = [blocks[0], *moved]
+    other = [own_other] + [other_core(block) for block in moved]
     grad_mine, grad_other = continue_all(
         omegas, sources, operators, rec_mine, rec_other, mine, other
     )

time: 35.2 us -> 34.9 us (level)
  waiting for transfers between devices: 8.16 us -> 9.59 us
  starting transfers between devices: 11.6 us -> 10.5 us
  Pallas kernels: 15.2 us -> 14.5 us
    ppermute x6, waiting for transfers between devices: 5.6 us -> 6.94 us  [along_depth(): lax.ppermute(block, 'depth', [(i, i ^ shift) for i in range(SECTIONS)])]
    pallas_call x1, Pallas kernels: 9.33 us -> 8.58 us  [continue_all(): pl.pallas_call(continue_kernel, out_shape=[jax.ShapeDtypeStruct((LEVELS,...]
    ppermute x6, starting transfers between devices: 10.3 us -> 9.55 us  [along_depth(): lax.ppermute(block, 'depth', [(i, i ^ shift) for i in range(SECTIONS)])]
    ppermute x6, starting transfers between devices: 1.33 us -> 0.91 us  [other_core(): return lax.ppermute(block, 'xline', [(i, i ^ 1) for i in range(count)])]
  transfers between devices with their start and end apart: 12 -> 12, of which waited for: 10 -> 9; matrix products, arithmetic and copies ran while one was open for 0% -> 0% of each run, Pallas kernels for 5% -> 5%
where the time goes in v3:
time: 34.9 us; the launch traced here: 34.7 us
  Pallas kernels  14.5 us (42%)
  starting transfers between devices  10.5 us (30%)
  waiting for transfers between devices  9.59 us (27%)
    ppermute x6, starting transfers between devices, along_depth(): lax.ppermute(block, 'depth', [(i, i ^ shift) for i in range(SECTIONS)])  9.55 us
    pallas_call x1, Pallas kernels, continue_all(): pl.pallas_call(continue_kernel, out_shape=[jax.ShapeDtypeStruct((LEVELS,...  8.58 us
    ppermute x6, waiting for transfers between devices, along_depth(): lax.ppermute(block, 'depth', [(i, i ^ shift) for i in range(SECTIONS)])  6.94 us
    pallas_call x1, Pallas kernels, pack(): pl.pallas_call(pack_kernel, out_shape=[block] * 4 + [part] * 2 + [field],...  3.3 us
    ppermute x6, waiting for transfers between devices, other_core(): return lax.ppermute(block, 'xline', [(i, i ^ 1) for i in range(count)])  2.65 us
    pallas_call x1, Pallas kernels, prepare(): pl.pallas_call(prepare_kernel, out_shape=jax.ShapeDtypeStruct((MINE, zone...  1.76 us
    ppermute x6, starting transfers between devices, other_core(): return lax.ppermute(block, 'xline', [(i, i ^ 1) for i in range(count)])  0.91 us
    pallas_call x1, Pallas kernels, assemble(): pl.pallas_call(assemble_kernel, out_shape=jax.ShapeDtypeStruct((1, SECTIO...  0.84 us
  transfers between devices with their start and end apart: 12, of which 9 were waited for; matrix products, arithmetic and copies ran while one was open for 0% of the time, Pallas kernels for 5%

profile of v3, /device:TPU:0, one launch (start us, length us, event | category | flops | bytes accessed | tf_op | source)
XLA Modules:
  0.0 34.7 jit_solution(790175073321424809)
XLA Ops:
  0.0 3.3 %pack.1 = (s16[272,128]{1,0:T(8,128)(2,1)}, s16[272,128]{1,0:T(8,128)(2,1)}, s16[272,128]{1,0:T(8,128)(2,1)}, s16[272,128]{1,0:T(8,128)(2,1)}, bf16[2,2,256,128]...) custom-call(f32[1,1024,128]{2,1,0:T(8,128)} %slow.1, s32[1,4]{1,0:T(1,128)} %zones_x.1, ...), custom_call_target="tpu_custom_call" | custom-call | tf_op jit(solution)/shard_map/pack/pallas_call | solution.py:110
  3.3 0.1 collective-permute-start.3
  3.4 1.7 %collective-permute-start = (s16[272,128]{1,0:T(8,128)(2,1)}, s16[272,128]{1,0:T(8,128)(2,1)S(1)}, u32[]{:S(2)}, u32[]{:S(2)}) collective-permute-start(s16[272,128]{1,0:T(8,128)(2,1)} %get-tuple-element.23), channel_id=1, source_target_pairs={{0,32},{32,0},{64,96},{96,64},{1,33},{33,1},{65,97},{97,65},{2,34}... | collective-permute-start | bytes 208904 | tf_op jit(solution)/shard_map/ppermute | solution.py:331
  5.1 2.9 %collective-permute-start.1 = (s16[272,128]{1,0:T(8,128)(2,1)}, s16[272,128]{1,0:T(8,128)(2,1)S(1)}, u32[]{:S(2)}, u32[]{:S(2)}) collective-permute-start(s16[272,128]{1,0:T(8,128)(2,1)} %get-tuple-element.24), channel_id=1, source_target_pairs={{0,64},{32,96},{64,0},{96,32},{1,65},{33,97},{65,1},{97,33},{2,66}... | collective-permute-start | bytes 208904 | tf_op jit(solution)/shard_map/ppermute | solution.py:331
  8.0 0.1 collective-permute-start.2
  8.2 0.1 collective-permute-start.4
  8.3 1.8 %prepare.1.operators = bf16[2,4,512,512]{3,2,1,0:T(8,128)(2,1)S(1)} custom-call(bf16[4,4,2,256,256]{4,3,2,1,0:T(8,128)(2,1)} %inverses.1), custom_call_target="tpu_custom_call" | custom-call | bytes 6291456 | tf_op jit(solution)/shard_map/prepare/pallas_call | solution.py:152
  10.0 0.0 collective-permute-done.q1
  10.1 2.2 %collective-permute-done.1.q2 = s16[272,128]{1,0:T(8,128)(2,1)S(1)} collective-permute-done((s16[272,128]{1,0:T(8,128)(2,1)}, s16[272,128]{1,0:T(8,128)(2,1)S(1)}, u32[]{:S(2)}, u32[]{:S(2)}) %collective-permute-start.1) | collective-permute-done | bytes 69664 | tf_op jit(solution)/shard_map/ppermute | solution.py:331
  12.3 1.5 %collective-permute-done.2.q3 = s16[272,128]{1,0:T(8,128)(2,1)S(1)} collective-permute-done((s16[272,128]{1,0:T(8,128)(2,1)}, s16[272,128]{1,0:T(8,128)(2,1)S(1)}, u32[]{:S(2)}, u32[]{:S(2)}) %collective-permute-start.2) | collective-permute-done | bytes 69664 | tf_op jit(solution)/shard_map/ppermute | solution.py:331
  13.8 0.0 collective-permute-start.5
  13.8 0.5 %collective-permute-start.6 = (s16[272,128]{1,0:T(8,128)(2,1)S(1)}, s16[272,128]{1,0:T(8,128)(2,1)S(1)}, u32[]{:S(2)}, u32[]{:S(2)}) collective-permute-start(s16[272,128]{1,0:T(8,128)(2,1)S(1)} %collective-permute-done.1.q2), channel_id=1, source_target_pairs={{0,1},{1,0},{2,3},{3,2},{4,5},{5,4},{6,7},{7,6},{8,9},{9,8},{10,11... | collective-permute-start | bytes 208904 | tf_op jit(solution)/shard_map/ppermute | solution.py:336
  14.3 0.0 collective-permute-start.7
  14.3 0.0 collective-permute-done.4.p0
  14.3 0.7 %collective-permute-done.5.p1 = s16[272,128]{1,0:T(8,128)(2,1)S(1)} collective-permute-done((s16[272,128]{1,0:T(8,128)(2,1)S(1)}, s16[272,128]{1,0:T(8,128)(2,1)S(1)}, u32[]{:S(2)}, u32[]{:S(2)}) %collective-permute-start.5) | collective-permute-done | bytes 69664 | tf_op jit(solution)/shard_map/ppermute | solution.py:336
  15.0 0.2 collective-permute-done.6.p2
  15.2 0.4 %collective-permute-done.7.p3 = s16[272,128]{1,0:T(8,128)(2,1)S(1)} collective-permute-done((s16[272,128]{1,0:T(8,128)(2,1)S(1)}, s16[272,128]{1,0:T(8,128)(2,1)S(1)}, u32[]{:S(2)}, u32[]{:S(2)}) %collective-permute-start.7) | collective-permute-done | bytes 69664 | tf_op jit(solution)/shard_map/ppermute | solution.py:336
  15.5 0.0 collective-permute-done.3.rec_other
  15.5 0.0 copy-done
  15.5 0.0 copy-done.2
  15.6 0.0 copy-done.3
  15.6 8.6 %continue_levels.1 = (f32[4,256,128]{2,1,0:T(8,128)S(1)}, bf16[4,256,128]{2,1,0:T(8,128)(2,1)S(1)}) custom-call(f32[4]{0:T(128)S(1)} %copy-done.3, bf16[2,256,512]{2,1,0:T(8,128)(2,1)S(1)} %copy-done, bf16[2,4,512,512]{3,2,1,0:T(8,128)(2,1)S(1)} %prepare.1.operators, bf16[2,2,256,128]{3,2,1,0:T(8,128)(2,1)S(1)} %copy-done.1, ...), custom_call_target="tpu_custom_call" | custom-call | flops 4294967296 | bytes 8388608 | tf_op jit(solution)/shard_map/continue_levels/pallas_call | solution.py:267
  24.2 0.2 collective-permute-start.8
  24.4 1.4 %collective-permute-done.8.got = bf16[4,256,128]{2,1,0:T(8,128)(2,1)S(1)} collective-permute-done((bf16[4,256,128]{2,1,0:T(8,128)(2,1)S(1)}, bf16[4,256,128]{2,1,0:T(8,128)(2,1)S(1)}, u32[]{:S(2)}, u32[]{:S(2)}) %collective-permute-start.8) | collective-permute-done | bytes 262176 | tf_op jit(solution)/shard_map/ppermute | solution.py:336
  25.8 0.1 merge.1
  25.8 0.1 collective-permute-start.9
  25.9 2.4 %collective-permute-start.10 = (bf16[256,128]{1,0:T(8,128)(2,1)S(1)}, bf16[256,128]{1,0:T(8,128)(2,1)S(1)}, u32[]{:S(2)}, u32[]{:S(2)}) collective-permute-start(bf16[256,128]{1,0:T(8,128)(2,1)S(1)} %get-tuple-element.37), channel_id=1, source_target_pairs={{0,64},{32,96},{64,0},{96,32},{1,65},{33,97},{65,1},{97,33},{2,66}... | collective-permute-start | bytes 196616 | tf_op jit(solution)/shard_map/ppermute | solution.py:331
  28.4 2.2 %collective-permute-start.11 = (bf16[256,128]{1,0:T(8,128)(2,1)S(1)}, bf16[256,128]{1,0:T(8,128)(2,1)S(1)}, u32[]{:S(2)}, u32[]{:S(2)}) collective-permute-start(bf16[256,128]{1,0:T(8,128)(2,1)S(1)} %get-tuple-element.38), channel_id=1, source_target_pairs={{0,96},{32,64},{64,32},{96,0},{1,97},{33,65},{65,33},{97,1},{2,98}... | collective-permute-start | bytes 196616 | tf_op jit(solution)/shard_map/ppermute | solution.py:331
  30.6 0.1 collective-permute-done.9.g1
  30.8 1.3 %collective-permute-done.10.g2 = bf16[256,128]{1,0:T(8,128)(2,1)S(1)} collective-permute-done((bf16[256,128]{1,0:T(8,128)(2,1)S(1)}, bf16[256,128]{1,0:T(8,128)(2,1)S(1)}, u32[]{:S(2)}, u32[]{:S(2)}) %collective-permute-start.10) | collective-permute-done | bytes 65568 | tf_op jit(solution)/shard_map/ppermute | solution.py:331
  32.0 1.8 %collective-permute-done.11.g3 = bf16[256,128]{1,0:T(8,128)(2,1)S(1)} collective-permute-done((bf16[256,128]{1,0:T(8,128)(2,1)S(1)}, bf16[256,128]{1,0:T(8,128)(2,1)S(1)}, u32[]{:S(2)}, u32[]{:S(2)}) %collective-permute-start.11) | collective-permute-done | bytes 65568 | tf_op jit(solution)/shard_map/ppermute | solution.py:331
  33.9 0.8 %assemble.1 = f32[1,1024,128]{2,1,0:T(8,128)} custom-call(f32[256,128]{1,0:T(8,128)S(1)} %get-tuple-element.35.own, bf16[256,128]{1,0:T(8,128)(2,1)S(1)} %collective-permute-done.9.g1, bf16[256,128]{1,0:T(8,128)(2,1)S(1)} %collective-permute-done.10.g2, bf16[256,128]{1,0:T(8,128)(2,1)S(1)} %collective-permute-done.11.g3), custom_call_target="tpu_custom_call" | custom-call | tf_op jit(solution)/shard_map/assemble/pallas_call | solution.py:320
  (5 shorter events, 0.0 us)
Async XLA Ops:
  3.3 12.2 %collective-permute-start.3 = (bf16[2,2,256,128]{3,2,1,0:T(8,128)(2,1)}, bf16[2,2,256,128]{3,2,1,0:T(8,128)(2,1)S(1)}, u32[]{:S(2)}, u32[]{:S(2)}) collective-permute-start(bf16[2,2,256,128]{3,2,1,0:T(8,128)(2,1)} %get-tuple-element.28), channel_id=1, source_target_pairs={{0,1},{1,0},{2,3},{3,2},{4,5},{5,4},{6,7},{7,6},{8,9},{9,8},{10,11... | collective-permute-start | bytes 786440 | tf_op jit(solution)/shard_map/ppermute | solution.py:336
  3.4 6.7 %collective-permute-start = (s16[272,128]{1,0:T(8,128)(2,1)}, s16[272,128]{1,0:T(8,128)(2,1)S(1)}, u32[]{:S(2)}, u32[]{:S(2)}) collective-permute-start(s16[272,128]{1,0:T(8,128)(2,1)} %get-tuple-element.23), channel_id=1, source_target_pairs={{0,32},{32,0},{64,96},{96,64},{1,33},{33,1},{65,97},{97,65},{2,34}... | collective-permute-start | bytes 208904 | tf_op jit(solution)/shard_map/ppermute | solution.py:331
  5.1 7.1 %collective-permute-start.1 = (s16[272,128]{1,0:T(8,128)(2,1)}, s16[272,128]{1,0:T(8,128)(2,1)S(1)}, u32[]{:S(2)}, u32[]{:S(2)}) collective-permute-start(s16[272,128]{1,0:T(8,128)(2,1)} %get-tuple-element.24), channel_id=1, source_target_pairs={{0,64},{32,96},{64,0},{96,32},{1,65},{33,97},{65,1},{97,33},{2,66}... | collective-permute-start | bytes 208904 | tf_op jit(solution)/shard_map/ppermute | solution.py:331
  8.0 5.7 %collective-permute-start.2 = (s16[272,128]{1,0:T(8,128)(2,1)}, s16[272,128]{1,0:T(8,128)(2,1)S(1)}, u32[]{:S(2)}, u32[]{:S(2)}) collective-permute-start(s16[272,128]{1,0:T(8,128)(2,1)} %get-tuple-element.25), channel_id=1, source_target_pairs={{0,96},{32,64},{64,32},{96,0},{1,97},{33,65},{65,33},{97,1},{2,98}... | collective-permute-start | bytes 208904 | tf_op jit(solution)/shard_map/ppermute | solution.py:331
  8.2 7.4 %copy-start = (bf16[2,256,512]{2,1,0:T(8,128)(2,1)S(1)}, bf16[2,256,512]{2,1,0:T(8,128)(2,1)}, u32[]{:S(2)}) copy-start(bf16[2,256,512]{2,1,0:T(8,128)(2,1)} %get-tuple-element.22.sources) | copy-start | bytes 1572868
  8.2 7.4 %copy-start.1 = (bf16[2,2,256,128]{3,2,1,0:T(8,128)(2,1)S(1)}, bf16[2,2,256,128]{3,2,1,0:T(8,128)(2,1)}, u32[]{:S(2)}) copy-start(bf16[2,2,256,128]{3,2,1,0:T(8,128)(2,1)} %get-tuple-element.27.rec_mine) | copy-start | bytes 786436
  8.2 7.4 %copy-start.2 = (s16[272,128]{1,0:T(8,128)(2,1)S(1)}, s16[272,128]{1,0:T(8,128)(2,1)}, u32[]{:S(2)}) copy-start(s16[272,128]{1,0:T(8,128)(2,1)} %get-tuple-element.29.q0) | copy-start | bytes 208900
  8.2 7.4 %copy-start.3 = (f32[4]{0:T(128)S(1)}, f32[4]{0:T(128)}, u32[]{:S(2)}) copy-start(f32[4]{0:T(128)} %omegas.1) | copy-start | bytes 52
  8.2 6.1 %collective-permute-start.4 = (s16[272,128]{1,0:T(8,128)(2,1)}, s16[272,128]{1,0:T(8,128)(2,1)S(1)}, u32[]{:S(2)}, u32[]{:S(2)}) collective-permute-start(s16[272,128]{1,0:T(8,128)(2,1)} %get-tuple-element.29.q0), channel_id=1, source_target_pairs={{0,1},{1,0},{2,3},{3,2},{4,5},{5,4},{6,7},{7,6},{8,9},{9,8},{10,11... | collective-permute-start | bytes 208904 | tf_op jit(solution)/shard_map/ppermute | solution.py:336
  13.8 1.3 %collective-permute-start.5 = (s16[272,128]{1,0:T(8,128)(2,1)S(1)}, s16[272,128]{1,0:T(8,128)(2,1)S(1)}, u32[]{:S(2)}, u32[]{:S(2)}) collective-permute-start(s16[272,128]{1,0:T(8,128)(2,1)S(1)} %collective-permute-done.q1), channel_id=1, source_target_pairs={{0,1},{1,0},{2,3},{3,2},{4,5},{5,4},{6,7},{7,6},{8,9},{9,8},{10,11... | collective-permute-start | bytes 208904 | tf_op jit(solution)/shard_map/ppermute | solution.py:336
  13.8 1.4 %collective-permute-start.6 = (s16[272,128]{1,0:T(8,128)(2,1)S(1)}, s16[272,128]{1,0:T(8,128)(2,1)S(1)}, u32[]{:S(2)}, u32[]{:S(2)}) collective-permute-start(s16[272,128]{1,0:T(8,128)(2,1)S(1)} %collective-permute-done.1.q2), channel_id=1, source_target_pairs={{0,1},{1,0},{2,3},{3,2},{4,5},{5,4},{6,7},{7,6},{8,9},{9,8},{10,11... | collective-permute-start | bytes 208904 | tf_op jit(solution)/shard_map/ppermute | solution.py:336
  14.3 1.3 %collective-permute-start.7 = (s16[272,128]{1,0:T(8,128)(2,1)S(1)}, s16[272,128]{1,0:T(8,128)(2,1)S(1)}, u32[]{:S(2)}, u32[]{:S(2)}) collective-permute-start(s16[272,128]{1,0:T(8,128)(2,1)S(1)} %collective-permute-done.2.q3), channel_id=1, source_target_pairs={{0,1},{1,0},{2,3},{3,2},{4,5},{5,4},{6,7},{7,6},{8,9},{9,8},{10,11... | collective-permute-start | bytes 208904 | tf_op jit(solution)/shard_map/ppermute | solution.py:336
  24.2 1.6 %collective-permute-start.8 = (bf16[4,256,128]{2,1,0:T(8,128)(2,1)S(1)}, bf16[4,256,128]{2,1,0:T(8,128)(2,1)S(1)}, u32[]{:S(2)}, u32[]{:S(2)}) collective-permute-start(bf16[4,256,128]{2,1,0:T(8,128)(2,1)S(1)} %get-tuple-element.34), channel_id=1, source_target_pairs={{0,1},{1,0},{2,3},{3,2},{4,5},{5,4},{6,7},{7,6},{8,9},{9,8},{10,11... | collective-permute-start | bytes 786440 | tf_op jit(solution)/shard_map/ppermute | solution.py:336
  25.8 4.9 %collective-permute-start.9 = (bf16[256,128]{1,0:T(8,128)(2,1)S(1)}, bf16[256,128]{1,0:T(8,128)(2,1)S(1)}, u32[]{:S(2)}, u32[]{:S(2)}) collective-permute-start(bf16[256,128]{1,0:T(8,128)(2,1)S(1)} %get-tuple-element.36), channel_id=1, source_target_pairs={{0,32},{32,0},{64,96},{96,64},{1,33},{33,1},{65,97},{97,65},{2,34}... | collective-permute-start | bytes 196616 | tf_op jit(solution)/shard_map/ppermute | solution.py:331
  25.9 6.1 %collective-permute-start.10 = (bf16[256,128]{1,0:T(8,128)(2,1)S(1)}, bf16[256,128]{1,0:T(8,128)(2,1)S(1)}, u32[]{:S(2)}, u32[]{:S(2)}) collective-permute-start(bf16[256,128]{1,0:T(8,128)(2,1)S(1)} %get-tuple-element.37), channel_id=1, source_target_pairs={{0,64},{32,96},{64,0},{96,32},{1,65},{33,97},{65,1},{97,33},{2,66}... | collective-permute-start | bytes 196616 | tf_op jit(solution)/shard_map/ppermute | solution.py:331
  28.4 5.5 %collective-permute-start.11 = (bf16[256,128]{1,0:T(8,128)(2,1)S(1)}, bf16[256,128]{1,0:T(8,128)(2,1)S(1)}, u32[]{:S(2)}, u32[]{:S(2)}) collective-permute-start(bf16[256,128]{1,0:T(8,128)(2,1)S(1)} %get-tuple-element.38), channel_id=1, source_target_pairs={{0,96},{32,64},{64,32},{96,0},{1,97},{33,65},{65,33},{97,1},{2,98}... | collective-permute-start | bytes 196616 | tf_op jit(solution)/shard_map/ppermute | solution.py:331

commit v4 on v3

v4 whole, which is shorter than its diff:
```python
import math

import jax
import jax.numpy as jnp
from jax import lax
from jax.experimental import pallas as pl
from jax.experimental.pallas import tpu as pltpu
from jax.sharding import PartitionSpec as P

F32 = jnp.float32
BF16 = jnp.bfloat16
I32 = jnp.int32
I16 = jnp.int16

SECTIONS = 4
LEVELS = 4
FREQS = 4
MINE = 2
B = 256
H = 128
EXTRA = 16

MIDDLE = 1.1
STEPS = 36000.0

SIN = (4.4428679, -7.30744341, 3.59478797, -0.78437374)
COS = (1.4142135, -6.97885099, 5.73946117, -1.88356295, 0.3106981)

MB = 1 << 20


def horner(u, coefs):
    total = coefs[-1]
    for c in coefs[-2::-1]:
        total = total * u + c
    return total


def place():
    line = lax.axis_index("xline")
    return lax.axis_index("depth"), line // 2, lax.rem(line, 2)


def pack_kernel(slow, zones_x, zones_y, q0, q1, q2, q3, raw, packed, in_sems, out_sems):
    section, pair, _ = place()
    order = ((1, q1), (2, q2), (3, q3), (0, q0))
    arrivals = []
    for shift, _ in order:
        start = pl.ds(pl.multiple_of(lax.bitwise_xor(section, shift) * B, B), B)
        arrivals.append(
            pltpu.make_async_copy(slow.at[0, start, :], raw.at[shift], in_sems.at[shift])
        )
        arrivals[-1].start()
    zone_y = zones_y[0, pair]
    upper = lax.broadcasted_iota(I32, (EXTRA, H), 0) < EXTRA // 2
    departures = []
    for (shift, q), arrival in zip(order, arrivals):
        to = lax.bitwise_xor(section, shift)
        packed[shift, B:, :] = jnp.where(upper, zones_x[0, to], zone_y).astype(I16)
        arrival.wait()
        for r in range(0, B, 32):
            level = (raw[shift, r : r + 32, :] - MIDDLE) * STEPS
            level = jnp.clip(level, -32767.0, 32767.0)
            packed[shift, r : r + 32, :] = jnp.round(level).astype(I32).astype(I16)
        departures.append(pltpu.make_async_copy(packed.at[shift], q, out_sems.at[shift]))
        departures[-1].start()
    for copy in departures:
        copy.wait()


def pack(slowness, zones_x, zones_y):
    smem = pl.BlockSpec(memory_space=pltpu.SMEM)
    hbm = pl.BlockSpec(memory_space=pl.ANY)
    return pl.pallas_call(
        pack_kernel,
        out_shape=[jax.ShapeDtypeStruct((B + EXTRA, H), I16)] * 4,
        in_specs=[hbm, smem, smem],
        out_specs=[hbm] * 4,
        scratch_shapes=[
            pltpu.VMEM((SECTIONS, B, H), F32),
            pltpu.VMEM((SECTIONS, B + EXTRA, H), I16),
            pltpu.SemaphoreType.DMA((SECTIONS,)),
            pltpu.SemaphoreType.DMA((SECTIONS,)),
        ],
        name="pack",
    )(slowness, zones_x, zones_y)


def fields_kernel(
    receiver, amp_hbm, source_x_hbm, source_y_hbm, _, rec_mine, rec_send, sources,
    rec, amp, source_x, source_y, spread, fields, in_sems, out_sems,
):
    section, pair, core = place()
    rows = pl.ds(pl.multiple_of(section * B, B), B)
    parts = [
        receiver.at[pl.ds(lax.rem(core + 1 - k, 2) * MINE, MINE), :, rows, :] for k in range(2)
    ]
    arrivals = [
        pltpu.make_async_copy(*ends, in_sems.at[k])
        for k, ends in enumerate(
            (
                (amp_hbm, amp),
                (source_x_hbm, source_x),
                (source_y_hbm, source_y),
                (parts[0], rec.at[0]),
                (parts[1], rec.at[1]),
            )
        )
    ]
    for copy in arrivals:
        copy.start()
    departures = [
        pltpu.make_async_copy(*ends, out_sems.at[k])
        for k, ends in enumerate(((rec.at[0], rec_send), (rec.at[1], rec_mine), (fields, sources)))
    ]
    for copy in arrivals:
        copy.wait()
    for copy in departures[:2]:
        copy.start()
    count = source_x.shape[1]
    cells = lax.broadcasted_iota(I32, (B, count), 0)
    hot_x = jnp.where(cells + section * B == source_x[...], 1.0, 0.0).astype(BF16)
    hot_y = cells + pair * B == source_y[...]
    for f in range(MINE):
        for part in range(2):
            row = amp[pl.ds(core * MINE + f, 1), part, :].astype(F32)
            spread[part * B : (part + 1) * B, :] = jnp.where(hot_y, row, 0.0).astype(BF16)
        fields[f] = lax.dot_general(
            hot_x, spread[...], (((1,), (1,)), ((), ())), preferred_element_type=F32
        ).astype(BF16)
    departures[2].start()
    for copy in departures:
        copy.wait()


def starting_fields(receiver, amp, source_x, source_y, after):
    part = jax.ShapeDtypeStruct((MINE, 2, B, H), BF16)
    field = jax.ShapeDtypeStruct((MINE, B, 2 * B), BF16)
    hbm = pl.BlockSpec(memory_space=pl.ANY)
    return pl.pallas_call(
        fields_kernel,
        out_shape=[part, part, field],
        in_specs=[hbm] * 5,
        out_specs=[hbm] * 3,
        scratch_shapes=[
            pltpu.VMEM((2, MINE, 2, B, H), BF16),
            pltpu.VMEM(amp.shape, BF16),
            pltpu.VMEM(source_x.shape, I32),
            pltpu.VMEM(source_y.shape, I32),
            pltpu.VMEM((2 * B, source_x.shape[1]), BF16),
            pltpu.VMEM((MINE, B, 2 * B), BF16),
            pltpu.SemaphoreType.DMA((5,)),
            pltpu.SemaphoreType.DMA((3,)),
        ],
        cost_estimate=pl.CostEstimate(flops=8 * B**3, bytes_accessed=3 * MB, transcendentals=0),
        name="starting_fields",
    )(receiver, amp, source_x, source_y, after)


def prepare_kernel(inverses, operators, table, sems):
    core = place()[2]
    copies = [
        pltpu.make_async_copy(inverses.at[core * MINE + f], table.at[f], sems.at[f])
        for f in range(MINE)
    ]
    for copy in copies:
        copy.start()
    for f in range(MINE):
        copies[f].wait()
        for zone in range(table.shape[1]):
            real = table[f, zone, 0]
            imag = table[f, zone, 1]
            operators[f, zone, :B, :B] = real
            operators[f, zone, B:, B:] = real
            operators[f, zone, B:, :B] = imag
            operators[f, zone, :B, B:] = -imag


def prepare(inverses):
    zones = inverses.shape[1]
    return pl.pallas_call(
        prepare_kernel,
        out_shape=jax.ShapeDtypeStruct((MINE, zones, 2 * B, 2 * B), BF16),
        in_specs=[pl.BlockSpec(memory_space=pltpu.HBM)],
        out_specs=pl.BlockSpec(memory_space=pltpu.VMEM),
        scratch_shapes=[
            pltpu.VMEM((MINE, zones, 2, B, B), BF16),
            pltpu.SemaphoreType.DMA((MINE,)),
        ],
        compiler_params=pltpu.CompilerParams(vmem_limit_bytes=48 * MB),
        cost_estimate=pl.CostEstimate(flops=0, bytes_accessed=6 * MB, transcendentals=0),
        name="prepare",
    )(inverses)


def continue_kernel(
    omegas, sources, operators, rec_mine, rec_other,
    q0, q1, q2, q3, p0, p1, p2, p3,
    grad_mine, grad_other,
    slow, zones, total, *waves,
):
    section, _, core = place()
    W, X, X32, Y, Y32 = (waves[k : k + MINE] for k in range(0, 5 * MINE, MINE))
    mine = pl.ds(pl.multiple_of(core * H, H), H)
    other = pl.ds(pl.multiple_of((1 - core) * H, H), H)

    for shift, (q, p) in enumerate(((q0, p0), (q1, p1), (q2, p2), (q3, p3))):
        level = lax.bitwise_xor(section, shift)
        for r in range(0, B, 32):
            slow[level, r : r + 32, mine] = q[r : r + 32, :].astype(I32).astype(F32)
            slow[level, r : r + 32, other] = p[r : r + 32, :].astype(I32).astype(F32)
        marks = q[B:, :].astype(I32)
        zones[level, 0] = jnp.max(marks[: EXTRA // 2])
        zones[level, 1] = jnp.max(marks[EXTRA // 2 :])

    for f in range(MINE):
        W[f][:B, :] = sources[f].astype(F32)
        for columns, rec in ((mine, rec_mine), (other, rec_other)):
            W[f][B:, columns] = rec[f, 0].astype(F32)
        imag_mine = pl.ds(pl.multiple_of(B + core * H, H), H)
        imag_other = pl.ds(pl.multiple_of(B + (1 - core) * H, H), H)
        for columns, rec in ((imag_mine, rec_mine), (imag_other, rec_other)):
            W[f][B:, columns] = -rec[f, 1].astype(F32)

    CH, PER = 8, 24

    def rotate(level, f):
        omega = omegas[core * MINE + f]
        scale = omega * (0.5 / math.pi / STEPS)
        base = omega * (0.5 / math.pi * MIDDLE) - 0.5
        for r in range(0, B, CH):
            for c in range(0, B, H):
                turn = slow[level, r : r + CH, c : c + H] * scale + base
                square = turn * turn
                half_sin = turn * horner(square, SIN)
                half_cos = horner(square, COS)
                cosine = half_sin * half_sin - 1.0
                sine = -half_sin * half_cos
                for wave in range(0, 2 * B, B):
                    rows = slice(wave + r, wave + r + CH)
                    columns = slice(wave + c, wave + c + H)
                    real = W[f][rows, c : c + H]
                    imag = W[f][rows, B + c : B + c + H]
                    for down, value in (
                        (r, real * cosine - imag * sine),
                        (B + r, real * sine + imag * cosine),
                    ):
                        X32[f][down : down + CH, columns] = value
                        X[f][down : down + CH, columns] = value.astype(BF16)
                yield

    def inline(level, f):
        zone = zones[level, 0]
        for wave in range(0, 2 * B, B):
            update = jnp.dot(
                operators[f, zone], X[f][:, wave : wave + B], preferred_element_type=F32
            )
            yield
            for part in range(0, 2 * B, B):
                value = X32[f][part : part + B, wave : wave + B] + update[part : part + B]
                Y32[f][wave : wave + B, part : part + B] = value
                Y[f][wave : wave + B, part : part + B] = value.astype(BF16)

    def crossline(level, f):
        zone = zones[level, 1]
        omega = omegas[core * MINE + f]
        for part in range(0, 2 * B, B):
            update = lax.dot_general(
                Y[f][...],
                operators[f, zone, part : part + B, :],
                (((1,), (1,)), ((), ())),
                preferred_element_type=F32,
            )
            yield
            for c in range(0, B, H):
                for r in range(0, B, CH):
                    new = []
                    columns = slice(part + c, part + c + H)
                    for wave in range(0, 2 * B, B):
                        rows = slice(wave + r, wave + r + CH)
                        value = Y32[f][rows, columns] + update[rows, c : c + H]
                        W[f][rows, columns] = value
                        new.append(value)
                    if part > 0:
                        term = W[f][r : r + CH, c : c + H] * W[f][B + r : B + r + CH, c : c + H]
                        term = (term - new[0] * new[1]) * (omega * omega)
                        if f > 0:
                            term += total[c // H, level, r : r + CH, :]
                        total[c // H, level, r : r + CH, :] = term

    def side_by_side(products, others):
        for _ in products:
            for _ in range(PER):
                next(others, None)
        for _ in others:
            pass

    def both(level, f):
        yield from inline(level, f)
        yield from crossline(level, f)

    def one_level(level, carry):
        @pl.when(level < LEVELS)
        def _():
            side_by_side(both(level, 0), rotate(level, 1))

        @pl.when(level >= 0)
        def _():
            following = jnp.minimum(level + 1, LEVELS - 1)
            side_by_side(both(level, 1), rotate(following, 0))

        return carry

    for _ in rotate(0, 0):
        pass
    lax.fori_loop(0, LEVELS, one_level, 0)
    grad_mine[...] = total[core]
    grad_other[...] = total[1 - core].astype(BF16)


def continue_all(omegas, sources, operators, rec_mine, rec_other, mine, other):
    vmem = pl.BlockSpec(memory_space=pltpu.VMEM)
    smem = pl.BlockSpec(memory_space=pltpu.SMEM)
    return pl.pallas_call(
        continue_kernel,
        out_shape=[
            jax.ShapeDtypeStruct((LEVELS, B, H), F32),
            jax.ShapeDtypeStruct((LEVELS, B, H), BF16),
        ],
        in_specs=[smem] + [vmem] * 12,
        out_specs=[vmem, vmem],
        scratch_shapes=[
            pltpu.VMEM((LEVELS, B, B), F32),
            pltpu.SMEM((LEVELS, 2), I32),
            pltpu.VMEM((2, LEVELS, B, H), F32),
            *[pltpu.VMEM((2 * B, 2 * B), kind) for kind in (F32, BF16, F32, BF16, F32) for _ in range(MINE)],
        ],
        compiler_params=pltpu.CompilerParams(vmem_limit_bytes=32 * MB),
        cost_estimate=pl.CostEstimate(
            flops=2 * 128 * B**3, bytes_accessed=8 * MB, transcendentals=0
        ),
        name="continue_levels",
    )(omegas, sources, operators, rec_mine, rec_other, *mine, *other)


def merge_kernel(mine, got, own, s1, s2, s3):
    section, _, _ = place()
    for shift, out in enumerate((own, s1, s2, s3)):
        level = lax.bitwise_xor(section, shift)
        out[...] = (mine[level] + got[level].astype(F32)).astype(out.dtype)


def merge(mine, got):
    vmem = pl.BlockSpec(memory_space=pltpu.VMEM)
    return pl.pallas_call(
        merge_kernel,
        out_shape=[jax.ShapeDtypeStruct((B, H), F32)]
        + [jax.ShapeDtypeStruct((B, H), BF16)] * 3,
        in_specs=[vmem, vmem],
        out_specs=[vmem] * 4,
        compiler_params=pltpu.CompilerParams(vmem_limit_bytes=8 * MB),
        name="merge",
    )(mine, got)


def assemble_kernel(own, g1, g2, g3, out):
    section, _, _ = place()
    for shift, block in enumerate((own, g1, g2, g3)):
        origin = lax.bitwise_xor(section, shift)
        out[0, pl.ds(pl.multiple_of(origin * B, B), B), :] = block[...].astype(F32)


def assemble(own, blocks):
    vmem = pl.BlockSpec(memory_space=pltpu.VMEM)
    return pl.pallas_call(
        assemble_kernel,
        out_shape=jax.ShapeDtypeStruct((1, SECTIONS * B, H), F32),
        in_specs=[vmem] * 4,
        out_specs=vmem,
        compiler_params=pltpu.CompilerParams(vmem_limit_bytes=8 * MB),
        name="assemble",
    )(own, *blocks)


def along_depth(block, shift):
    return lax.ppermute(block, "depth", [(i, i ^ shift) for i in range(SECTIONS)])


def other_core(block):
    count = lax.axis_size("xline")
    return lax.ppermute(block, "xline", [(i, i ^ 1) for i in range(count)])


def per_device(
    receiver_data, source_amp, source_x, source_y, omegas, slowness, inverses, zones_x, zones_y
):
    blocks = pack(slowness, zones_x, zones_y)
    moved = [along_depth(blocks[k], k) for k in (1, 2, 3)]
    rec_mine, rec_send, sources = starting_fields(
        receiver_data, source_amp, source_x.reshape(1, -1), source_y.reshape(1, -1), blocks[0]
    )
    own_other = other_core(blocks[0])
    inverses, sources = lax.optimization_barrier((inverses, sources))
    operators, rec_send, *moved = lax.optimization_barrier(
        (prepare(inverses), rec_send, *moved)
    )
    rec_other = other_core(rec_send)
    mine = [blocks[0], *moved]
    other = [own_other] + [other_core(block) for block in moved]
    grad_mine, grad_other = continue_all(
        omegas, sources, operators, rec_mine, rec_other, mine, other
    )
    own, *parts = merge(grad_mine, other_core(grad_other))
    return assemble(own, [along_depth(parts[k - 1], k) for k in (1, 2, 3)])


def solution(mesh):
    in_specs = (
        P(None, None, None, "xline"),
        P(),
        P(),
        P(),
        P(),
        P("depth", None, "xline"),
        P(),
        P("depth", None),
        P("depth", None),
    )
    return jax.shard_map(
        per_device,
        mesh=mesh,
        in_specs=in_specs,
        out_specs=P("depth", None, "xline"),
        check_vma=False,
    )
```

time: 34.9 us -> 34 us (0.974)
  waiting for transfers between devices: 9.59 us -> 8.01 us
  starting transfers between devices: 10.5 us -> 10.9 us
    ppermute x6, waiting for transfers between devices: 6.94 us -> 5.44 us  [along_depth(): lax.ppermute(block, 'depth', [(i, i ^ shift) for i in range(SECTIONS)])]
    pallas_call x1 -> x2, Pallas kernels: 3.3 us -> 4.78 us  [the longest x1 2.5 us: pack(): pl.pallas_call(pack_kernel, out_shape=[jax.ShapeDtypeStruct((B + EXTRA, H...]
    pallas_call x1, Pallas kernels: 8.58 us -> 7.33 us  [continue_all(): pl.pallas_call(continue_kernel, out_shape=[jax.ShapeDtypeStruct((LEVELS,...]
    ppermute x6, starting transfers between devices: 0.91 us -> 1.33 us  [other_core(): return lax.ppermute(block, 'xline', [(i, i ^ 1) for i in range(count)])]
  transfers between devices with their start and end apart: 12 -> 12, of which waited for: 9 -> 9; matrix products, arithmetic and copies ran while one was open for 0% -> 0% of each run, Pallas kernels for 5% -> 12%
where the time goes in v4:
time: 34 us; the launch traced here: 33.8 us
  Pallas kernels  14.8 us (44%)
  starting transfers between devices  10.9 us (32%)
  waiting for transfers between devices  8.01 us (24%)
    ppermute x6, starting transfers between devices, along_depth(): lax.ppermute(block, 'depth', [(i, i ^ shift) for i in range(SECTIONS)])  9.55 us
    pallas_call x1, Pallas kernels, continue_all(): pl.pallas_call(continue_kernel, out_shape=[jax.ShapeDtypeStruct((LEVELS,...  7.33 us
    ppermute x6, waiting for transfers between devices, along_depth(): lax.ppermute(block, 'depth', [(i, i ^ shift) for i in range(SECTIONS)])  5.44 us
    ppermute x6, waiting for transfers between devices, other_core(): return lax.ppermute(block, 'xline', [(i, i ^ 1) for i in range(count)])  2.56 us
    pallas_call x1, Pallas kernels, pack(): pl.pallas_call(pack_kernel, out_shape=[jax.ShapeDtypeStruct((B + EXTRA, H...  2.5 us
    pallas_call x1, Pallas kernels, starting_fields(): pl.pallas_call(fields_kernel, out_shape=[part, part, field], in_specs=[hb...  2.28 us
    pallas_call x1, Pallas kernels, prepare(): pl.pallas_call(prepare_kernel, out_shape=jax.ShapeDtypeStruct((MINE, zone...  1.78 us
    ppermute x6, starting transfers between devices, other_core(): return lax.ppermute(block, 'xline', [(i, i ^ 1) for i in range(count)])  1.33 us
  transfers between devices with their start and end apart: 12, of which 9 were waited for; matrix products, arithmetic and copies ran while one was open for 0% of the time, Pallas kernels for 12%

profile of v4, /device:TPU:0, one launch (start us, length us, event | category | flops | bytes accessed | tf_op | source)
XLA Modules:
  0.0 33.8 jit_solution(151498353711193624)
XLA Ops:
  0.0 2.5 %pack.1 = (s16[272,128]{1,0:T(8,128)(2,1)}, s16[272,128]{1,0:T(8,128)(2,1)}, s16[272,128]{1,0:T(8,128)(2,1)}, s16[272,128]{1,0:T(8,128)(2,1)}) custom-call(f32[1,1024,128]{2,1,0:T(8,128)} %slow.1, s32[1,4]{1,0:T(1,128)} %zones_x.1, s32[1,16]{1,0:T(1,128)} %zones_y.1), custom_call_target="tpu_custom_call" | custom-call | tf_op jit(solution)/shard_map/pack/pallas_call | solution.py:74
  2.5 1.7 %collective-permute-start = (s16[272,128]{1,0:T(8,128)(2,1)}, s16[272,128]{1,0:T(8,128)(2,1)S(1)}, u32[]{:S(2)}, u32[]{:S(2)}) collective-permute-start(s16[272,128]{1,0:T(8,128)(2,1)} %get-tuple-element.30), channel_id=1, source_target_pairs={{0,32},{32,0},{64,96},{96,64},{1,33},{33,1},{65,97},{97,65},{2,34}... | collective-permute-start | bytes 208904 | tf_op jit(solution)/shard_map/ppermute | solution.py:386
  4.2 2.9 %collective-permute-start.1 = (s16[272,128]{1,0:T(8,128)(2,1)}, s16[272,128]{1,0:T(8,128)(2,1)S(1)}, u32[]{:S(2)}, u32[]{:S(2)}) collective-permute-start(s16[272,128]{1,0:T(8,128)(2,1)} %get-tuple-element.31), channel_id=1, source_target_pairs={{0,64},{32,96},{64,0},{96,32},{1,65},{33,97},{65,1},{97,33},{2,66}... | collective-permute-start | bytes 208904 | tf_op jit(solution)/shard_map/ppermute | solution.py:386
  7.1 0.1 collective-permute-start.2
  7.3 2.3 %starting_fields.1 = (bf16[2,2,256,128]{3,2,1,0:T(8,128)(2,1)}, bf16[2,2,256,128]{3,2,1,0:T(8,128)(2,1)}, bf16[2,256,512]{2,1,0:T(8,128)(2,1)}) custom-call(bf16[4,2,1024,128]{3,2,1,0:T(8,128)(2,1)} %receiver.1, bf16[4,2,256]{2,1,0:T(2,128)(2,1)} %amp_hbm.1, s32[1,256]{1,0:T(1,128)} %bitcast.2, s32[1,256]{1,0:T(1,128)} %bitcast.3, ...), custom_call_target="tpu_custom_call" | custom-call | flops 134217728 | bytes 3145728 | tf_op jit(solution)/shard_map/starting_fields/pallas_call | solution.py:140
  9.6 0.0 copy-start.1
  9.6 0.0 copy-start.3
  9.6 1.8 %prepare.1.operators = bf16[2,4,512,512]{3,2,1,0:T(8,128)(2,1)S(1)} custom-call(bf16[4,4,2,256,256]{4,3,2,1,0:T(8,128)(2,1)} %inverses), custom_call_target="tpu_custom_call" | custom-call | bytes 6291456 | tf_op jit(solution)/shard_map/prepare/pallas_call | solution.py:181
  11.4 0.0 collective-permute-done.q1
  11.4 0.0 collective-permute-done.1.q2
  11.4 1.4 %collective-permute-done.2.q3 = s16[272,128]{1,0:T(8,128)(2,1)S(1)} collective-permute-done((s16[272,128]{1,0:T(8,128)(2,1)}, s16[272,128]{1,0:T(8,128)(2,1)S(1)}, u32[]{:S(2)}, u32[]{:S(2)}) %collective-permute-start.2) | collective-permute-done | bytes 69664 | tf_op jit(solution)/shard_map/ppermute | solution.py:386
  12.9 0.0 collective-permute-start.3
  12.9 0.5 %collective-permute-start.4 = (s16[272,128]{1,0:T(8,128)(2,1)S(1)}, s16[272,128]{1,0:T(8,128)(2,1)S(1)}, u32[]{:S(2)}, u32[]{:S(2)}) collective-permute-start(s16[272,128]{1,0:T(8,128)(2,1)S(1)} %copy-done), channel_id=1, source_target_pairs={{0,1},{1,0},{2,3},{3,2},{4,5},{5,4},{6,7},{7,6},{8,9},{9,8},{10,11... | collective-permute-start | bytes 208904 | tf_op jit(solution)/shard_map/ppermute | solution.py:391
  13.4 0.1 collective-permute-start.5
  13.5 0.4 %collective-permute-start.6 = (s16[272,128]{1,0:T(8,128)(2,1)S(1)}, s16[272,128]{1,0:T(8,128)(2,1)S(1)}, u32[]{:S(2)}, u32[]{:S(2)}) collective-permute-start(s16[272,128]{1,0:T(8,128)(2,1)S(1)} %collective-permute-done.1.q2), channel_id=1, source_target_pairs={{0,1},{1,0},{2,3},{3,2},{4,5},{5,4},{6,7},{7,6},{8,9},{9,8},{10,11... | collective-permute-start | bytes 208904 | tf_op jit(solution)/shard_map/ppermute | solution.py:391
  13.9 0.1 collective-permute-start.7
  14.0 0.5 %collective-permute-done.4.p0 = s16[272,128]{1,0:T(8,128)(2,1)S(1)} collective-permute-done((s16[272,128]{1,0:T(8,128)(2,1)S(1)}, s16[272,128]{1,0:T(8,128)(2,1)S(1)}, u32[]{:S(2)}, u32[]{:S(2)}) %collective-permute-start.4) | collective-permute-done | bytes 69664 | tf_op jit(solution)/shard_map/ppermute | solution.py:391
  14.5 0.1 collective-permute-done.5.p1
  14.7 0.2 collective-permute-done.6.p2
  14.8 0.4 %collective-permute-done.7.p3 = s16[272,128]{1,0:T(8,128)(2,1)S(1)} collective-permute-done((s16[272,128]{1,0:T(8,128)(2,1)S(1)}, s16[272,128]{1,0:T(8,128)(2,1)S(1)}, u32[]{:S(2)}, u32[]{:S(2)}) %collective-permute-start.7) | collective-permute-done | bytes 69664 | tf_op jit(solution)/shard_map/ppermute | solution.py:391
  15.2 0.0 collective-permute-done.3.rec_other
  15.2 7.3 %continue_levels.1 = (f32[4,256,128]{2,1,0:T(8,128)S(1)}, bf16[4,256,128]{2,1,0:T(8,128)(2,1)S(1)}) custom-call(f32[4]{0:T(128)S(1)} %copy-done.3, bf16[2,256,512]{2,1,0:T(8,128)(2,1)S(1)} %copy-done.1, bf16[2,4,512,512]{3,2,1,0:T(8,128)(2,1)S(1)} %prepare.1.operators, bf16[2,2,256,128]{3,2,1,0:T(8,128)(2,1)S(1)} %copy-done.2, ...), custom_call_target="tpu_custom_call" | custom-call | flops 4294967296 | bytes 8388608 | tf_op jit(solution)/shard_map/continue_levels/pallas_call | solution.py:324
  22.5 0.2 collective-permute-start.8
  22.8 1.4 %collective-permute-done.8.got = bf16[4,256,128]{2,1,0:T(8,128)(2,1)S(1)} collective-permute-done((bf16[4,256,128]{2,1,0:T(8,128)(2,1)S(1)}, bf16[4,256,128]{2,1,0:T(8,128)(2,1)S(1)}, u32[]{:S(2)}, u32[]{:S(2)}) %collective-permute-start.8) | collective-permute-done | bytes 262176 | tf_op jit(solution)/shard_map/ppermute | solution.py:391
  24.1 0.1 merge.1
  24.2 0.1 collective-permute-start.9
  24.3 3.2 %collective-permute-start.10 = (bf16[256,128]{1,0:T(8,128)(2,1)S(1)}, bf16[256,128]{1,0:T(8,128)(2,1)S(1)}, u32[]{:S(2)}, u32[]{:S(2)}) collective-permute-start(bf16[256,128]{1,0:T(8,128)(2,1)S(1)} %get-tuple-element.43), channel_id=1, source_target_pairs={{0,64},{32,96},{64,0},{96,32},{1,65},{33,97},{65,1},{97,33},{2,66}... | collective-permute-start | bytes 196616 | tf_op jit(solution)/shard_map/ppermute | solution.py:386
  27.5 1.5 %collective-permute-start.11 = (bf16[256,128]{1,0:T(8,128)(2,1)S(1)}, bf16[256,128]{1,0:T(8,128)(2,1)S(1)}, u32[]{:S(2)}, u32[]{:S(2)}) collective-permute-start(bf16[256,128]{1,0:T(8,128)(2,1)S(1)} %get-tuple-element.44), channel_id=1, source_target_pairs={{0,96},{32,64},{64,32},{96,0},{1,97},{33,65},{65,33},{97,1},{2,98}... | collective-permute-start | bytes 196616 | tf_op jit(solution)/shard_map/ppermute | solution.py:386
  29.0 0.1 collective-permute-done.9.g1
  29.1 1.9 %collective-permute-done.10.g2 = bf16[256,128]{1,0:T(8,128)(2,1)S(1)} collective-permute-done((bf16[256,128]{1,0:T(8,128)(2,1)S(1)}, bf16[256,128]{1,0:T(8,128)(2,1)S(1)}, u32[]{:S(2)}, u32[]{:S(2)}) %collective-permute-start.10) | collective-permute-done | bytes 65568 | tf_op jit(solution)/shard_map/ppermute | solution.py:386
  31.0 1.9 %collective-permute-done.11.g3 = bf16[256,128]{1,0:T(8,128)(2,1)S(1)} collective-permute-done((bf16[256,128]{1,0:T(8,128)(2,1)S(1)}, bf16[256,128]{1,0:T(8,128)(2,1)S(1)}, u32[]{:S(2)}, u32[]{:S(2)}) %collective-permute-start.11) | collective-permute-done | bytes 65568 | tf_op jit(solution)/shard_map/ppermute | solution.py:386
  33.0 0.8 %assemble.1 = f32[1,1024,128]{2,1,0:T(8,128)} custom-call(f32[256,128]{1,0:T(8,128)S(1)} %get-tuple-element.41.own, bf16[256,128]{1,0:T(8,128)(2,1)S(1)} %collective-permute-done.9.g1, bf16[256,128]{1,0:T(8,128)(2,1)S(1)} %collective-permute-done.10.g2, bf16[256,128]{1,0:T(8,128)(2,1)S(1)} %collective-permute-done.11.g3), custom_call_target="tpu_custom_call" | custom-call | tf_op jit(solution)/shard_map/assemble/pallas_call | solution.py:375
  (8 shorter events, 0.0 us)
Async XLA Ops:
  2.5 8.9 %collective-permute-start = (s16[272,128]{1,0:T(8,128)(2,1)}, s16[272,128]{1,0:T(8,128)(2,1)S(1)}, u32[]{:S(2)}, u32[]{:S(2)}) collective-permute-start(s16[272,128]{1,0:T(8,128)(2,1)} %get-tuple-element.30), channel_id=1, source_target_pairs={{0,32},{32,0},{64,96},{96,64},{1,33},{33,1},{65,97},{97,65},{2,34}... | collective-permute-start | bytes 208904 | tf_op jit(solution)/shard_map/ppermute | solution.py:386
  4.2 7.2 %collective-permute-start.1 = (s16[272,128]{1,0:T(8,128)(2,1)}, s16[272,128]{1,0:T(8,128)(2,1)S(1)}, u32[]{:S(2)}, u32[]{:S(2)}) collective-permute-start(s16[272,128]{1,0:T(8,128)(2,1)} %get-tuple-element.31), channel_id=1, source_target_pairs={{0,64},{32,96},{64,0},{96,32},{1,65},{33,97},{65,1},{97,33},{2,66}... | collective-permute-start | bytes 208904 | tf_op jit(solution)/shard_map/ppermute | solution.py:386
  7.1 5.7 %collective-permute-start.2 = (s16[272,128]{1,0:T(8,128)(2,1)}, s16[272,128]{1,0:T(8,128)(2,1)S(1)}, u32[]{:S(2)}, u32[]{:S(2)}) collective-permute-start(s16[272,128]{1,0:T(8,128)(2,1)} %get-tuple-element.32), channel_id=1, source_target_pairs={{0,96},{32,64},{64,32},{96,0},{1,97},{33,65},{65,33},{97,1},{2,98}... | collective-permute-start | bytes 208904 | tf_op jit(solution)/shard_map/ppermute | solution.py:386
  9.6 3.3 %copy-start.4 = (bf16[2,2,256,128]{3,2,1,0:T(8,128)(2,1)S(1)}, bf16[2,2,256,128]{3,2,1,0:T(8,128)(2,1)}, u32[]{:S(2)}) copy-start(bf16[2,2,256,128]{3,2,1,0:T(8,128)(2,1)} %get-tuple-element.35) | copy-start | bytes 786436
  9.6 3.3 %copy-start = (s16[272,128]{1,0:T(8,128)(2,1)S(1)}, s16[272,128]{1,0:T(8,128)(2,1)}, u32[]{:S(2)}) copy-start(s16[272,128]{1,0:T(8,128)(2,1)} %get-tuple-element.25._.q0) | copy-start | bytes 208900
  9.6 5.6 %copy-start.1 = (bf16[2,256,512]{2,1,0:T(8,128)(2,1)S(1)}, bf16[2,256,512]{2,1,0:T(8,128)(2,1)}, u32[]{:S(2)}) copy-start(bf16[2,256,512]{2,1,0:T(8,128)(2,1)} %get-tuple-element.27.sources) | copy-start | bytes 1572868
  9.6 5.6 %copy-start.2 = (bf16[2,2,256,128]{3,2,1,0:T(8,128)(2,1)S(1)}, bf16[2,2,256,128]{3,2,1,0:T(8,128)(2,1)}, u32[]{:S(2)}) copy-start(bf16[2,2,256,128]{3,2,1,0:T(8,128)(2,1)} %get-tuple-element.34.rec_mine) | copy-start | bytes 786436
  9.6 5.6 %copy-start.3 = (f32[4]{0:T(128)S(1)}, f32[4]{0:T(128)}, u32[]{:S(2)}) copy-start(f32[4]{0:T(128)} %omegas.1) | copy-start | bytes 52
  12.9 2.3 %collective-permute-start.3 = (bf16[2,2,256,128]{3,2,1,0:T(8,128)(2,1)S(1)}, bf16[2,2,256,128]{3,2,1,0:T(8,128)(2,1)S(1)}, u32[]{:S(2)}, u32[]{:S(2)}) collective-permute-start(bf16[2,2,256,128]{3,2,1,0:T(8,128)(2,1)S(1)} %copy-done.4), channel_id=1, source_target_pairs={{0,1},{1,0},{2,3},{3,2},{4,5},{5,4},{6,7},{7,6},{8,9},{9,8},{10,11... | collective-permute-start | bytes 786440 | tf_op jit(solution)/shard_map/ppermute | solution.py:391
  12.9 1.6 %collective-permute-start.4 = (s16[272,128]{1,0:T(8,128)(2,1)S(1)}, s16[272,128]{1,0:T(8,128)(2,1)S(1)}, u32[]{:S(2)}, u32[]{:S(2)}) collective-permute-start(s16[272,128]{1,0:T(8,128)(2,1)S(1)} %copy-done), channel_id=1, source_target_pairs={{0,1},{1,0},{2,3},{3,2},{4,5},{5,4},{6,7},{7,6},{8,9},{9,8},{10,11... | collective-permute-start | bytes 208904 | tf_op jit(solution)/shard_map/ppermute | solution.py:391
  13.4 1.3 %collective-permute-start.5 = (s16[272,128]{1,0:T(8,128)(2,1)S(1)}, s16[272,128]{1,0:T(8,128)(2,1)S(1)}, u32[]{:S(2)}, u32[]{:S(2)}) collective-permute-start(s16[272,128]{1,0:T(8,128)(2,1)S(1)} %collective-permute-done.q1), channel_id=1, source_target_pairs={{0,1},{1,0},{2,3},{3,2},{4,5},{5,4},{6,7},{7,6},{8,9},{9,8},{10,11... | collective-permute-start | bytes 208904 | tf_op jit(solution)/shard_map/ppermute | solution.py:391
  13.5 1.3 %collective-permute-start.6 = (s16[272,128]{1,0:T(8,128)(2,1)S(1)}, s16[272,128]{1,0:T(8,128)(2,1)S(1)}, u32[]{:S(2)}, u32[]{:S(2)}) collective-permute-start(s16[272,128]{1,0:T(8,128)(2,1)S(1)} %collective-permute-done.1.q2), channel_id=1, source_target_pairs={{0,1},{1,0},{2,3},{3,2},{4,5},{5,4},{6,7},{7,6},{8,9},{9,8},{10,11... | collective-permute-start | bytes 208904 | tf_op jit(solution)/shard_map/ppermute | solution.py:391
  13.9 1.3 %collective-permute-start.7 = (s16[272,128]{1,0:T(8,128)(2,1)S(1)}, s16[272,128]{1,0:T(8,128)(2,1)S(1)}, u32[]{:S(2)}, u32[]{:S(2)}) collective-permute-start(s16[272,128]{1,0:T(8,128)(2,1)S(1)} %collective-permute-done.2.q3), channel_id=1, source_target_pairs={{0,1},{1,0},{2,3},{3,2},{4,5},{5,4},{6,7},{7,6},{8,9},{9,8},{10,11... | collective-permute-start | bytes 208904 | tf_op jit(solution)/shard_map/ppermute | solution.py:391
  22.5 1.6 %collective-permute-start.8 = (bf16[4,256,128]{2,1,0:T(8,128)(2,1)S(1)}, bf16[4,256,128]{2,1,0:T(8,128)(2,1)S(1)}, u32[]{:S(2)}, u32[]{:S(2)}) collective-permute-start(bf16[4,256,128]{2,1,0:T(8,128)(2,1)S(1)} %get-tuple-element.40), channel_id=1, source_target_pairs={{0,1},{1,0},{2,3},{3,2},{4,5},{5,4},{6,7},{7,6},{8,9},{9,8},{10,11... | collective-permute-start | bytes 786440 | tf_op jit(solution)/shard_map/ppermute | solution.py:391
  24.2 4.9 %collective-permute-start.9 = (bf16[256,128]{1,0:T(8,128)(2,1)S(1)}, bf16[256,128]{1,0:T(8,128)(2,1)S(1)}, u32[]{:S(2)}, u32[]{:S(2)}) collective-permute-start(bf16[256,128]{1,0:T(8,128)(2,1)S(1)} %get-tuple-element.42), channel_id=1, source_target_pairs={{0,32},{32,0},{64,96},{96,64},{1,33},{33,1},{65,97},{97,65},{2,34}... | collective-permute-start | bytes 196616 | tf_op jit(solution)/shard_map/ppermute | solution.py:386
  24.3 6.7 %collective-permute-start.10 = (bf16[256,128]{1,0:T(8,128)(2,1)S(1)}, bf16[256,128]{1,0:T(8,128)(2,1)S(1)}, u32[]{:S(2)}, u32[]{:S(2)}) collective-permute-start(bf16[256,128]{1,0:T(8,128)(2,1)S(1)} %get-tuple-element.43), channel_id=1, source_target_pairs={{0,64},{32,96},{64,0},{96,32},{1,65},{33,97},{65,1},{97,33},{2,66}... | collective-permute-start | bytes 196616 | tf_op jit(solution)/shard_map/ppermute | solution.py:386
  27.5 5.5 %collective-permute-start.11 = (bf16[256,128]{1,0:T(8,128)(2,1)S(1)}, bf16[256,128]{1,0:T(8,128)(2,1)S(1)}, u32[]{:S(2)}, u32[]{:S(2)}) collective-permute-start(bf16[256,128]{1,0:T(8,128)(2,1)S(1)} %get-tuple-element.44), channel_id=1, source_target_pairs={{0,96},{32,64},{64,32},{96,0},{1,97},{33,65},{65,33},{97,1},{2,98}... | collective-permute-start | bytes 196616 | tf_op jit(solution)/shard_map/ppermute | solution.py:386

commit v5 on v4

--- a/solution.py
+++ b/solution.py
@@ -46,7 +46,7 @@
     order = ((1, q1), (2, q2), (3, q3), (0, q0))
     arrivals = []
     for shift, _ in order:
-        start = pl.ds(pl.multiple_of(lax.bitwise_xor(section, shift) * B, B), B)
+        start = pl.ds(pl.multiple_of(lax.rem(section + shift, SECTIONS) * B, B), B)
         arrivals.append(
             pltpu.make_async_copy(slow.at[0, start, :], raw.at[shift], in_sems.at[shift])
         )
@@ -55,7 +55,7 @@
     upper = lax.broadcasted_iota(I32, (EXTRA, H), 0) < EXTRA // 2
     departures = []
     for (shift, q), arrival in zip(order, arrivals):
-        to = lax.bitwise_xor(section, shift)
+        to = lax.rem(section + shift, SECTIONS)
         packed[shift, B:, :] = jnp.where(upper, zones_x[0, to], zone_y).astype(I16)
         arrival.wait()
         for r in range(0, B, 32):
@@ -205,7 +205,7 @@
     other = pl.ds(pl.multiple_of((1 - core) * H, H), H)
 
     for shift, (q, p) in enumerate(((q0, p0), (q1, p1), (q2, p2), (q3, p3))):
-        level = lax.bitwise_xor(section, shift)
+        level = lax.rem(section + SECTIONS - shift, SECTIONS)
         for r in range(0, B, 32):
             slow[level, r : r + 32, mine] = q[r : r + 32, :].astype(I32).astype(F32)
             slow[level, r : r + 32, other] = p[r : r + 32, :].astype(I32).astype(F32)
@@ -346,7 +346,7 @@
 def merge_kernel(mine, got, own, s1, s2, s3):
     section, _, _ = place()
     for shift, out in enumerate((own, s1, s2, s3)):
-        level = lax.bitwise_xor(section, shift)
+        level = lax.rem(section + shift, SECTIONS)
         out[...] = (mine[level] + got[level].astype(F32)).astype(out.dtype)
 
 
@@ -366,7 +366,7 @@
 def assemble_kernel(own, g1, g2, g3, out):
     section, _, _ = place()
     for shift, block in enumerate((own, g1, g2, g3)):
-        origin = lax.bitwise_xor(section, shift)
+        origin = lax.rem(section + SECTIONS - shift, SECTIONS)
         out[0, pl.ds(pl.multiple_of(origin * B, B), B), :] = block[...].astype(F32)
 
 
@@ -383,7 +383,7 @@
 
 
 def along_depth(block, shift):
-    return lax.ppermute(block, "depth", [(i, i ^ shift) for i in range(SECTIONS)])
+    return lax.ppermute(block, "depth", [(i, (i + shift) % SECTIONS) for i in range(SECTIONS)])
 
 
 def other_core(block):

time: 34 us -> 32.5 us (0.956)
  waiting for transfers between devices: 8.01 us -> 6.45 us
    ppermute x6, waiting for transfers between devices: 5.44 us -> 3.9 us  [along_depth(): lax.ppermute(block, 'depth', [(i, (i + shift) % SECTIONS) for i in range(...]
  transfers between devices with their start and end apart: 12 -> 12, of which waited for: 9 -> 7; matrix products, arithmetic and copies ran while one was open for 0% -> 0% of each run, Pallas kernels for 12% -> 13%
where the time goes in v5:
time: 32.5 us; the launch traced here: 32.3 us
  Pallas kernels  14.8 us (46%)
  starting transfers between devices  10.9 us (34%)
  waiting for transfers between devices  6.45 us (20%)
    ppermute x6, starting transfers between devices, along_depth(): lax.ppermute(block, 'depth', [(i, (i + shift) % SECTIONS) for i in range(...  9.49 us
    pallas_call x1, Pallas kernels, continue_all(): pl.pallas_call(continue_kernel, out_shape=[jax.ShapeDtypeStruct((LEVELS,...  7.33 us
    ppermute x6, waiting for transfers between devices, along_depth(): lax.ppermute(block, 'depth', [(i, (i + shift) % SECTIONS) for i in range(...  3.9 us
    ppermute x6, waiting for transfers between devices, other_core(): return lax.ppermute(block, 'xline', [(i, i ^ 1) for i in range(count)])  2.55 us
    pallas_call x1, Pallas kernels, pack(): pl.pallas_call(pack_kernel, out_shape=[jax.ShapeDtypeStruct((B + EXTRA, H...  2.5 us
    pallas_call x1, Pallas kernels, starting_fields(): pl.pallas_call(fields_kernel, out_shape=[part, part, field], in_specs=[hb...  2.28 us
    pallas_call x1, Pallas kernels, prepare(): pl.pallas_call(prepare_kernel, out_shape=jax.ShapeDtypeStruct((MINE, zone...  1.78 us
    ppermute x6, starting transfers between devices, other_core(): return lax.ppermute(block, 'xline', [(i, i ^ 1) for i in range(count)])  1.42 us
  transfers between devices with their start and end apart: 12, of which 7 were waited for; matrix products, arithmetic and copies ran while one was open for 0% of the time, Pallas kernels for 13%

profile of v5, /device:TPU:0, one launch (start us, length us, event | category | flops | bytes accessed | tf_op | source)
XLA Modules:
  0.0 32.3 jit_solution(12050896178743470469)
XLA Ops:
  0.0 2.5 %pack.1 = (s16[272,128]{1,0:T(8,128)(2,1)}, s16[272,128]{1,0:T(8,128)(2,1)}, s16[272,128]{1,0:T(8,128)(2,1)}, s16[272,128]{1,0:T(8,128)(2,1)}) custom-call(f32[1,1024,128]{2,1,0:T(8,128)} %slow.1, s32[1,4]{1,0:T(1,128)} %zones_x.1, s32[1,16]{1,0:T(1,128)} %zones_y.1), custom_call_target="tpu_custom_call" | custom-call | tf_op jit(solution)/shard_map/pack/pallas_call | solution.py:74
  2.5 1.7 %collective-permute-start = (s16[272,128]{1,0:T(8,128)(2,1)}, s16[272,128]{1,0:T(8,128)(2,1)S(1)}, u32[]{:S(2)}, u32[]{:S(2)}) collective-permute-start(s16[272,128]{1,0:T(8,128)(2,1)} %get-tuple-element.30), channel_id=1, source_target_pairs={{0,32},{32,64},{64,96},{96,0},{1,33},{33,65},{65,97},{97,1},{2,34}... | collective-permute-start | bytes 208904 | tf_op jit(solution)/shard_map/ppermute | solution.py:386
  4.2 2.9 %collective-permute-start.1 = (s16[272,128]{1,0:T(8,128)(2,1)}, s16[272,128]{1,0:T(8,128)(2,1)S(1)}, u32[]{:S(2)}, u32[]{:S(2)}) collective-permute-start(s16[272,128]{1,0:T(8,128)(2,1)} %get-tuple-element.31), channel_id=1, source_target_pairs={{0,64},{32,96},{64,0},{96,32},{1,65},{33,97},{65,1},{97,33},{2,66}... | collective-permute-start | bytes 208904 | tf_op jit(solution)/shard_map/ppermute | solution.py:386
  7.1 1.3 %collective-permute-start.2 = (s16[272,128]{1,0:T(8,128)(2,1)}, s16[272,128]{1,0:T(8,128)(2,1)S(1)}, u32[]{:S(2)}, u32[]{:S(2)}) collective-permute-start(s16[272,128]{1,0:T(8,128)(2,1)} %get-tuple-element.32), channel_id=1, source_target_pairs={{0,96},{32,0},{64,32},{96,64},{1,97},{33,1},{65,33},{97,65},{2,98}... | collective-permute-start | bytes 208904 | tf_op jit(solution)/shard_map/ppermute | solution.py:386
  8.5 2.3 %starting_fields.1 = (bf16[2,2,256,128]{3,2,1,0:T(8,128)(2,1)}, bf16[2,2,256,128]{3,2,1,0:T(8,128)(2,1)}, bf16[2,256,512]{2,1,0:T(8,128)(2,1)}) custom-call(bf16[4,2,1024,128]{3,2,1,0:T(8,128)(2,1)} %receiver.1, bf16[4,2,256]{2,1,0:T(2,128)(2,1)} %amp_hbm.1, s32[1,256]{1,0:T(1,128)} %bitcast.2, s32[1,256]{1,0:T(1,128)} %bitcast.3, ...), custom_call_target="tpu_custom_call" | custom-call | flops 134217728 | bytes 3145728 | tf_op jit(solution)/shard_map/starting_fields/pallas_call | solution.py:140
  10.8 0.0 copy-start.1
  10.8 0.0 copy-start.3
  10.8 1.8 %prepare.1.operators = bf16[2,4,512,512]{3,2,1,0:T(8,128)(2,1)S(1)} custom-call(bf16[4,4,2,256,256]{4,3,2,1,0:T(8,128)(2,1)} %inverses), custom_call_target="tpu_custom_call" | custom-call | bytes 6291456 | tf_op jit(solution)/shard_map/prepare/pallas_call | solution.py:181
  12.6 0.0 collective-permute-done.q1
  12.6 0.0 collective-permute-done.1.q2
  12.6 0.0 collective-permute-done.2.q3
  12.7 0.1 collective-permute-start.3
  12.8 0.5 %collective-permute-start.4 = (s16[272,128]{1,0:T(8,128)(2,1)S(1)}, s16[272,128]{1,0:T(8,128)(2,1)S(1)}, u32[]{:S(2)}, u32[]{:S(2)}) collective-permute-start(s16[272,128]{1,0:T(8,128)(2,1)S(1)} %copy-done), channel_id=1, source_target_pairs={{0,1},{1,0},{2,3},{3,2},{4,5},{5,4},{6,7},{7,6},{8,9},{9,8},{10,11... | collective-permute-start | bytes 208904 | tf_op jit(solution)/shard_map/ppermute | solution.py:391
  13.3 0.1 collective-permute-start.5
  13.4 0.4 %collective-permute-start.6 = (s16[272,128]{1,0:T(8,128)(2,1)S(1)}, s16[272,128]{1,0:T(8,128)(2,1)S(1)}, u32[]{:S(2)}, u32[]{:S(2)}) collective-permute-start(s16[272,128]{1,0:T(8,128)(2,1)S(1)} %collective-permute-done.1.q2), channel_id=1, source_target_pairs={{0,1},{1,0},{2,3},{3,2},{4,5},{5,4},{6,7},{7,6},{8,9},{9,8},{10,11... | collective-permute-start | bytes 208904 | tf_op jit(solution)/shard_map/ppermute | solution.py:391
  13.8 0.1 collective-permute-start.7
  13.9 0.5 %collective-permute-done.4.p0 = s16[272,128]{1,0:T(8,128)(2,1)S(1)} collective-permute-done((s16[272,128]{1,0:T(8,128)(2,1)S(1)}, s16[272,128]{1,0:T(8,128)(2,1)S(1)}, u32[]{:S(2)}, u32[]{:S(2)}) %collective-permute-start.4) | collective-permute-done | bytes 69664 | tf_op jit(solution)/shard_map/ppermute | solution.py:391
  14.4 0.1 collective-permute-done.5.p1
  14.5 0.2 collective-permute-done.6.p2
  14.7 0.4 %collective-permute-done.7.p3 = s16[272,128]{1,0:T(8,128)(2,1)S(1)} collective-permute-done((s16[272,128]{1,0:T(8,128)(2,1)S(1)}, s16[272,128]{1,0:T(8,128)(2,1)S(1)}, u32[]{:S(2)}, u32[]{:S(2)}) %collective-permute-start.7) | collective-permute-done | bytes 69664 | tf_op jit(solution)/shard_map/ppermute | solution.py:391
  15.0 0.0 collective-permute-done.3.rec_other
  15.1 7.3 %continue_levels.1 = (f32[4,256,128]{2,1,0:T(8,128)S(1)}, bf16[4,256,128]{2,1,0:T(8,128)(2,1)S(1)}) custom-call(f32[4]{0:T(128)S(1)} %copy-done.3, bf16[2,256,512]{2,1,0:T(8,128)(2,1)S(1)} %copy-done.1, bf16[2,4,512,512]{3,2,1,0:T(8,128)(2,1)S(1)} %prepare.1.operators, bf16[2,2,256,128]{3,2,1,0:T(8,128)(2,1)S(1)} %copy-done.2, ...), custom_call_target="tpu_custom_call" | custom-call | flops 4294967296 | bytes 8388608 | tf_op jit(solution)/shard_map/continue_levels/pallas_call | solution.py:324
  22.4 0.2 collective-permute-start.8
  22.6 1.4 %collective-permute-done.8.got = bf16[4,256,128]{2,1,0:T(8,128)(2,1)S(1)} collective-permute-done((bf16[4,256,128]{2,1,0:T(8,128)(2,1)S(1)}, bf16[4,256,128]{2,1,0:T(8,128)(2,1)S(1)}, u32[]{:S(2)}, u32[]{:S(2)}) %collective-permute-start.8) | collective-permute-done | bytes 262176 | tf_op jit(solution)/shard_map/ppermute | solution.py:391
  24.0 0.1 merge.1
  24.1 0.7 %collective-permute-start.9 = (bf16[256,128]{1,0:T(8,128)(2,1)S(1)}, bf16[256,128]{1,0:T(8,128)(2,1)S(1)}, u32[]{:S(2)}, u32[]{:S(2)}) collective-permute-start(bf16[256,128]{1,0:T(8,128)(2,1)S(1)} %get-tuple-element.42), channel_id=1, source_target_pairs={{0,32},{32,64},{64,96},{96,0},{1,33},{33,65},{65,97},{97,1},{2,34}... | collective-permute-start | bytes 196616 | tf_op jit(solution)/shard_map/ppermute | solution.py:386
  24.8 2.3 %collective-permute-start.10 = (bf16[256,128]{1,0:T(8,128)(2,1)S(1)}, bf16[256,128]{1,0:T(8,128)(2,1)S(1)}, u32[]{:S(2)}, u32[]{:S(2)}) collective-permute-start(bf16[256,128]{1,0:T(8,128)(2,1)S(1)} %get-tuple-element.43), channel_id=1, source_target_pairs={{0,64},{32,96},{64,0},{96,32},{1,65},{33,97},{65,1},{97,33},{2,66}... | collective-permute-start | bytes 196616 | tf_op jit(solution)/shard_map/ppermute | solution.py:386
  27.1 0.5 %collective-permute-start.11 = (bf16[256,128]{1,0:T(8,128)(2,1)S(1)}, bf16[256,128]{1,0:T(8,128)(2,1)S(1)}, u32[]{:S(2)}, u32[]{:S(2)}) collective-permute-start(bf16[256,128]{1,0:T(8,128)(2,1)S(1)} %get-tuple-element.44), channel_id=1, source_target_pairs={{0,96},{32,0},{64,32},{96,64},{1,97},{33,1},{65,33},{97,65},{2,98}... | collective-permute-start | bytes 196616 | tf_op jit(solution)/shard_map/ppermute | solution.py:386
  27.6 3.4 %collective-permute-done.9.g1 = bf16[256,128]{1,0:T(8,128)(2,1)S(1)} collective-permute-done((bf16[256,128]{1,0:T(8,128)(2,1)S(1)}, bf16[256,128]{1,0:T(8,128)(2,1)S(1)}, u32[]{:S(2)}, u32[]{:S(2)}) %collective-permute-start.9) | collective-permute-done | bytes 65568 | tf_op jit(solution)/shard_map/ppermute | solution.py:386
  31.0 0.0 collective-permute-done.10.g2
  31.0 0.5 %collective-permute-done.11.g3 = bf16[256,128]{1,0:T(8,128)(2,1)S(1)} collective-permute-done((bf16[256,128]{1,0:T(8,128)(2,1)S(1)}, bf16[256,128]{1,0:T(8,128)(2,1)S(1)}, u32[]{:S(2)}, u32[]{:S(2)}) %collective-permute-start.11) | collective-permute-done | bytes 65568 | tf_op jit(solution)/shard_map/ppermute | solution.py:386
  31.5 0.8 %assemble.1 = f32[1,1024,128]{2,1,0:T(8,128)} custom-call(f32[256,128]{1,0:T(8,128)S(1)} %get-tuple-element.41.own, bf16[256,128]{1,0:T(8,128)(2,1)S(1)} %collective-permute-done.9.g1, bf16[256,128]{1,0:T(8,128)(2,1)S(1)} %collective-permute-done.10.g2, bf16[256,128]{1,0:T(8,128)(2,1)S(1)} %collective-permute-done.11.g3), custom_call_target="tpu_custom_call" | custom-call | tf_op jit(solution)/shard_map/assemble/pallas_call | solution.py:375
  (8 shorter events, 0.0 us)
Async XLA Ops:
  2.5 10.1 %collective-permute-start = (s16[272,128]{1,0:T(8,128)(2,1)}, s16[272,128]{1,0:T(8,128)(2,1)S(1)}, u32[]{:S(2)}, u32[]{:S(2)}) collective-permute-start(s16[272,128]{1,0:T(8,128)(2,1)} %get-tuple-element.30), channel_id=1, source_target_pairs={{0,32},{32,64},{64,96},{96,0},{1,33},{33,65},{65,97},{97,1},{2,34}... | collective-permute-start | bytes 208904 | tf_op jit(solution)/shard_map/ppermute | solution.py:386
  4.2 8.4 %collective-permute-start.1 = (s16[272,128]{1,0:T(8,128)(2,1)}, s16[272,128]{1,0:T(8,128)(2,1)S(1)}, u32[]{:S(2)}, u32[]{:S(2)}) collective-permute-start(s16[272,128]{1,0:T(8,128)(2,1)} %get-tuple-element.31), channel_id=1, source_target_pairs={{0,64},{32,96},{64,0},{96,32},{1,65},{33,97},{65,1},{97,33},{2,66}... | collective-permute-start | bytes 208904 | tf_op jit(solution)/shard_map/ppermute | solution.py:386
  7.1 5.5 %collective-permute-start.2 = (s16[272,128]{1,0:T(8,128)(2,1)}, s16[272,128]{1,0:T(8,128)(2,1)S(1)}, u32[]{:S(2)}, u32[]{:S(2)}) collective-permute-start(s16[272,128]{1,0:T(8,128)(2,1)} %get-tuple-element.32), channel_id=1, source_target_pairs={{0,96},{32,0},{64,32},{96,64},{1,97},{33,1},{65,33},{97,65},{2,98}... | collective-permute-start | bytes 208904 | tf_op jit(solution)/shard_map/ppermute | solution.py:386
  10.8 1.9 %copy-start.4 = (bf16[2,2,256,128]{3,2,1,0:T(8,128)(2,1)S(1)}, bf16[2,2,256,128]{3,2,1,0:T(8,128)(2,1)}, u32[]{:S(2)}) copy-start(bf16[2,2,256,128]{3,2,1,0:T(8,128)(2,1)} %get-tuple-element.35) | copy-start | bytes 786436
  10.8 2.0 %copy-start = (s16[272,128]{1,0:T(8,128)(2,1)S(1)}, s16[272,128]{1,0:T(8,128)(2,1)}, u32[]{:S(2)}) copy-start(s16[272,128]{1,0:T(8,128)(2,1)} %get-tuple-element.25._.q0) | copy-start | bytes 208900
  10.8 4.2 %copy-start.1 = (bf16[2,256,512]{2,1,0:T(8,128)(2,1)S(1)}, bf16[2,256,512]{2,1,0:T(8,128)(2,1)}, u32[]{:S(2)}) copy-start(bf16[2,256,512]{2,1,0:T(8,128)(2,1)} %get-tuple-element.27.sources) | copy-start | bytes 1572868
  10.8 4.2 %copy-start.2 = (bf16[2,2,256,128]{3,2,1,0:T(8,128)(2,1)S(1)}, bf16[2,2,256,128]{3,2,1,0:T(8,128)(2,1)}, u32[]{:S(2)}) copy-start(bf16[2,2,256,128]{3,2,1,0:T(8,128)(2,1)} %get-tuple-element.34.rec_mine) | copy-start | bytes 786436
  10.8 4.2 %copy-start.3 = (f32[4]{0:T(128)S(1)}, f32[4]{0:T(128)}, u32[]{:S(2)}) copy-start(f32[4]{0:T(128)} %omegas.1) | copy-start | bytes 52
  12.7 2.4 %collective-permute-start.3 = (bf16[2,2,256,128]{3,2,1,0:T(8,128)(2,1)S(1)}, bf16[2,2,256,128]{3,2,1,0:T(8,128)(2,1)S(1)}, u32[]{:S(2)}, u32[]{:S(2)}) collective-permute-start(bf16[2,2,256,128]{3,2,1,0:T(8,128)(2,1)S(1)} %copy-done.4), channel_id=1, source_target_pairs={{0,1},{1,0},{2,3},{3,2},{4,5},{5,4},{6,7},{7,6},{8,9},{9,8},{10,11... | collective-permute-start | bytes 786440 | tf_op jit(solution)/shard_map/ppermute | solution.py:391
  12.8 1.6 %collective-permute-start.4 = (s16[272,128]{1,0:T(8,128)(2,1)S(1)}, s16[272,128]{1,0:T(8,128)(2,1)S(1)}, u32[]{:S(2)}, u32[]{:S(2)}) collective-permute-start(s16[272,128]{1,0:T(8,128)(2,1)S(1)} %copy-done), channel_id=1, source_target_pairs={{0,1},{1,0},{2,3},{3,2},{4,5},{5,4},{6,7},{7,6},{8,9},{9,8},{10,11... | collective-permute-start | bytes 208904 | tf_op jit(solution)/shard_map/ppermute | solution.py:391
  13.3 1.3 %collective-permute-start.5 = (s16[272,128]{1,0:T(8,128)(2,1)S(1)}, s16[272,128]{1,0:T(8,128)(2,1)S(1)}, u32[]{:S(2)}, u32[]{:S(2)}) collective-permute-start(s16[272,128]{1,0:T(8,128)(2,1)S(1)} %collective-permute-done.q1), channel_id=1, source_target_pairs={{0,1},{1,0},{2,3},{3,2},{4,5},{5,4},{6,7},{7,6},{8,9},{9,8},{10,11... | collective-permute-start | bytes 208904 | tf_op jit(solution)/shard_map/ppermute | solution.py:391
  13.4 1.3 %collective-permute-start.6 = (s16[272,128]{1,0:T(8,128)(2,1)S(1)}, s16[272,128]{1,0:T(8,128)(2,1)S(1)}, u32[]{:S(2)}, u32[]{:S(2)}) collective-permute-start(s16[272,128]{1,0:T(8,128)(2,1)S(1)} %collective-permute-done.1.q2), channel_id=1, source_target_pairs={{0,1},{1,0},{2,3},{3,2},{4,5},{5,4},{6,7},{7,6},{8,9},{9,8},{10,11... | collective-permute-start | bytes 208904 | tf_op jit(solution)/shard_map/ppermute | solution.py:391
  13.8 1.3 %collective-permute-start.7 = (s16[272,128]{1,0:T(8,128)(2,1)S(1)}, s16[272,128]{1,0:T(8,128)(2,1)S(1)}, u32[]{:S(2)}, u32[]{:S(2)}) collective-permute-start(s16[272,128]{1,0:T(8,128)(2,1)S(1)} %collective-permute-done.2.q3), channel_id=1, source_target_pairs={{0,1},{1,0},{2,3},{3,2},{4,5},{5,4},{6,7},{7,6},{8,9},{9,8},{10,11... | collective-permute-start | bytes 208904 | tf_op jit(solution)/shard_map/ppermute | solution.py:391
  22.4 1.6 %collective-permute-start.8 = (bf16[4,256,128]{2,1,0:T(8,128)(2,1)S(1)}, bf16[4,256,128]{2,1,0:T(8,128)(2,1)S(1)}, u32[]{:S(2)}, u32[]{:S(2)}) collective-permute-start(bf16[4,256,128]{2,1,0:T(8,128)(2,1)S(1)} %get-tuple-element.40), channel_id=1, source_target_pairs={{0,1},{1,0},{2,3},{3,2},{4,5},{5,4},{6,7},{7,6},{8,9},{9,8},{10,11... | collective-permute-start | bytes 786440 | tf_op jit(solution)/shard_map/ppermute | solution.py:391
  24.1 6.9 %collective-permute-start.9 = (bf16[256,128]{1,0:T(8,128)(2,1)S(1)}, bf16[256,128]{1,0:T(8,128)(2,1)S(1)}, u32[]{:S(2)}, u32[]{:S(2)}) collective-permute-start(bf16[256,128]{1,0:T(8,128)(2,1)S(1)} %get-tuple-element.42), channel_id=1, source_target_pairs={{0,32},{32,64},{64,96},{96,0},{1,33},{33,65},{65,97},{97,1},{2,34}... | collective-permute-start | bytes 196616 | tf_op jit(solution)/shard_map/ppermute | solution.py:386
  24.8 6.1 %collective-permute-start.10 = (bf16[256,128]{1,0:T(8,128)(2,1)S(1)}, bf16[256,128]{1,0:T(8,128)(2,1)S(1)}, u32[]{:S(2)}, u32[]{:S(2)}) collective-permute-start(bf16[256,128]{1,0:T(8,128)(2,1)S(1)} %get-tuple-element.43), channel_id=1, source_target_pairs={{0,64},{32,96},{64,0},{96,32},{1,65},{33,97},{65,1},{97,33},{2,66}... | collective-permute-start | bytes 196616 | tf_op jit(solution)/shard_map/ppermute | solution.py:386
  27.1 4.4 %collective-permute-start.11 = (bf16[256,128]{1,0:T(8,128)(2,1)S(1)}, bf16[256,128]{1,0:T(8,128)(2,1)S(1)}, u32[]{:S(2)}, u32[]{:S(2)}) collective-permute-start(bf16[256,128]{1,0:T(8,128)(2,1)S(1)} %get-tuple-element.44), channel_id=1, source_target_pairs={{0,96},{32,0},{64,32},{96,64},{1,97},{33,1},{65,33},{97,65},{2,98}... | collective-permute-start | bytes 196616 | tf_op jit(solution)/shard_map/ppermute | solution.py:386

commit v6 on v5

--- a/solution.py
+++ b/solution.py
@@ -400,11 +400,9 @@
         receiver_data, source_amp, source_x.reshape(1, -1), source_y.reshape(1, -1), blocks[0]
     )
     own_other = other_core(blocks[0])
-    inverses, sources = lax.optimization_barrier((inverses, sources))
-    operators, rec_send, *moved = lax.optimization_barrier(
-        (prepare(inverses), rec_send, *moved)
-    )
+    inverses, rec_send, *moved = lax.optimization_barrier((inverses, rec_send, *moved))
     rec_other = other_core(rec_send)
+    operators = prepare(inverses)
     mine = [blocks[0], *moved]
     other = [own_other] + [other_core(block) for block in moved]
     grad_mine, grad_other = continue_all(

time: 32.5 us -> 33.1 us (1.018)
  starting transfers between devices: 10.9 us -> 12 us
  waiting for transfers between devices: 6.45 us -> 6.08 us
    ppermute x6, waiting for transfers between devices: 2.55 us -> 1.18 us  [other_core(): return lax.ppermute(block, 'xline', [(i, i ^ 1) for i in range(count)])]
    ppermute x6, waiting for transfers between devices: 3.9 us -> 4.91 us  [along_depth(): lax.ppermute(block, 'depth', [(i, (i + shift) % SECTIONS) for i in range(...]
    ppermute x6, starting transfers between devices: 9.49 us -> 10.3 us  [along_depth(): lax.ppermute(block, 'depth', [(i, (i + shift) % SECTIONS) for i in range(...]
  transfers between devices with their start and end apart: 12 -> 12, of which waited for: 7 -> 5; matrix products, arithmetic and copies ran while one was open for 0% -> 0% of each run, Pallas kernels for 13% -> 12%
where the time goes in v6:
time: 33.1 us; the launch traced here: 32.9 us
  Pallas kernels  14.7 us (44%)
  starting transfers between devices  12 us (36%)
  waiting for transfers between devices  6.08 us (18%)
    ppermute x6, starting transfers between devices, along_depth(): lax.ppermute(block, 'depth', [(i, (i + shift) % SECTIONS) for i in range(...  10.3 us
    pallas_call x1, Pallas kernels, continue_all(): pl.pallas_call(continue_kernel, out_shape=[jax.ShapeDtypeStruct((LEVELS,...  7.32 us
    ppermute x6, waiting for transfers between devices, along_depth(): lax.ppermute(block, 'depth', [(i, (i + shift) % SECTIONS) for i in range(...  4.91 us
    pallas_call x1, Pallas kernels, pack(): pl.pallas_call(pack_kernel, out_shape=[jax.ShapeDtypeStruct((B + EXTRA, H...  2.5 us
    pallas_call x1, Pallas kernels, starting_fields(): pl.pallas_call(fields_kernel, out_shape=[part, part, field], in_specs=[hb...  2.28 us
    pallas_call x1, Pallas kernels, prepare(): pl.pallas_call(prepare_kernel, out_shape=jax.ShapeDtypeStruct((MINE, zone...  1.69 us
    ppermute x6, starting transfers between devices, other_core(): return lax.ppermute(block, 'xline', [(i, i ^ 1) for i in range(count)])  1.69 us
    ppermute x6, waiting for transfers between devices, other_core(): return lax.ppermute(block, 'xline', [(i, i ^ 1) for i in range(count)])  1.18 us
  transfers between devices with their start and end apart: 12, of which 5 were waited for; matrix products, arithmetic and copies ran while one was open for 0% of the time, Pallas kernels for 12%

profile of v6, /device:TPU:0, one launch (start us, length us, event | category | flops | bytes accessed | tf_op | source)
XLA Modules:
  0.0 32.9 jit_solution(11840799204842734203)
XLA Ops:
  0.0 2.5 %pack.1 = (s16[272,128]{1,0:T(8,128)(2,1)}, s16[272,128]{1,0:T(8,128)(2,1)}, s16[272,128]{1,0:T(8,128)(2,1)}, s16[272,128]{1,0:T(8,128)(2,1)}) custom-call(f32[1,1024,128]{2,1,0:T(8,128)} %slow.1, s32[1,4]{1,0:T(1,128)} %zones_x.1, s32[1,16]{1,0:T(1,128)} %zones_y.1), custom_call_target="tpu_custom_call" | custom-call | tf_op jit(solution)/shard_map/pack/pallas_call | solution.py:74
  2.5 1.7 %collective-permute-start = (s16[272,128]{1,0:T(8,128)(2,1)}, s16[272,128]{1,0:T(8,128)(2,1)S(1)}, u32[]{:S(2)}, u32[]{:S(2)}) collective-permute-start(s16[272,128]{1,0:T(8,128)(2,1)} %get-tuple-element.26), channel_id=1, source_target_pairs={{0,32},{32,64},{64,96},{96,0},{1,33},{33,65},{65,97},{97,1},{2,34}... | collective-permute-start | bytes 208904 | tf_op jit(solution)/shard_map/ppermute | solution.py:386
  4.2 2.9 %collective-permute-start.1 = (s16[272,128]{1,0:T(8,128)(2,1)}, s16[272,128]{1,0:T(8,128)(2,1)S(1)}, u32[]{:S(2)}, u32[]{:S(2)}) collective-permute-start(s16[272,128]{1,0:T(8,128)(2,1)} %get-tuple-element.27), channel_id=1, source_target_pairs={{0,64},{32,96},{64,0},{96,32},{1,65},{33,97},{65,1},{97,33},{2,66}... | collective-permute-start | bytes 208904 | tf_op jit(solution)/shard_map/ppermute | solution.py:386
  7.1 1.3 %collective-permute-start.2 = (s16[272,128]{1,0:T(8,128)(2,1)}, s16[272,128]{1,0:T(8,128)(2,1)S(1)}, u32[]{:S(2)}, u32[]{:S(2)}) collective-permute-start(s16[272,128]{1,0:T(8,128)(2,1)} %get-tuple-element.28), channel_id=1, source_target_pairs={{0,96},{32,0},{64,32},{96,64},{1,97},{33,1},{65,33},{97,65},{2,98}... | collective-permute-start | bytes 208904 | tf_op jit(solution)/shard_map/ppermute | solution.py:386
  8.5 2.3 %starting_fields.1 = (bf16[2,2,256,128]{3,2,1,0:T(8,128)(2,1)}, bf16[2,2,256,128]{3,2,1,0:T(8,128)(2,1)}, bf16[2,256,512]{2,1,0:T(8,128)(2,1)}) custom-call(bf16[4,2,1024,128]{3,2,1,0:T(8,128)(2,1)} %receiver.1, bf16[4,2,256]{2,1,0:T(2,128)(2,1)} %amp_hbm.1, s32[1,256]{1,0:T(1,128)} %bitcast.2, s32[1,256]{1,0:T(1,128)} %bitcast.3, ...), custom_call_target="tpu_custom_call" | custom-call | flops 134217728 | bytes 3145728 | tf_op jit(solution)/shard_map/starting_fields/pallas_call | solution.py:140
  10.8 0.0 collective-permute-done.q1
  10.8 0.0 collective-permute-done.1.q2
  10.8 0.9 %collective-permute-done.2.q3 = s16[272,128]{1,0:T(8,128)(2,1)S(1)} collective-permute-done((s16[272,128]{1,0:T(8,128)(2,1)}, s16[272,128]{1,0:T(8,128)(2,1)S(1)}, u32[]{:S(2)}, u32[]{:S(2)}) %collective-permute-start.2) | collective-permute-done | bytes 69664 | tf_op jit(solution)/shard_map/ppermute | solution.py:386
  11.7 0.1 collective-permute-start.3
  11.8 0.5 %collective-permute-start.4 = (s16[272,128]{1,0:T(8,128)(2,1)}, s16[272,128]{1,0:T(8,128)(2,1)S(1)}, u32[]{:S(2)}, u32[]{:S(2)}) collective-permute-start(s16[272,128]{1,0:T(8,128)(2,1)} %get-tuple-element.23._.q0), channel_id=1, source_target_pairs={{0,1},{1,0},{2,3},{3,2},{4,5},{5,4},{6,7},{7,6},{8,9},{9,8},{10,11... | collective-permute-start | bytes 208904 | tf_op jit(solution)/shard_map/ppermute | solution.py:391
  12.3 0.1 collective-permute-start.5
  12.4 0.4 %collective-permute-start.6 = (s16[272,128]{1,0:T(8,128)(2,1)S(1)}, s16[272,128]{1,0:T(8,128)(2,1)S(1)}, u32[]{:S(2)}, u32[]{:S(2)}) collective-permute-start(s16[272,128]{1,0:T(8,128)(2,1)S(1)} %collective-permute-done.1.q2), channel_id=1, source_target_pairs={{0,1},{1,0},{2,3},{3,2},{4,5},{5,4},{6,7},{7,6},{8,9},{9,8},{10,11... | collective-permute-start | bytes 208904 | tf_op jit(solution)/shard_map/ppermute | solution.py:391
  12.8 0.1 collective-permute-start.7
  12.9 1.7 %prepare.1.operators = bf16[2,4,512,512]{3,2,1,0:T(8,128)(2,1)S(1)} custom-call(bf16[4,4,2,256,256]{4,3,2,1,0:T(8,128)(2,1)} %inverses), custom_call_target="tpu_custom_call" | custom-call | bytes 6291456 | tf_op jit(solution)/shard_map/prepare/pallas_call | solution.py:181
  14.6 0.0 collective-permute-done.4.p0
  14.6 0.0 collective-permute-done.5.p1
  14.6 0.0 collective-permute-done.6.p2
  14.6 0.0 collective-permute-done.7.p3
  14.6 0.0 collective-permute-done.3.rec_other
  14.6 0.0 copy-done
  14.6 0.0 copy-done.1
  14.7 7.3 %continue_levels.1 = (f32[4,256,128]{2,1,0:T(8,128)S(1)}, bf16[4,256,128]{2,1,0:T(8,128)(2,1)S(1)}) custom-call(f32[4]{0:T(128)S(1)} %copy-done.3, bf16[2,256,512]{2,1,0:T(8,128)(2,1)S(1)} %copy-done.1, bf16[2,4,512,512]{3,2,1,0:T(8,128)(2,1)S(1)} %prepare.1.operators, bf16[2,2,256,128]{3,2,1,0:T(8,128)(2,1)S(1)} %copy-done.2, ...), custom_call_target="tpu_custom_call" | custom-call | flops 4294967296 | bytes 8388608 | tf_op jit(solution)/shard_map/continue_levels/pallas_call | solution.py:324
  22.0 0.5 %collective-permute-start.8 = (bf16[4,256,128]{2,1,0:T(8,128)(2,1)S(1)}, bf16[4,256,128]{2,1,0:T(8,128)(2,1)S(1)}, u32[]{:S(2)}, u32[]{:S(2)}) collective-permute-start(bf16[4,256,128]{2,1,0:T(8,128)(2,1)S(1)} %get-tuple-element.36), channel_id=1, source_target_pairs={{0,1},{1,0},{2,3},{3,2},{4,5},{5,4},{6,7},{7,6},{8,9},{9,8},{10,11... | collective-permute-start | bytes 786440 | tf_op jit(solution)/shard_map/ppermute | solution.py:391
  22.5 1.2 %collective-permute-done.8.got = bf16[4,256,128]{2,1,0:T(8,128)(2,1)S(1)} collective-permute-done((bf16[4,256,128]{2,1,0:T(8,128)(2,1)S(1)}, bf16[4,256,128]{2,1,0:T(8,128)(2,1)S(1)}, u32[]{:S(2)}, u32[]{:S(2)}) %collective-permute-start.8) | collective-permute-done | bytes 262176 | tf_op jit(solution)/shard_map/ppermute | solution.py:391
  23.7 0.1 merge.1
  23.7 0.4 %collective-permute-start.9 = (bf16[256,128]{1,0:T(8,128)(2,1)S(1)}, bf16[256,128]{1,0:T(8,128)(2,1)S(1)}, u32[]{:S(2)}, u32[]{:S(2)}) collective-permute-start(bf16[256,128]{1,0:T(8,128)(2,1)S(1)} %get-tuple-element.38), channel_id=1, source_target_pairs={{0,32},{32,64},{64,96},{96,0},{1,33},{33,65},{65,97},{97,1},{2,34}... | collective-permute-start | bytes 196616 | tf_op jit(solution)/shard_map/ppermute | solution.py:386
  24.1 3.7 %collective-permute-start.10 = (bf16[256,128]{1,0:T(8,128)(2,1)S(1)}, bf16[256,128]{1,0:T(8,128)(2,1)S(1)}, u32[]{:S(2)}, u32[]{:S(2)}) collective-permute-start(bf16[256,128]{1,0:T(8,128)(2,1)S(1)} %get-tuple-element.39), channel_id=1, source_target_pairs={{0,64},{32,96},{64,0},{96,32},{1,65},{33,97},{65,1},{97,33},{2,66}... | collective-permute-start | bytes 196616 | tf_op jit(solution)/shard_map/ppermute | solution.py:386
  27.8 0.2 collective-permute-start.11
  28.0 1.3 %collective-permute-done.9.g1 = bf16[256,128]{1,0:T(8,128)(2,1)S(1)} collective-permute-done((bf16[256,128]{1,0:T(8,128)(2,1)S(1)}, bf16[256,128]{1,0:T(8,128)(2,1)S(1)}, u32[]{:S(2)}, u32[]{:S(2)}) %collective-permute-start.9) | collective-permute-done | bytes 65568 | tf_op jit(solution)/shard_map/ppermute | solution.py:386
  29.4 2.2 %collective-permute-done.10.g2 = bf16[256,128]{1,0:T(8,128)(2,1)S(1)} collective-permute-done((bf16[256,128]{1,0:T(8,128)(2,1)S(1)}, bf16[256,128]{1,0:T(8,128)(2,1)S(1)}, u32[]{:S(2)}, u32[]{:S(2)}) %collective-permute-start.10) | collective-permute-done | bytes 65568 | tf_op jit(solution)/shard_map/ppermute | solution.py:386
  31.6 0.5 %collective-permute-done.11.g3 = bf16[256,128]{1,0:T(8,128)(2,1)S(1)} collective-permute-done((bf16[256,128]{1,0:T(8,128)(2,1)S(1)}, bf16[256,128]{1,0:T(8,128)(2,1)S(1)}, u32[]{:S(2)}, u32[]{:S(2)}) %collective-permute-start.11) | collective-permute-done | bytes 65568 | tf_op jit(solution)/shard_map/ppermute | solution.py:386
  32.1 0.8 %assemble.1 = f32[1,1024,128]{2,1,0:T(8,128)} custom-call(f32[256,128]{1,0:T(8,128)S(1)} %get-tuple-element.37.own, bf16[256,128]{1,0:T(8,128)(2,1)S(1)} %collective-permute-done.9.g1, bf16[256,128]{1,0:T(8,128)(2,1)S(1)} %collective-permute-done.10.g2, bf16[256,128]{1,0:T(8,128)(2,1)S(1)} %collective-permute-done.11.g3), custom_call_target="tpu_custom_call" | custom-call | tf_op jit(solution)/shard_map/assemble/pallas_call | solution.py:375
  (6 shorter events, 0.0 us)
Async XLA Ops:
  2.5 8.3 %collective-permute-start = (s16[272,128]{1,0:T(8,128)(2,1)}, s16[272,128]{1,0:T(8,128)(2,1)S(1)}, u32[]{:S(2)}, u32[]{:S(2)}) collective-permute-start(s16[272,128]{1,0:T(8,128)(2,1)} %get-tuple-element.26), channel_id=1, source_target_pairs={{0,32},{32,64},{64,96},{96,0},{1,33},{33,65},{65,97},{97,1},{2,34}... | collective-permute-start | bytes 208904 | tf_op jit(solution)/shard_map/ppermute | solution.py:386
  4.2 6.6 %collective-permute-start.1 = (s16[272,128]{1,0:T(8,128)(2,1)}, s16[272,128]{1,0:T(8,128)(2,1)S(1)}, u32[]{:S(2)}, u32[]{:S(2)}) collective-permute-start(s16[272,128]{1,0:T(8,128)(2,1)} %get-tuple-element.27), channel_id=1, source_target_pairs={{0,64},{32,96},{64,0},{96,32},{1,65},{33,97},{65,1},{97,33},{2,66}... | collective-permute-start | bytes 208904 | tf_op jit(solution)/shard_map/ppermute | solution.py:386
  7.1 4.5 %collective-permute-start.2 = (s16[272,128]{1,0:T(8,128)(2,1)}, s16[272,128]{1,0:T(8,128)(2,1)S(1)}, u32[]{:S(2)}, u32[]{:S(2)}) collective-permute-start(s16[272,128]{1,0:T(8,128)(2,1)} %get-tuple-element.28), channel_id=1, source_target_pairs={{0,96},{32,0},{64,32},{96,64},{1,97},{33,1},{65,33},{97,65},{2,98}... | collective-permute-start | bytes 208904 | tf_op jit(solution)/shard_map/ppermute | solution.py:386
  11.7 3.0 %copy-start = (s16[272,128]{1,0:T(8,128)(2,1)S(1)}, s16[272,128]{1,0:T(8,128)(2,1)}, u32[]{:S(2)}) copy-start(s16[272,128]{1,0:T(8,128)(2,1)} %get-tuple-element.23._.q0) | copy-start | bytes 208900
  11.7 3.0 %copy-start.1 = (bf16[2,256,512]{2,1,0:T(8,128)(2,1)S(1)}, bf16[2,256,512]{2,1,0:T(8,128)(2,1)}, u32[]{:S(2)}) copy-start(bf16[2,256,512]{2,1,0:T(8,128)(2,1)} %get-tuple-element.24.sources) | copy-start | bytes 1572868
  11.7 3.0 %copy-start.2 = (bf16[2,2,256,128]{3,2,1,0:T(8,128)(2,1)S(1)}, bf16[2,2,256,128]{3,2,1,0:T(8,128)(2,1)}, u32[]{:S(2)}) copy-start(bf16[2,2,256,128]{3,2,1,0:T(8,128)(2,1)} %get-tuple-element.30.rec_mine) | copy-start | bytes 786436
  11.7 3.0 %copy-start.3 = (f32[4]{0:T(128)S(1)}, f32[4]{0:T(128)}, u32[]{:S(2)}) copy-start(f32[4]{0:T(128)} %omegas.1) | copy-start | bytes 52
  11.7 2.9 %collective-permute-start.3 = (bf16[2,2,256,128]{3,2,1,0:T(8,128)(2,1)}, bf16[2,2,256,128]{3,2,1,0:T(8,128)(2,1)S(1)}, u32[]{:S(2)}, u32[]{:S(2)}) collective-permute-start(bf16[2,2,256,128]{3,2,1,0:T(8,128)(2,1)} %get-tuple-element.31), channel_id=1, source_target_pairs={{0,1},{1,0},{2,3},{3,2},{4,5},{5,4},{6,7},{7,6},{8,9},{9,8},{10,11... | collective-permute-start | bytes 786440 | tf_op jit(solution)/shard_map/ppermute | solution.py:391
  11.8 2.8 %collective-permute-start.4 = (s16[272,128]{1,0:T(8,128)(2,1)}, s16[272,128]{1,0:T(8,128)(2,1)S(1)}, u32[]{:S(2)}, u32[]{:S(2)}) collective-permute-start(s16[272,128]{1,0:T(8,128)(2,1)} %get-tuple-element.23._.q0), channel_id=1, source_target_pairs={{0,1},{1,0},{2,3},{3,2},{4,5},{5,4},{6,7},{7,6},{8,9},{9,8},{10,11... | collective-permute-start | bytes 208904 | tf_op jit(solution)/shard_map/ppermute | solution.py:391
  12.3 2.3 %collective-permute-start.5 = (s16[272,128]{1,0:T(8,128)(2,1)S(1)}, s16[272,128]{1,0:T(8,128)(2,1)S(1)}, u32[]{:S(2)}, u32[]{:S(2)}) collective-permute-start(s16[272,128]{1,0:T(8,128)(2,1)S(1)} %collective-permute-done.q1), channel_id=1, source_target_pairs={{0,1},{1,0},{2,3},{3,2},{4,5},{5,4},{6,7},{7,6},{8,9},{9,8},{10,11... | collective-permute-start | bytes 208904 | tf_op jit(solution)/shard_map/ppermute | solution.py:391
  12.4 2.2 %collective-permute-start.6 = (s16[272,128]{1,0:T(8,128)(2,1)S(1)}, s16[272,128]{1,0:T(8,128)(2,1)S(1)}, u32[]{:S(2)}, u32[]{:S(2)}) collective-permute-start(s16[272,128]{1,0:T(8,128)(2,1)S(1)} %collective-permute-done.1.q2), channel_id=1, source_target_pairs={{0,1},{1,0},{2,3},{3,2},{4,5},{5,4},{6,7},{7,6},{8,9},{9,8},{10,11... | collective-permute-start | bytes 208904 | tf_op jit(solution)/shard_map/ppermute | solution.py:391
  12.8 1.8 %collective-permute-start.7 = (s16[272,128]{1,0:T(8,128)(2,1)S(1)}, s16[272,128]{1,0:T(8,128)(2,1)S(1)}, u32[]{:S(2)}, u32[]{:S(2)}) collective-permute-start(s16[272,128]{1,0:T(8,128)(2,1)S(1)} %collective-permute-done.2.q3), channel_id=1, source_target_pairs={{0,1},{1,0},{2,3},{3,2},{4,5},{5,4},{6,7},{7,6},{8,9},{9,8},{10,11... | collective-permute-start | bytes 208904 | tf_op jit(solution)/shard_map/ppermute | solution.py:391
  22.0 1.7 %collective-permute-start.8 = (bf16[4,256,128]{2,1,0:T(8,128)(2,1)S(1)}, bf16[4,256,128]{2,1,0:T(8,128)(2,1)S(1)}, u32[]{:S(2)}, u32[]{:S(2)}) collective-permute-start(bf16[4,256,128]{2,1,0:T(8,128)(2,1)S(1)} %get-tuple-element.36), channel_id=1, source_target_pairs={{0,1},{1,0},{2,3},{3,2},{4,5},{5,4},{6,7},{7,6},{8,9},{9,8},{10,11... | collective-permute-start | bytes 786440 | tf_op jit(solution)/shard_map/ppermute | solution.py:391
  23.7 5.7 %collective-permute-start.9 = (bf16[256,128]{1,0:T(8,128)(2,1)S(1)}, bf16[256,128]{1,0:T(8,128)(2,1)S(1)}, u32[]{:S(2)}, u32[]{:S(2)}) collective-permute-start(bf16[256,128]{1,0:T(8,128)(2,1)S(1)} %get-tuple-element.38), channel_id=1, source_target_pairs={{0,32},{32,64},{64,96},{96,0},{1,33},{33,65},{65,97},{97,1},{2,34}... | collective-permute-start | bytes 196616 | tf_op jit(solution)/shard_map/ppermute | solution.py:386
  24.1 7.4 %collective-permute-start.10 = (bf16[256,128]{1,0:T(8,128)(2,1)S(1)}, bf16[256,128]{1,0:T(8,128)(2,1)S(1)}, u32[]{:S(2)}, u32[]{:S(2)}) collective-permute-start(bf16[256,128]{1,0:T(8,128)(2,1)S(1)} %get-tuple-element.39), channel_id=1, source_target_pairs={{0,64},{32,96},{64,0},{96,32},{1,65},{33,97},{65,1},{97,33},{2,66}... | collective-permute-start | bytes 196616 | tf_op jit(solution)/shard_map/ppermute | solution.py:386
  27.8 4.3 %collective-permute-start.11 = (bf16[256,128]{1,0:T(8,128)(2,1)S(1)}, bf16[256,128]{1,0:T(8,128)(2,1)S(1)}, u32[]{:S(2)}, u32[]{:S(2)}) collective-permute-start(bf16[256,128]{1,0:T(8,128)(2,1)S(1)} %get-tuple-element.40), channel_id=1, source_target_pairs={{0,96},{32,0},{64,32},{96,64},{1,97},{33,1},{65,33},{97,65},{2,98}... | collective-permute-start | bytes 196616 | tf_op jit(solution)/shard_map/ppermute | solution.py:386

commit v7 on v6

--- a/solution.py
+++ b/solution.py
@@ -18,6 +18,7 @@
 MINE = 2
 B = 256
 H = 128
+ORDER = (0, 2, 1, 3)
 EXTRA = 16
 
 MIDDLE = 1.1
@@ -43,7 +44,8 @@
 
 def pack_kernel(slow, zones_x, zones_y, q0, q1, q2, q3, raw, packed, in_sems, out_sems):
     section, pair, _ = place()
-    order = ((1, q1), (2, q2), (3, q3), (0, q0))
+    order = tuple(zip(ORDER, (q0, q1, q2, q3)))
+    order = order[1:] + order[:1]
     arrivals = []
     for shift, _ in order:
         start = pl.ds(pl.multiple_of(lax.rem(section + shift, SECTIONS) * B, B), B)
@@ -204,7 +206,7 @@
     mine = pl.ds(pl.multiple_of(core * H, H), H)
     other = pl.ds(pl.multiple_of((1 - core) * H, H), H)
 
-    for shift, (q, p) in enumerate(((q0, p0), (q1, p1), (q2, p2), (q3, p3))):
+    for shift, q, p in zip(ORDER, (q0, q1, q2, q3), (p0, p1, p2, p3)):
         level = lax.rem(section + SECTIONS - shift, SECTIONS)
         for r in range(0, B, 32):
             slow[level, r : r + 32, mine] = q[r : r + 32, :].astype(I32).astype(F32)
@@ -345,7 +347,7 @@
 
 def merge_kernel(mine, got, own, s1, s2, s3):
     section, _, _ = place()
-    for shift, out in enumerate((own, s1, s2, s3)):
+    for shift, out in zip(ORDER, (own, s1, s2, s3)):
         level = lax.rem(section + shift, SECTIONS)
         out[...] = (mine[level] + got[level].astype(F32)).astype(out.dtype)
 
@@ -365,7 +367,7 @@
 
 def assemble_kernel(own, g1, g2, g3, out):
     section, _, _ = place()
-    for shift, block in enumerate((own, g1, g2, g3)):
+    for shift, block in zip(ORDER, (own, g1, g2, g3)):
         origin = lax.rem(section + SECTIONS - shift, SECTIONS)
         out[0, pl.ds(pl.multiple_of(origin * B, B), B), :] = block[...].astype(F32)
 
@@ -386,6 +388,10 @@
     return lax.ppermute(block, "depth", [(i, (i + shift) % SECTIONS) for i in range(SECTIONS)])
 
 
+def all_along_depth(blocks):
+    return [along_depth(block, shift) for block, shift in zip(blocks, ORDER[1:])]
+
+
 def other_core(block):
     count = lax.axis_size("xline")
     return lax.ppermute(block, "xline", [(i, i ^ 1) for i in range(count)])
@@ -395,7 +401,7 @@
     receiver_data, source_amp, source_x, source_y, omegas, slowness, inverses, zones_x, zones_y
 ):
     blocks = pack(slowness, zones_x, zones_y)
-    moved = [along_depth(blocks[k], k) for k in (1, 2, 3)]
+    moved = all_along_depth(blocks[1:])
     rec_mine, rec_send, sources = starting_fields(
         receiver_data, source_amp, source_x.reshape(1, -1), source_y.reshape(1, -1), blocks[0]
     )
@@ -409,7 +415,7 @@
         omegas, sources, operators, rec_mine, rec_other, mine, other
     )
     own, *parts = merge(grad_mine, other_core(grad_other))
-    return assemble(own, [along_depth(parts[k - 1], k) for k in (1, 2, 3)])
+    return assemble(own, all_along_depth(parts))
 
 
 def solution(mesh):

time: 33.1 us -> 33.1 us (level)
  starting transfers between devices: 12 us -> 13.1 us
  waiting for transfers between devices: 6.08 us -> 5.03 us
    ppermute x6, starting transfers between devices: 10.3 us -> 11.4 us  [along_depth(): lax.ppermute(block, 'depth', [(i, (i + shift) % SECTIONS) for i in range(...]
    ppermute x6, waiting for transfers between devices: 4.91 us -> 3.85 us  [along_depth(): lax.ppermute(block, 'depth', [(i, (i + shift) % SECTIONS) for i in range(...]
where the time goes in v7:
time: 33.1 us; the launch traced here: 33 us
  Pallas kernels  14.7 us (44%)
  starting transfers between devices  13.1 us (40%)
  waiting for transfers between devices  5.03 us (15%)
    ppermute x6, starting transfers between devices, along_depth(): lax.ppermute(block, 'depth', [(i, (i + shift) % SECTIONS) for i in range(...  11.4 us
    pallas_call x1, Pallas kernels, continue_all(): pl.pallas_call(continue_kernel, out_shape=[jax.ShapeDtypeStruct((LEVELS,...  7.33 us
    ppermute x6, waiting for transfers between devices, along_depth(): lax.ppermute(block, 'depth', [(i, (i + shift) % SECTIONS) for i in range(...  3.85 us
    pallas_call x1, Pallas kernels, pack(): pl.pallas_call(pack_kernel, out_shape=[jax.ShapeDtypeStruct((B + EXTRA, H...  2.5 us
    pallas_call x1, Pallas kernels, starting_fields(): pl.pallas_call(fields_kernel, out_shape=[part, part, field], in_specs=[hb...  2.28 us
    pallas_call x1, Pallas kernels, prepare(): pl.pallas_call(prepare_kernel, out_shape=jax.ShapeDtypeStruct((MINE, zone...  1.69 us
    ppermute x6, starting transfers between devices, other_core(): return lax.ppermute(block, 'xline', [(i, i ^ 1) for i in range(count)])  1.68 us
    ppermute x6, waiting for transfers between devices, other_core(): return lax.ppermute(block, 'xline', [(i, i ^ 1) for i in range(count)])  1.18 us
  transfers between devices with their start and end apart: 12, of which 5 were waited for; matrix products, arithmetic and copies ran while one was open for 0% of the time, Pallas kernels for 12%

profile of v7, /device:TPU:0, one launch (start us, length us, event | category | flops | bytes accessed | tf_op | source)
XLA Modules:
  0.0 33.0 jit_solution(14112117177731789133)
XLA Ops:
  0.0 2.5 %pack.1 = (s16[272,128]{1,0:T(8,128)(2,1)}, s16[272,128]{1,0:T(8,128)(2,1)}, s16[272,128]{1,0:T(8,128)(2,1)}, s16[272,128]{1,0:T(8,128)(2,1)}) custom-call(f32[1,1024,128]{2,1,0:T(8,128)} %slow.1, s32[1,4]{1,0:T(1,128)} %zones_x.1, s32[1,16]{1,0:T(1,128)} %zones_y.1), custom_call_target="tpu_custom_call" | custom-call | tf_op jit(solution)/shard_map/pack/pallas_call | solution.py:76
  2.5 3.4 %collective-permute-start = (s16[272,128]{1,0:T(8,128)(2,1)}, s16[272,128]{1,0:T(8,128)(2,1)S(1)}, u32[]{:S(2)}, u32[]{:S(2)}) collective-permute-start(s16[272,128]{1,0:T(8,128)(2,1)} %get-tuple-element.26), channel_id=1, source_target_pairs={{0,64},{32,96},{64,0},{96,32},{1,65},{33,97},{65,1},{97,33},{2,66}... | collective-permute-start | bytes 208904 | tf_op jit(solution)/shard_map/ppermute | solution.py:388
  5.9 0.7 %collective-permute-start.1 = (s16[272,128]{1,0:T(8,128)(2,1)}, s16[272,128]{1,0:T(8,128)(2,1)S(1)}, u32[]{:S(2)}, u32[]{:S(2)}) collective-permute-start(s16[272,128]{1,0:T(8,128)(2,1)} %get-tuple-element.27), channel_id=1, source_target_pairs={{0,32},{32,64},{64,96},{96,0},{1,33},{33,65},{65,97},{97,1},{2,34}... | collective-permute-start | bytes 208904 | tf_op jit(solution)/shard_map/ppermute | solution.py:388
  6.5 2.6 %collective-permute-start.2 = (s16[272,128]{1,0:T(8,128)(2,1)}, s16[272,128]{1,0:T(8,128)(2,1)S(1)}, u32[]{:S(2)}, u32[]{:S(2)}) collective-permute-start(s16[272,128]{1,0:T(8,128)(2,1)} %get-tuple-element.28), channel_id=1, source_target_pairs={{0,96},{32,0},{64,32},{96,64},{1,97},{33,1},{65,33},{97,65},{2,98}... | collective-permute-start | bytes 208904 | tf_op jit(solution)/shard_map/ppermute | solution.py:388
  9.1 2.3 %starting_fields.1 = (bf16[2,2,256,128]{3,2,1,0:T(8,128)(2,1)}, bf16[2,2,256,128]{3,2,1,0:T(8,128)(2,1)}, bf16[2,256,512]{2,1,0:T(8,128)(2,1)}) custom-call(bf16[4,2,1024,128]{3,2,1,0:T(8,128)(2,1)} %receiver.1, bf16[4,2,256]{2,1,0:T(2,128)(2,1)} %amp_hbm.1, s32[1,256]{1,0:T(1,128)} %bitcast.2, s32[1,256]{1,0:T(1,128)} %bitcast.3, ...), custom_call_target="tpu_custom_call" | custom-call | flops 134217728 | bytes 3145728 | tf_op jit(solution)/shard_map/starting_fields/pallas_call | solution.py:142
  11.4 0.0 collective-permute-done.q1
  11.4 0.2 collective-permute-done.1.q2
  11.6 0.0 collective-permute-done.2.q3
  11.6 0.0 copy-start.3
  11.6 0.1 collective-permute-start.3
  11.7 0.5 %collective-permute-start.4 = (s16[272,128]{1,0:T(8,128)(2,1)}, s16[272,128]{1,0:T(8,128)(2,1)S(1)}, u32[]{:S(2)}, u32[]{:S(2)}) collective-permute-start(s16[272,128]{1,0:T(8,128)(2,1)} %get-tuple-element.23._.q0), channel_id=1, source_target_pairs={{0,1},{1,0},{2,3},{3,2},{4,5},{5,4},{6,7},{7,6},{8,9},{9,8},{10,11... | collective-permute-start | bytes 208904 | tf_op jit(solution)/shard_map/ppermute | solution.py:397
  12.2 0.1 collective-permute-start.5
  12.3 0.4 %collective-permute-start.6 = (s16[272,128]{1,0:T(8,128)(2,1)S(1)}, s16[272,128]{1,0:T(8,128)(2,1)S(1)}, u32[]{:S(2)}, u32[]{:S(2)}) collective-permute-start(s16[272,128]{1,0:T(8,128)(2,1)S(1)} %collective-permute-done.1.q2), channel_id=1, source_target_pairs={{0,1},{1,0},{2,3},{3,2},{4,5},{5,4},{6,7},{7,6},{8,9},{9,8},{10,11... | collective-permute-start | bytes 208904 | tf_op jit(solution)/shard_map/ppermute | solution.py:397
  12.7 0.1 collective-permute-start.7
  12.8 1.7 %prepare.1.operators = bf16[2,4,512,512]{3,2,1,0:T(8,128)(2,1)S(1)} custom-call(bf16[4,4,2,256,256]{4,3,2,1,0:T(8,128)(2,1)} %inverses), custom_call_target="tpu_custom_call" | custom-call | bytes 6291456 | tf_op jit(solution)/shard_map/prepare/pallas_call | solution.py:183
  14.5 0.0 collective-permute-done.4.p0
  14.5 0.0 collective-permute-done.5.p1
  14.5 0.0 collective-permute-done.6.p2
  14.5 0.0 collective-permute-done.7.p3
  14.6 0.0 collective-permute-done.3.rec_other
  14.6 0.0 copy-done
  14.6 7.3 %continue_levels.1 = (f32[4,256,128]{2,1,0:T(8,128)S(1)}, bf16[4,256,128]{2,1,0:T(8,128)(2,1)S(1)}) custom-call(f32[4]{0:T(128)S(1)} %copy-done.3, bf16[2,256,512]{2,1,0:T(8,128)(2,1)S(1)} %copy-done.1, bf16[2,4,512,512]{3,2,1,0:T(8,128)(2,1)S(1)} %prepare.1.operators, bf16[2,2,256,128]{3,2,1,0:T(8,128)(2,1)S(1)} %copy-done.2, ...), custom_call_target="tpu_custom_call" | custom-call | flops 4294967296 | bytes 8388608 | tf_op jit(solution)/shard_map/continue_levels/pallas_call | solution.py:326
  21.9 0.5 %collective-permute-start.8 = (bf16[4,256,128]{2,1,0:T(8,128)(2,1)S(1)}, bf16[4,256,128]{2,1,0:T(8,128)(2,1)S(1)}, u32[]{:S(2)}, u32[]{:S(2)}) collective-permute-start(bf16[4,256,128]{2,1,0:T(8,128)(2,1)S(1)} %get-tuple-element.36), channel_id=1, source_target_pairs={{0,1},{1,0},{2,3},{3,2},{4,5},{5,4},{6,7},{7,6},{8,9},{9,8},{10,11... | collective-permute-start | bytes 786440 | tf_op jit(solution)/shard_map/ppermute | solution.py:397
  22.4 1.2 %collective-permute-done.8.got = bf16[4,256,128]{2,1,0:T(8,128)(2,1)S(1)} collective-permute-done((bf16[4,256,128]{2,1,0:T(8,128)(2,1)S(1)}, bf16[4,256,128]{2,1,0:T(8,128)(2,1)S(1)}, u32[]{:S(2)}, u32[]{:S(2)}) %collective-permute-start.8) | collective-permute-done | bytes 262176 | tf_op jit(solution)/shard_map/ppermute | solution.py:397
  23.6 0.1 merge.1
  23.7 1.5 %collective-permute-start.9 = (bf16[256,128]{1,0:T(8,128)(2,1)S(1)}, bf16[256,128]{1,0:T(8,128)(2,1)S(1)}, u32[]{:S(2)}, u32[]{:S(2)}) collective-permute-start(bf16[256,128]{1,0:T(8,128)(2,1)S(1)} %get-tuple-element.38), channel_id=1, source_target_pairs={{0,64},{32,96},{64,0},{96,32},{1,65},{33,97},{65,1},{97,33},{2,66}... | collective-permute-start | bytes 196616 | tf_op jit(solution)/shard_map/ppermute | solution.py:388
  25.2 2.6 %collective-permute-start.10 = (bf16[256,128]{1,0:T(8,128)(2,1)S(1)}, bf16[256,128]{1,0:T(8,128)(2,1)S(1)}, u32[]{:S(2)}, u32[]{:S(2)}) collective-permute-start(bf16[256,128]{1,0:T(8,128)(2,1)S(1)} %get-tuple-element.39), channel_id=1, source_target_pairs={{0,32},{32,64},{64,96},{96,0},{1,33},{33,65},{65,97},{97,1},{2,34}... | collective-permute-start | bytes 196616 | tf_op jit(solution)/shard_map/ppermute | solution.py:388
  27.8 0.6 %collective-permute-start.11 = (bf16[256,128]{1,0:T(8,128)(2,1)S(1)}, bf16[256,128]{1,0:T(8,128)(2,1)S(1)}, u32[]{:S(2)}, u32[]{:S(2)}) collective-permute-start(bf16[256,128]{1,0:T(8,128)(2,1)S(1)} %get-tuple-element.40), channel_id=1, source_target_pairs={{0,96},{32,0},{64,32},{96,64},{1,97},{33,1},{65,33},{97,65},{2,98}... | collective-permute-start | bytes 196616 | tf_op jit(solution)/shard_map/ppermute | solution.py:388
  28.5 1.4 %collective-permute-done.9.g1 = bf16[256,128]{1,0:T(8,128)(2,1)S(1)} collective-permute-done((bf16[256,128]{1,0:T(8,128)(2,1)S(1)}, bf16[256,128]{1,0:T(8,128)(2,1)S(1)}, u32[]{:S(2)}, u32[]{:S(2)}) %collective-permute-start.9) | collective-permute-done | bytes 65568 | tf_op jit(solution)/shard_map/ppermute | solution.py:388
  29.8 1.2 %collective-permute-done.10.g2 = bf16[256,128]{1,0:T(8,128)(2,1)S(1)} collective-permute-done((bf16[256,128]{1,0:T(8,128)(2,1)S(1)}, bf16[256,128]{1,0:T(8,128)(2,1)S(1)}, u32[]{:S(2)}, u32[]{:S(2)}) %collective-permute-start.10) | collective-permute-done | bytes 65568 | tf_op jit(solution)/shard_map/ppermute | solution.py:388
  31.0 1.1 %collective-permute-done.11.g3 = bf16[256,128]{1,0:T(8,128)(2,1)S(1)} collective-permute-done((bf16[256,128]{1,0:T(8,128)(2,1)S(1)}, bf16[256,128]{1,0:T(8,128)(2,1)S(1)}, u32[]{:S(2)}, u32[]{:S(2)}) %collective-permute-start.11) | collective-permute-done | bytes 65568 | tf_op jit(solution)/shard_map/ppermute | solution.py:388
  32.1 0.8 %assemble.1 = f32[1,1024,128]{2,1,0:T(8,128)} custom-call(f32[256,128]{1,0:T(8,128)S(1)} %get-tuple-element.37.own, bf16[256,128]{1,0:T(8,128)(2,1)S(1)} %collective-permute-done.9.g1, bf16[256,128]{1,0:T(8,128)(2,1)S(1)} %collective-permute-done.10.g2, bf16[256,128]{1,0:T(8,128)(2,1)S(1)} %collective-permute-done.11.g3), custom_call_target="tpu_custom_call" | custom-call | tf_op jit(solution)/shard_map/assemble/pallas_call | solution.py:377
  (6 shorter events, 0.0 us)
Async XLA Ops:
  2.5 8.9 %collective-permute-start = (s16[272,128]{1,0:T(8,128)(2,1)}, s16[272,128]{1,0:T(8,128)(2,1)S(1)}, u32[]{:S(2)}, u32[]{:S(2)}) collective-permute-start(s16[272,128]{1,0:T(8,128)(2,1)} %get-tuple-element.26), channel_id=1, source_target_pairs={{0,64},{32,96},{64,0},{96,32},{1,65},{33,97},{65,1},{97,33},{2,66}... | collective-permute-start | bytes 208904 | tf_op jit(solution)/shard_map/ppermute | solution.py:388
  5.9 5.7 %collective-permute-start.1 = (s16[272,128]{1,0:T(8,128)(2,1)}, s16[272,128]{1,0:T(8,128)(2,1)S(1)}, u32[]{:S(2)}, u32[]{:S(2)}) collective-permute-start(s16[272,128]{1,0:T(8,128)(2,1)} %get-tuple-element.27), channel_id=1, source_target_pairs={{0,32},{32,64},{64,96},{96,0},{1,33},{33,65},{65,97},{97,1},{2,34}... | collective-permute-start | bytes 208904 | tf_op jit(solution)/shard_map/ppermute | solution.py:388
  6.5 5.1 %collective-permute-start.2 = (s16[272,128]{1,0:T(8,128)(2,1)}, s16[272,128]{1,0:T(8,128)(2,1)S(1)}, u32[]{:S(2)}, u32[]{:S(2)}) collective-permute-start(s16[272,128]{1,0:T(8,128)(2,1)} %get-tuple-element.28), channel_id=1, source_target_pairs={{0,96},{32,0},{64,32},{96,64},{1,97},{33,1},{65,33},{97,65},{2,98}... | collective-permute-start | bytes 208904 | tf_op jit(solution)/shard_map/ppermute | solution.py:388
  11.6 3.0 %copy-start = (s16[272,128]{1,0:T(8,128)(2,1)S(1)}, s16[272,128]{1,0:T(8,128)(2,1)}, u32[]{:S(2)}) copy-start(s16[272,128]{1,0:T(8,128)(2,1)} %get-tuple-element.23._.q0) | copy-start | bytes 208900
  11.6 3.0 %copy-start.1 = (bf16[2,256,512]{2,1,0:T(8,128)(2,1)S(1)}, bf16[2,256,512]{2,1,0:T(8,128)(2,1)}, u32[]{:S(2)}) copy-start(bf16[2,256,512]{2,1,0:T(8,128)(2,1)} %get-tuple-element.24.sources) | copy-start | bytes 1572868
  11.6 3.0 %copy-start.2 = (bf16[2,2,256,128]{3,2,1,0:T(8,128)(2,1)S(1)}, bf16[2,2,256,128]{3,2,1,0:T(8,128)(2,1)}, u32[]{:S(2)}) copy-start(bf16[2,2,256,128]{3,2,1,0:T(8,128)(2,1)} %get-tuple-element.30.rec_mine) | copy-start | bytes 786436
  11.6 3.0 %copy-start.3 = (f32[4]{0:T(128)S(1)}, f32[4]{0:T(128)}, u32[]{:S(2)}) copy-start(f32[4]{0:T(128)} %omegas.1) | copy-start | bytes 52
  11.6 2.9 %collective-permute-start.3 = (bf16[2,2,256,128]{3,2,1,0:T(8,128)(2,1)}, bf16[2,2,256,128]{3,2,1,0:T(8,128)(2,1)S(1)}, u32[]{:S(2)}, u32[]{:S(2)}) collective-permute-start(bf16[2,2,256,128]{3,2,1,0:T(8,128)(2,1)} %get-tuple-element.31), channel_id=1, source_target_pairs={{0,1},{1,0},{2,3},{3,2},{4,5},{5,4},{6,7},{7,6},{8,9},{9,8},{10,11... | collective-permute-start | bytes 786440 | tf_op jit(solution)/shard_map/ppermute | solution.py:397
  11.7 2.8 %collective-permute-start.4 = (s16[272,128]{1,0:T(8,128)(2,1)}, s16[272,128]{1,0:T(8,128)(2,1)S(1)}, u32[]{:S(2)}, u32[]{:S(2)}) collective-permute-start(s16[272,128]{1,0:T(8,128)(2,1)} %get-tuple-element.23._.q0), channel_id=1, source_target_pairs={{0,1},{1,0},{2,3},{3,2},{4,5},{5,4},{6,7},{7,6},{8,9},{9,8},{10,11... | collective-permute-start | bytes 208904 | tf_op jit(solution)/shard_map/ppermute | solution.py:397
  12.2 2.3 %collective-permute-start.5 = (s16[272,128]{1,0:T(8,128)(2,1)S(1)}, s16[272,128]{1,0:T(8,128)(2,1)S(1)}, u32[]{:S(2)}, u32[]{:S(2)}) collective-permute-start(s16[272,128]{1,0:T(8,128)(2,1)S(1)} %collective-permute-done.q1), channel_id=1, source_target_pairs={{0,1},{1,0},{2,3},{3,2},{4,5},{5,4},{6,7},{7,6},{8,9},{9,8},{10,11... | collective-permute-start | bytes 208904 | tf_op jit(solution)/shard_map/ppermute | solution.py:397
  12.3 2.2 %collective-permute-start.6 = (s16[272,128]{1,0:T(8,128)(2,1)S(1)}, s16[272,128]{1,0:T(8,128)(2,1)S(1)}, u32[]{:S(2)}, u32[]{:S(2)}) collective-permute-start(s16[272,128]{1,0:T(8,128)(2,1)S(1)} %collective-permute-done.1.q2), channel_id=1, source_target_pairs={{0,1},{1,0},{2,3},{3,2},{4,5},{5,4},{6,7},{7,6},{8,9},{9,8},{10,11... | collective-permute-start | bytes 208904 | tf_op jit(solution)/shard_map/ppermute | solution.py:397
  12.7 1.8 %collective-permute-start.7 = (s16[272,128]{1,0:T(8,128)(2,1)S(1)}, s16[272,128]{1,0:T(8,128)(2,1)S(1)}, u32[]{:S(2)}, u32[]{:S(2)}) collective-permute-start(s16[272,128]{1,0:T(8,128)(2,1)S(1)} %collective-permute-done.2.q3), channel_id=1, source_target_pairs={{0,1},{1,0},{2,3},{3,2},{4,5},{5,4},{6,7},{7,6},{8,9},{9,8},{10,11... | collective-permute-start | bytes 208904 | tf_op jit(solution)/shard_map/ppermute | solution.py:397
  21.9 1.7 %collective-permute-start.8 = (bf16[4,256,128]{2,1,0:T(8,128)(2,1)S(1)}, bf16[4,256,128]{2,1,0:T(8,128)(2,1)S(1)}, u32[]{:S(2)}, u32[]{:S(2)}) collective-permute-start(bf16[4,256,128]{2,1,0:T(8,128)(2,1)S(1)} %get-tuple-element.36), channel_id=1, source_target_pairs={{0,1},{1,0},{2,3},{3,2},{4,5},{5,4},{6,7},{7,6},{8,9},{9,8},{10,11... | collective-permute-start | bytes 786440 | tf_op jit(solution)/shard_map/ppermute | solution.py:397
  23.7 6.2 %collective-permute-start.9 = (bf16[256,128]{1,0:T(8,128)(2,1)S(1)}, bf16[256,128]{1,0:T(8,128)(2,1)S(1)}, u32[]{:S(2)}, u32[]{:S(2)}) collective-permute-start(bf16[256,128]{1,0:T(8,128)(2,1)S(1)} %get-tuple-element.38), channel_id=1, source_target_pairs={{0,64},{32,96},{64,0},{96,32},{1,65},{33,97},{65,1},{97,33},{2,66}... | collective-permute-start | bytes 196616 | tf_op jit(solution)/shard_map/ppermute | solution.py:388
  25.2 5.8 %collective-permute-start.10 = (bf16[256,128]{1,0:T(8,128)(2,1)S(1)}, bf16[256,128]{1,0:T(8,128)(2,1)S(1)}, u32[]{:S(2)}, u32[]{:S(2)}) collective-permute-start(bf16[256,128]{1,0:T(8,128)(2,1)S(1)} %get-tuple-element.39), channel_id=1, source_target_pairs={{0,32},{32,64},{64,96},{96,0},{1,33},{33,65},{65,97},{97,1},{2,34}... | collective-permute-start | bytes 196616 | tf_op jit(solution)/shard_map/ppermute | solution.py:388
  27.8 4.3 %collective-permute-start.11 = (bf16[256,128]{1,0:T(8,128)(2,1)S(1)}, bf16[256,128]{1,0:T(8,128)(2,1)S(1)}, u32[]{:S(2)}, u32[]{:S(2)}) collective-permute-start(bf16[256,128]{1,0:T(8,128)(2,1)S(1)} %get-tuple-element.40), channel_id=1, source_target_pairs={{0,96},{32,0},{64,32},{96,64},{1,97},{33,1},{65,33},{97,65},{2,98}... | collective-permute-start | bytes 196616 | tf_op jit(solution)/shard_map/ppermute | solution.py:388

commit v8 on v5

--- a/solution.py
+++ b/solution.py
@@ -159,15 +159,22 @@
 
 def prepare_kernel(inverses, operators, table, sems):
     core = place()[2]
+    zones = table.shape[1]
     copies = [
-        pltpu.make_async_copy(inverses.at[core * MINE + f], table.at[f], sems.at[f])
+        [
+            pltpu.make_async_copy(
+                inverses.at[core * MINE + f, zone], table.at[f, zone], sems.at[f, zone]
+            )
+            for zone in range(zones)
+        ]
         for f in range(MINE)
     ]
-    for copy in copies:
-        copy.start()
     for f in range(MINE):
-        copies[f].wait()
-        for zone in range(table.shape[1]):
+        for copy in copies[f]:
+            copy.start()
+    for f in range(MINE):
+        for zone in range(zones):
+            copies[f][zone].wait()
             real = table[f, zone, 0]
             imag = table[f, zone, 1]
             operators[f, zone, :B, :B] = real
@@ -185,7 +192,7 @@
         out_specs=pl.BlockSpec(memory_space=pltpu.VMEM),
         scratch_shapes=[
             pltpu.VMEM((MINE, zones, 2, B, B), BF16),
-            pltpu.SemaphoreType.DMA((MINE,)),
+            pltpu.SemaphoreType.DMA((MINE, zones)),
         ],
         compiler_params=pltpu.CompilerParams(vmem_limit_bytes=48 * MB),
         cost_estimate=pl.CostEstimate(flops=0, bytes_accessed=6 * MB, transcendentals=0),

time: 32.5 us -> 32.4 us (level)
  transfers between devices with their start and end apart: 12 -> 12, of which waited for: 7 -> 7; matrix products, arithmetic and copies ran while one was open for 0% -> 0% of each run, Pallas kernels for 13% -> 12%
where the time goes in v8:
time: 32.4 us; the launch traced here: 32.2 us
  Pallas kernels  14.7 us (45%)
  starting transfers between devices  10.9 us (34%)
  waiting for transfers between devices  6.45 us (20%)
    ppermute x6, starting transfers between devices, along_depth(): lax.ppermute(block, 'depth', [(i, (i + shift) % SECTIONS) for i in range(...  9.49 us
    pallas_call x1, Pallas kernels, continue_all(): pl.pallas_call(continue_kernel, out_shape=[jax.ShapeDtypeStruct((LEVELS,...  7.33 us
    ppermute x6, waiting for transfers between devices, along_depth(): lax.ppermute(block, 'depth', [(i, (i + shift) % SECTIONS) for i in range(...  3.9 us
    ppermute x6, waiting for transfers between devices, other_core(): return lax.ppermute(block, 'xline', [(i, i ^ 1) for i in range(count)])  2.55 us
    pallas_call x1, Pallas kernels, pack(): pl.pallas_call(pack_kernel, out_shape=[jax.ShapeDtypeStruct((B + EXTRA, H...  2.5 us
    pallas_call x1, Pallas kernels, starting_fields(): pl.pallas_call(fields_kernel, out_shape=[part, part, field], in_specs=[hb...  2.28 us
    pallas_call x1, Pallas kernels, prepare(): pl.pallas_call(prepare_kernel, out_shape=jax.ShapeDtypeStruct((MINE, zone...  1.7 us
    ppermute x6, starting transfers between devices, other_core(): return lax.ppermute(block, 'xline', [(i, i ^ 1) for i in range(count)])  1.41 us
  transfers between devices with their start and end apart: 12, of which 7 were waited for; matrix products, arithmetic and copies ran while one was open for 0% of the time, Pallas kernels for 12%

profile of v8, /device:TPU:0, one launch (start us, length us, event | category | flops | bytes accessed | tf_op | source)
XLA Modules:
  0.0 32.2 jit_solution(3708556377239427611)
XLA Ops:
  0.0 2.5 %pack.1 = (s16[272,128]{1,0:T(8,128)(2,1)}, s16[272,128]{1,0:T(8,128)(2,1)}, s16[272,128]{1,0:T(8,128)(2,1)}, s16[272,128]{1,0:T(8,128)(2,1)}) custom-call(f32[1,1024,128]{2,1,0:T(8,128)} %slow.1, s32[1,4]{1,0:T(1,128)} %zones_x.1, s32[1,16]{1,0:T(1,128)} %zones_y.1), custom_call_target="tpu_custom_call" | custom-call | tf_op jit(solution)/shard_map/pack/pallas_call | solution.py:74
  2.5 1.7 %collective-permute-start = (s16[272,128]{1,0:T(8,128)(2,1)}, s16[272,128]{1,0:T(8,128)(2,1)S(1)}, u32[]{:S(2)}, u32[]{:S(2)}) collective-permute-start(s16[272,128]{1,0:T(8,128)(2,1)} %get-tuple-element.30), channel_id=1, source_target_pairs={{0,32},{32,64},{64,96},{96,0},{1,33},{33,65},{65,97},{97,1},{2,34}... | collective-permute-start | bytes 208904 | tf_op jit(solution)/shard_map/ppermute | solution.py:393
  4.2 2.9 %collective-permute-start.1 = (s16[272,128]{1,0:T(8,128)(2,1)}, s16[272,128]{1,0:T(8,128)(2,1)S(1)}, u32[]{:S(2)}, u32[]{:S(2)}) collective-permute-start(s16[272,128]{1,0:T(8,128)(2,1)} %get-tuple-element.31), channel_id=1, source_target_pairs={{0,64},{32,96},{64,0},{96,32},{1,65},{33,97},{65,1},{97,33},{2,66}... | collective-permute-start | bytes 208904 | tf_op jit(solution)/shard_map/ppermute | solution.py:393
  7.1 1.3 %collective-permute-start.2 = (s16[272,128]{1,0:T(8,128)(2,1)}, s16[272,128]{1,0:T(8,128)(2,1)S(1)}, u32[]{:S(2)}, u32[]{:S(2)}) collective-permute-start(s16[272,128]{1,0:T(8,128)(2,1)} %get-tuple-element.32), channel_id=1, source_target_pairs={{0,96},{32,0},{64,32},{96,64},{1,97},{33,1},{65,33},{97,65},{2,98}... | collective-permute-start | bytes 208904 | tf_op jit(solution)/shard_map/ppermute | solution.py:393
  8.5 2.3 %starting_fields.1 = (bf16[2,2,256,128]{3,2,1,0:T(8,128)(2,1)}, bf16[2,2,256,128]{3,2,1,0:T(8,128)(2,1)}, bf16[2,256,512]{2,1,0:T(8,128)(2,1)}) custom-call(bf16[4,2,1024,128]{3,2,1,0:T(8,128)(2,1)} %receiver.1, bf16[4,2,256]{2,1,0:T(2,128)(2,1)} %amp_hbm.1, s32[1,256]{1,0:T(1,128)} %bitcast.2, s32[1,256]{1,0:T(1,128)} %bitcast.3, ...), custom_call_target="tpu_custom_call" | custom-call | flops 134217728 | bytes 3145728 | tf_op jit(solution)/shard_map/starting_fields/pallas_call | solution.py:140
  10.8 0.0 copy-start.1
  10.8 0.0 copy-start.3
  10.8 1.7 %prepare.1.operators = bf16[2,4,512,512]{3,2,1,0:T(8,128)(2,1)S(1)} custom-call(bf16[4,4,2,256,256]{4,3,2,1,0:T(8,128)(2,1)} %inverses), custom_call_target="tpu_custom_call" | custom-call | bytes 6291456 | tf_op jit(solution)/shard_map/prepare/pallas_call | solution.py:188
  12.5 0.0 collective-permute-done.q1
  12.5 0.0 collective-permute-done.1.q2
  12.6 0.0 collective-permute-done.2.q3
  12.6 0.1 collective-permute-start.3
  12.7 0.5 %collective-permute-start.4 = (s16[272,128]{1,0:T(8,128)(2,1)S(1)}, s16[272,128]{1,0:T(8,128)(2,1)S(1)}, u32[]{:S(2)}, u32[]{:S(2)}) collective-permute-start(s16[272,128]{1,0:T(8,128)(2,1)S(1)} %copy-done), channel_id=1, source_target_pairs={{0,1},{1,0},{2,3},{3,2},{4,5},{5,4},{6,7},{7,6},{8,9},{9,8},{10,11... | collective-permute-start | bytes 208904 | tf_op jit(solution)/shard_map/ppermute | solution.py:398
  13.2 0.1 collective-permute-start.5
  13.3 0.4 %collective-permute-start.6 = (s16[272,128]{1,0:T(8,128)(2,1)S(1)}, s16[272,128]{1,0:T(8,128)(2,1)S(1)}, u32[]{:S(2)}, u32[]{:S(2)}) collective-permute-start(s16[272,128]{1,0:T(8,128)(2,1)S(1)} %collective-permute-done.1.q2), channel_id=1, source_target_pairs={{0,1},{1,0},{2,3},{3,2},{4,5},{5,4},{6,7},{7,6},{8,9},{9,8},{10,11... | collective-permute-start | bytes 208904 | tf_op jit(solution)/shard_map/ppermute | solution.py:398
  13.7 0.1 collective-permute-start.7
  13.8 0.5 %collective-permute-done.4.p0 = s16[272,128]{1,0:T(8,128)(2,1)S(1)} collective-permute-done((s16[272,128]{1,0:T(8,128)(2,1)S(1)}, s16[272,128]{1,0:T(8,128)(2,1)S(1)}, u32[]{:S(2)}, u32[]{:S(2)}) %collective-permute-start.4) | collective-permute-done | bytes 69664 | tf_op jit(solution)/shard_map/ppermute | solution.py:398
  14.3 0.1 collective-permute-done.5.p1
  14.4 0.2 collective-permute-done.6.p2
  14.6 0.4 %collective-permute-done.7.p3 = s16[272,128]{1,0:T(8,128)(2,1)S(1)} collective-permute-done((s16[272,128]{1,0:T(8,128)(2,1)S(1)}, s16[272,128]{1,0:T(8,128)(2,1)S(1)}, u32[]{:S(2)}, u32[]{:S(2)}) %collective-permute-start.7) | collective-permute-done | bytes 69664 | tf_op jit(solution)/shard_map/ppermute | solution.py:398
  14.9 0.0 collective-permute-done.3.rec_other
  15.0 7.3 %continue_levels.1 = (f32[4,256,128]{2,1,0:T(8,128)S(1)}, bf16[4,256,128]{2,1,0:T(8,128)(2,1)S(1)}) custom-call(f32[4]{0:T(128)S(1)} %copy-done.3, bf16[2,256,512]{2,1,0:T(8,128)(2,1)S(1)} %copy-done.1, bf16[2,4,512,512]{3,2,1,0:T(8,128)(2,1)S(1)} %prepare.1.operators, bf16[2,2,256,128]{3,2,1,0:T(8,128)(2,1)S(1)} %copy-done.2, ...), custom_call_target="tpu_custom_call" | custom-call | flops 4294967296 | bytes 8388608 | tf_op jit(solution)/shard_map/continue_levels/pallas_call | solution.py:331
  22.3 0.2 collective-permute-start.8
  22.5 1.4 %collective-permute-done.8.got = bf16[4,256,128]{2,1,0:T(8,128)(2,1)S(1)} collective-permute-done((bf16[4,256,128]{2,1,0:T(8,128)(2,1)S(1)}, bf16[4,256,128]{2,1,0:T(8,128)(2,1)S(1)}, u32[]{:S(2)}, u32[]{:S(2)}) %collective-permute-start.8) | collective-permute-done | bytes 262176 | tf_op jit(solution)/shard_map/ppermute | solution.py:398
  23.9 0.1 merge.1
  24.0 0.7 %collective-permute-start.9 = (bf16[256,128]{1,0:T(8,128)(2,1)S(1)}, bf16[256,128]{1,0:T(8,128)(2,1)S(1)}, u32[]{:S(2)}, u32[]{:S(2)}) collective-permute-start(bf16[256,128]{1,0:T(8,128)(2,1)S(1)} %get-tuple-element.42), channel_id=1, source_target_pairs={{0,32},{32,64},{64,96},{96,0},{1,33},{33,65},{65,97},{97,1},{2,34}... | collective-permute-start | bytes 196616 | tf_op jit(solution)/shard_map/ppermute | solution.py:393
  24.7 2.4 %collective-permute-start.10 = (bf16[256,128]{1,0:T(8,128)(2,1)S(1)}, bf16[256,128]{1,0:T(8,128)(2,1)S(1)}, u32[]{:S(2)}, u32[]{:S(2)}) collective-permute-start(bf16[256,128]{1,0:T(8,128)(2,1)S(1)} %get-tuple-element.43), channel_id=1, source_target_pairs={{0,64},{32,96},{64,0},{96,32},{1,65},{33,97},{65,1},{97,33},{2,66}... | collective-permute-start | bytes 196616 | tf_op jit(solution)/shard_map/ppermute | solution.py:393
  27.1 0.4 %collective-permute-start.11 = (bf16[256,128]{1,0:T(8,128)(2,1)S(1)}, bf16[256,128]{1,0:T(8,128)(2,1)S(1)}, u32[]{:S(2)}, u32[]{:S(2)}) collective-permute-start(bf16[256,128]{1,0:T(8,128)(2,1)S(1)} %get-tuple-element.44), channel_id=1, source_target_pairs={{0,96},{32,0},{64,32},{96,64},{1,97},{33,1},{65,33},{97,65},{2,98}... | collective-permute-start | bytes 196616 | tf_op jit(solution)/shard_map/ppermute | solution.py:393
  27.5 3.4 %collective-permute-done.9.g1 = bf16[256,128]{1,0:T(8,128)(2,1)S(1)} collective-permute-done((bf16[256,128]{1,0:T(8,128)(2,1)S(1)}, bf16[256,128]{1,0:T(8,128)(2,1)S(1)}, u32[]{:S(2)}, u32[]{:S(2)}) %collective-permute-start.9) | collective-permute-done | bytes 65568 | tf_op jit(solution)/shard_map/ppermute | solution.py:393
  30.9 0.0 collective-permute-done.10.g2
  30.9 0.5 %collective-permute-done.11.g3 = bf16[256,128]{1,0:T(8,128)(2,1)S(1)} collective-permute-done((bf16[256,128]{1,0:T(8,128)(2,1)S(1)}, bf16[256,128]{1,0:T(8,128)(2,1)S(1)}, u32[]{:S(2)}, u32[]{:S(2)}) %collective-permute-start.11) | collective-permute-done | bytes 65568 | tf_op jit(solution)/shard_map/ppermute | solution.py:393
  31.4 0.8 %assemble.1 = f32[1,1024,128]{2,1,0:T(8,128)} custom-call(f32[256,128]{1,0:T(8,128)S(1)} %get-tuple-element.41.own, bf16[256,128]{1,0:T(8,128)(2,1)S(1)} %collective-permute-done.9.g1, bf16[256,128]{1,0:T(8,128)(2,1)S(1)} %collective-permute-done.10.g2, bf16[256,128]{1,0:T(8,128)(2,1)S(1)} %collective-permute-done.11.g3), custom_call_target="tpu_custom_call" | custom-call | tf_op jit(solution)/shard_map/assemble/pallas_call | solution.py:382
  (8 shorter events, 0.0 us)
Async XLA Ops:
  2.5 10.0 %collective-permute-start = (s16[272,128]{1,0:T(8,128)(2,1)}, s16[272,128]{1,0:T(8,128)(2,1)S(1)}, u32[]{:S(2)}, u32[]{:S(2)}) collective-permute-start(s16[272,128]{1,0:T(8,128)(2,1)} %get-tuple-element.30), channel_id=1, source_target_pairs={{0,32},{32,64},{64,96},{96,0},{1,33},{33,65},{65,97},{97,1},{2,34}... | collective-permute-start | bytes 208904 | tf_op jit(solution)/shard_map/ppermute | solution.py:393
  4.2 8.3 %collective-permute-start.1 = (s16[272,128]{1,0:T(8,128)(2,1)}, s16[272,128]{1,0:T(8,128)(2,1)S(1)}, u32[]{:S(2)}, u32[]{:S(2)}) collective-permute-start(s16[272,128]{1,0:T(8,128)(2,1)} %get-tuple-element.31), channel_id=1, source_target_pairs={{0,64},{32,96},{64,0},{96,32},{1,65},{33,97},{65,1},{97,33},{2,66}... | collective-permute-start | bytes 208904 | tf_op jit(solution)/shard_map/ppermute | solution.py:393
  7.1 5.4 %collective-permute-start.2 = (s16[272,128]{1,0:T(8,128)(2,1)}, s16[272,128]{1,0:T(8,128)(2,1)S(1)}, u32[]{:S(2)}, u32[]{:S(2)}) collective-permute-start(s16[272,128]{1,0:T(8,128)(2,1)} %get-tuple-element.32), channel_id=1, source_target_pairs={{0,96},{32,0},{64,32},{96,64},{1,97},{33,1},{65,33},{97,65},{2,98}... | collective-permute-start | bytes 208904 | tf_op jit(solution)/shard_map/ppermute | solution.py:393
  10.8 1.8 %copy-start.4 = (bf16[2,2,256,128]{3,2,1,0:T(8,128)(2,1)S(1)}, bf16[2,2,256,128]{3,2,1,0:T(8,128)(2,1)}, u32[]{:S(2)}) copy-start(bf16[2,2,256,128]{3,2,1,0:T(8,128)(2,1)} %get-tuple-element.35) | copy-start | bytes 786436
  10.8 1.9 %copy-start = (s16[272,128]{1,0:T(8,128)(2,1)S(1)}, s16[272,128]{1,0:T(8,128)(2,1)}, u32[]{:S(2)}) copy-start(s16[272,128]{1,0:T(8,128)(2,1)} %get-tuple-element.25._.q0) | copy-start | bytes 208900
  10.8 4.1 %copy-start.1 = (bf16[2,256,512]{2,1,0:T(8,128)(2,1)S(1)}, bf16[2,256,512]{2,1,0:T(8,128)(2,1)}, u32[]{:S(2)}) copy-start(bf16[2,256,512]{2,1,0:T(8,128)(2,1)} %get-tuple-element.27.sources) | copy-start | bytes 1572868
  10.8 4.1 %copy-start.2 = (bf16[2,2,256,128]{3,2,1,0:T(8,128)(2,1)S(1)}, bf16[2,2,256,128]{3,2,1,0:T(8,128)(2,1)}, u32[]{:S(2)}) copy-start(bf16[2,2,256,128]{3,2,1,0:T(8,128)(2,1)} %get-tuple-element.34.rec_mine) | copy-start | bytes 786436
  10.8 4.1 %copy-start.3 = (f32[4]{0:T(128)S(1)}, f32[4]{0:T(128)}, u32[]{:S(2)}) copy-start(f32[4]{0:T(128)} %omegas.1) | copy-start | bytes 52
  12.6 2.4 %collective-permute-start.3 = (bf16[2,2,256,128]{3,2,1,0:T(8,128)(2,1)S(1)}, bf16[2,2,256,128]{3,2,1,0:T(8,128)(2,1)S(1)}, u32[]{:S(2)}, u32[]{:S(2)}) collective-permute-start(bf16[2,2,256,128]{3,2,1,0:T(8,128)(2,1)S(1)} %copy-done.4), channel_id=1, source_target_pairs={{0,1},{1,0},{2,3},{3,2},{4,5},{5,4},{6,7},{7,6},{8,9},{9,8},{10,11... | collective-permute-start | bytes 786440 | tf_op jit(solution)/shard_map/ppermute | solution.py:398
  12.7 1.6 %collective-permute-start.4 = (s16[272,128]{1,0:T(8,128)(2,1)S(1)}, s16[272,128]{1,0:T(8,128)(2,1)S(1)}, u32[]{:S(2)}, u32[]{:S(2)}) collective-permute-start(s16[272,128]{1,0:T(8,128)(2,1)S(1)} %copy-done), channel_id=1, source_target_pairs={{0,1},{1,0},{2,3},{3,2},{4,5},{5,4},{6,7},{7,6},{8,9},{9,8},{10,11... | collective-permute-start | bytes 208904 | tf_op jit(solution)/shard_map/ppermute | solution.py:398
  13.2 1.3 %collective-permute-start.5 = (s16[272,128]{1,0:T(8,128)(2,1)S(1)}, s16[272,128]{1,0:T(8,128)(2,1)S(1)}, u32[]{:S(2)}, u32[]{:S(2)}) collective-permute-start(s16[272,128]{1,0:T(8,128)(2,1)S(1)} %collective-permute-done.q1), channel_id=1, source_target_pairs={{0,1},{1,0},{2,3},{3,2},{4,5},{5,4},{6,7},{7,6},{8,9},{9,8},{10,11... | collective-permute-start | bytes 208904 | tf_op jit(solution)/shard_map/ppermute | solution.py:398
  13.3 1.3 %collective-permute-start.6 = (s16[272,128]{1,0:T(8,128)(2,1)S(1)}, s16[272,128]{1,0:T(8,128)(2,1)S(1)}, u32[]{:S(2)}, u32[]{:S(2)}) collective-permute-start(s16[272,128]{1,0:T(8,128)(2,1)S(1)} %collective-permute-done.1.q2), channel_id=1, source_target_pairs={{0,1},{1,0},{2,3},{3,2},{4,5},{5,4},{6,7},{7,6},{8,9},{9,8},{10,11... | collective-permute-start | bytes 208904 | tf_op jit(solution)/shard_map/ppermute | solution.py:398
  13.7 1.3 %collective-permute-start.7 = (s16[272,128]{1,0:T(8,128)(2,1)S(1)}, s16[272,128]{1,0:T(8,128)(2,1)S(1)}, u32[]{:S(2)}, u32[]{:S(2)}) collective-permute-start(s16[272,128]{1,0:T(8,128)(2,1)S(1)} %collective-permute-done.2.q3), channel_id=1, source_target_pairs={{0,1},{1,0},{2,3},{3,2},{4,5},{5,4},{6,7},{7,6},{8,9},{9,8},{10,11... | collective-permute-start | bytes 208904 | tf_op jit(solution)/shard_map/ppermute | solution.py:398
  22.3 1.6 %collective-permute-start.8 = (bf16[4,256,128]{2,1,0:T(8,128)(2,1)S(1)}, bf16[4,256,128]{2,1,0:T(8,128)(2,1)S(1)}, u32[]{:S(2)}, u32[]{:S(2)}) collective-permute-start(bf16[4,256,128]{2,1,0:T(8,128)(2,1)S(1)} %get-tuple-element.40), channel_id=1, source_target_pairs={{0,1},{1,0},{2,3},{3,2},{4,5},{5,4},{6,7},{7,6},{8,9},{9,8},{10,11... | collective-permute-start | bytes 786440 | tf_op jit(solution)/shard_map/ppermute | solution.py:398
  24.0 6.9 %collective-permute-start.9 = (bf16[256,128]{1,0:T(8,128)(2,1)S(1)}, bf16[256,128]{1,0:T(8,128)(2,1)S(1)}, u32[]{:S(2)}, u32[]{:S(2)}) collective-permute-start(bf16[256,128]{1,0:T(8,128)(2,1)S(1)} %get-tuple-element.42), channel_id=1, source_target_pairs={{0,32},{32,64},{64,96},{96,0},{1,33},{33,65},{65,97},{97,1},{2,34}... | collective-permute-start | bytes 196616 | tf_op jit(solution)/shard_map/ppermute | solution.py:393
  24.7 6.1 %collective-permute-start.10 = (bf16[256,128]{1,0:T(8,128)(2,1)S(1)}, bf16[256,128]{1,0:T(8,128)(2,1)S(1)}, u32[]{:S(2)}, u32[]{:S(2)}) collective-permute-start(bf16[256,128]{1,0:T(8,128)(2,1)S(1)} %get-tuple-element.43), channel_id=1, source_target_pairs={{0,64},{32,96},{64,0},{96,32},{1,65},{33,97},{65,1},{97,33},{2,66}... | collective-permute-start | bytes 196616 | tf_op jit(solution)/shard_map/ppermute | solution.py:393
  27.1 4.3 %collective-permute-start.11 = (bf16[256,128]{1,0:T(8,128)(2,1)S(1)}, bf16[256,128]{1,0:T(8,128)(2,1)S(1)}, u32[]{:S(2)}, u32[]{:S(2)}) collective-permute-start(bf16[256,128]{1,0:T(8,128)(2,1)S(1)} %get-tuple-element.44), channel_id=1, source_target_pairs={{0,96},{32,0},{64,32},{96,64},{1,97},{33,1},{65,33},{97,65},{2,98}... | collective-permute-start | bytes 196616 | tf_op jit(solution)/shard_map/ppermute | solution.py:393
